TPU v7x, 32 devices: a whole 2x2x4 slice. The times are simulated.
32 devices in a mesh: leaf: 8 (over z, y), rhs: 4 (over x, core).
Axes of the slice: x: 2, y: 2, z: 4, core: 2. Of those that a mesh axis runs over, the one named last changes fastest.
Arguments:
- right_sides: bfloat16 [512, 8192], P('rhs', 'leaf'), may hold values from -6 to 6
- block_order: int32 [64], replicated, may hold values from 0 to 63, each once
- leaf_basis: bfloat16 [8, 1024, 256], P('leaf'), may hold values from -0.1875 to 0.1875
- leaf_inner: bfloat16 [8, 256, 256], P('leaf'), may hold values from -0.375 to 0.375
- leaf_inverse: bfloat16 [8, 768, 768], P('leaf', 'rhs'), may hold values from -0.21875 to 0.21875
- leaf_coupling: bfloat16 [8, 768, 256], P('leaf'), may hold values from -0.21875 to 0.21875
- merge_one: bfloat16 [2048, 512], P('leaf'), may hold values from -0.25 to 0.25
- merge_two: bfloat16 [1024, 512], P('leaf'), may hold values from -0.25 to 0.25
- merge_three: bfloat16 [512, 512], P('leaf'), may hold values from -0.25 to 0.25
Outputs:
- leaf_part: bfloat16 [512, 6144], P('rhs', 'leaf')
- level_one: float32 [512, 1024], P('rhs', 'leaf')
- level_two: float32 [512, 512], P('rhs', 'leaf')
- level_three: float32 [512, 256], P('rhs', 'leaf')
- top_skeleton: float32 [512, 256], P('rhs', 'leaf')
Inputs may be any that keep to these rules, and one draw needn't show every extreme that they name: block_order is a permutation: every block of the 64 appears exactly once.
All inputs are finite; a program needn't handle non-finite values.
Results may differ from a plain program's by a relative error of at most 0.007.
Values may be sent and summed in bfloat16 or wider, within the bound.
No kernel may reach another device: no remote copies, remote signals or barrier semaphores. Data moves between devices by JAX's collectives and lax.ppermute only.
A program may use at most 64 MiB of HBM per device.

v0:
```python
import jax
import jax.numpy as jnp
from jax import lax
from jax.sharding import PartitionSpec as P

BLOCK = 128


def swapped(block, axis, bit):
    count = lax.axis_size(axis)
    route = []
    for low in range(count):
        high = low | 1 << bit
        if high != low and high < count:
            route += [(low, high), (high, low)]
    return lax.ppermute(block, axis, route)


def shards(
    right_sides,
    block_order,
    leaf_basis,
    leaf_inner,
    leaf_inverse,
    leaf_coupling,
    merge_one,
    merge_two,
    merge_three,
):
    leaf_count = lax.axis_size("leaf")
    columns, row_count = right_sides.shape
    per_group = columns // leaf_count
    group_size = per_group * row_count
    tile_width = 128
    outgoing = right_sides.reshape(leaf_count, group_size // tile_width, tile_width)
    arrived = lax.all_to_all(outgoing, "leaf", split_axis=0, concat_axis=1, tiled=True)
    full_rows = jnp.transpose(arrived.reshape(leaf_count, per_group, row_count), (1, 0, 2))
    blocks = full_rows.reshape(per_group, -1, BLOCK)
    reordered = jnp.take(blocks, block_order, axis=1).reshape(per_group, leaf_count, row_count)
    returning = jnp.transpose(reordered, (1, 0, 2)).reshape(
        leaf_count, group_size // tile_width, tile_width
    )
    placed = lax.all_to_all(returning, "leaf", split_axis=0, concat_axis=1, tiled=True).reshape(
        columns, row_count
    )
    basis_matrix = leaf_basis[0]
    projected = jnp.dot(placed, basis_matrix, preferred_element_type=jnp.float32).astype(
        jnp.bfloat16
    )
    middle = jnp.dot(projected, leaf_inner[0], preferred_element_type=jnp.float32).astype(
        jnp.bfloat16
    )
    correction = lax.dot_general(
        middle, basis_matrix, (((1,), (1,)), ((), ())), preferred_element_type=jnp.float32
    )
    reflected = (placed.astype(jnp.float32) - correction).astype(jnp.bfloat16)
    split_at = row_count - basis_matrix.shape[1]
    leading = reflected[:, :split_at]
    trailing = reflected[:, split_at:]
    eliminated = jnp.dot(
        leading,
        lax.all_gather(leaf_inverse, "rhs", axis=1, tiled=True)[0],
        preferred_element_type=jnp.float32,
    ).astype(jnp.bfloat16)
    coupled = jnp.dot(eliminated, leaf_coupling[0], preferred_element_type=jnp.float32)
    current = (trailing.astype(jnp.float32) - coupled).astype(jnp.bfloat16)
    position = lax.axis_index("leaf")
    outputs = []
    top_part = None
    for level_index, merge_table in enumerate((merge_one, merge_two, merge_three), start=1):
        contribution = jnp.dot(current, merge_table, preferred_element_type=jnp.float32)
        group_count = 2**level_index
        piece_width = contribution.shape[1] // group_count
        shares = contribution.reshape(columns, group_count, piece_width)
        for bit_index in reversed(range(level_index)):
            half_count = shares.shape[1] // 2
            lower_half = shares[:, :half_count]
            upper_half = shares[:, half_count:]
            upper_side = position >> bit_index & 1 == 1
            retained = jnp.where(upper_side, upper_half, lower_half)
            outgoing_half = jnp.where(upper_side, lower_half, upper_half)
            shares = retained + swapped(outgoing_half, "leaf", bit_index)
        own_group = shares.reshape(columns, piece_width)
        outputs.append(own_group[:, : piece_width // 2])
        top_part = own_group[:, piece_width // 2 :]
        current = top_part.astype(jnp.bfloat16)
    return (eliminated, outputs[0], outputs[1], outputs[2], top_part)


def solution(mesh):
    placed = (
        P("rhs", "leaf"),
        P(),
        P("leaf", None, None),
        P("leaf", None, None),
        P("leaf", "rhs", None),
        P("leaf", None, None),
        P("leaf", None),
        P("leaf", None),
        P("leaf", None),
    )
    return jax.shard_map(
        shards,
        mesh=mesh,
        in_specs=placed,
        out_specs=(
            P("rhs", "leaf"),
            P("rhs", "leaf"),
            P("rhs", "leaf"),
            P("rhs", "leaf"),
            P("rhs", "leaf"),
        ),
        check_vma=False,
    )
```

profile of v0, /device:TPU:0, one launch (start us, length us, event | category | flops | bytes accessed | tf_op | source)
XLA Modules:
  0.0 81.4 jit_solution(16737803261247207425)
XLA Ops:
  7.2 1.8 %reshape.62 = bf16[8,128,128]{2,1,0:T(8,128)(2,1)} reshape(bf16[128,1024]{1,0:T(8,128)(2,1)} %param.9) | data formatting | bytes 524288 | tf_op jit(solution)/shard_map/reshape | solution.py:35
  9.0 7.3 %all-to-all-start = ((bf16[8,128,128]{2,1,0:T(8,128)(2,1)}), bf16[8,128,128]{2,1,0:T(8,128)(2,1)S(1)}, u32[]{:S(2)}, u32[]{:S(2)}) async-start(bf16[8,128,128]{2,1,0:T(8,128)(2,1)} %reshape.62), calls=%async_computation | async-start | bytes 524288 | tf_op jit(solution)/shard_map/all_to_all | solution.py:36
  16.4 0.7 all-gather.2.cloned.1.call-update
  17.3 7.9 %all-to-all-done = bf16[8,128,128]{2,1,0:T(8,128)(2,1)S(1)} async-done(((bf16[8,128,128]{2,1,0:T(8,128)(2,1)}), bf16[8,128,128]{2,1,0:T(8,128)(2,1)S(1)}, u32[]{:S(2)}, u32[]{:S(2)}) %all-to-all-start) | async-done | bytes 262176 | tf_op jit(solution)/shard_map/all_to_all | solution.py:36
  25.8 0.6 gather_fusion
  26.9 0.8 %reshape.65 = bf16[8,128,128]{2,1,0:T(8,128)(2,1)} reshape(bf16[8,16,1024]{2,1,0:T(8,128)(2,1)S(1)} %copy.33) | data formatting | bytes 524288 | tf_op jit(solution)/shard_map/reshape | solution.py:40
  27.7 3.6 %all-to-all-start.1 = ((bf16[8,128,128]{2,1,0:T(8,128)(2,1)}), bf16[8,128,128]{2,1,0:T(8,128)(2,1)S(1)}, u32[]{:S(2)}, u32[]{:S(2)}) async-start(bf16[8,128,128]{2,1,0:T(8,128)(2,1)} %reshape.65), calls=%async_computation.1 | async-start | bytes 524288 | tf_op jit(solution)/shard_map/all_to_all | solution.py:43
  31.3 8.6 %all-to-all-done.1 = bf16[8,128,128]{2,1,0:T(8,128)(2,1)S(1)} async-done(((bf16[8,128,128]{2,1,0:T(8,128)(2,1)}), bf16[8,128,128]{2,1,0:T(8,128)(2,1)S(1)}, u32[]{:S(2)}, u32[]{:S(2)}) %all-to-all-start.1) | async-done | bytes 262176 | tf_op jit(solution)/shard_map/all_to_all | solution.py:43
  40.7 1.6 %fusion.3 = bf16[128,768]{1,0:T(8,128)(2,1)S(1)} fusion(bf16[1,768,768]{2,1,0:T(8,128)(2,1)} %all-gather.2.cloned.1.call-done, bf16[128,1024]{1,0:T(8,128)(2,1)S(1)} %fusion), kind=kOutput, calls=%fused_computation.5 | convolution fusion | flops 151093248 | bytes 1572864 | tf_op jit(solution)/shard_map/dot_general | solution.py:60
  42.4 0.4 fusion.7
  43.2 1.5 %collective-permute-start = (f32[128,1,256]{2,0,1:T(8,128)S(1)}, f32[128,1,256]{2,0,1:T(8,128)S(1)}, u32[]{:S(2)}, u32[]{:S(2)}) collective-permute-start(f32[128,1,256]{2,0,1:T(8,128)S(1)} %copy_select_fusion), channel_id=1, source_target_pairs={{0,4},{4,0},{8,12},{12,8},{16,20},{20,16},{24,28},{28,24},{1,5},{5... | collective-permute-start | bytes 393224 | tf_op jit(solution)/shard_map/ppermute | solution.py:16
  44.7 3.5 %collective-permute-done = f32[128,1,256]{2,0,1:T(8,128)S(1)} collective-permute-done((f32[128,1,256]{2,0,1:T(8,128)S(1)}, f32[128,1,256]{2,0,1:T(8,128)S(1)}, u32[]{:S(2)}, u32[]{:S(2)}) %collective-permute-start) | collective-permute-done | bytes 131104 | tf_op jit(solution)/shard_map/ppermute | solution.py:16
  48.5 1.2 %collective-permute-start.1 = (f32[128,2,128]{0,2,1:T(8,128)S(1)}, f32[128,2,128]{0,2,1:T(8,128)S(1)}, u32[]{:S(2)}, u32[]{:S(2)}) collective-permute-start(f32[128,2,128]{0,2,1:T(8,128)S(1)} %slice_select_fusion.1), channel_id=1, source_target_pairs={{0,8},{8,0},{4,12},{12,4},{16,24},{24,16},{20,28},{28,20},{1,9},{9... | collective-permute-start | bytes 393224 | tf_op jit(solution)/shard_map/ppermute | solution.py:16
  49.7 3.9 %collective-permute-done.1 = f32[128,2,128]{0,2,1:T(8,128)S(1)} collective-permute-done((f32[128,2,128]{0,2,1:T(8,128)S(1)}, f32[128,2,128]{0,2,1:T(8,128)S(1)}, u32[]{:S(2)}, u32[]{:S(2)}) %collective-permute-start.1) | collective-permute-done | bytes 131104 | tf_op jit(solution)/shard_map/ppermute | solution.py:16
  53.6 1.5 %collective-permute-start.2 = (f32[128,1,128]{0,2,1:T(8,128)S(1)}, f32[128,1,128]{0,2,1:T(8,128)S(1)}, u32[]{:S(2)}, u32[]{:S(2)}) collective-permute-start(f32[128,1,128]{0,2,1:T(8,128)S(1)} %slice_select_fusion.3), channel_id=1, source_target_pairs={{0,4},{4,0},{8,12},{12,8},{16,20},{20,16},{24,28},{28,24},{1,5},{5... | collective-permute-start | bytes 196616 | tf_op jit(solution)/shard_map/ppermute | solution.py:16
  55.1 2.8 %collective-permute-done.2 = f32[128,1,128]{0,2,1:T(8,128)S(1)} collective-permute-done((f32[128,1,128]{0,2,1:T(8,128)S(1)}, f32[128,1,128]{0,2,1:T(8,128)S(1)}, u32[]{:S(2)}, u32[]{:S(2)}) %collective-permute-start.2) | collective-permute-done | bytes 65568 | tf_op jit(solution)/shard_map/ppermute | solution.py:16
  58.2 1.1 %collective-permute-start.3 = (f32[128,4,64]{0,2,1:T(8,128)S(1)}, f32[128,4,64]{0,2,1:T(8,128)S(1)}, u32[]{:S(2)}, u32[]{:S(2)}) collective-permute-start(f32[128,4,64]{0,2,1:T(8,128)S(1)} %slice_select_fusion), channel_id=1, source_target_pairs={{0,16},{16,0},{4,20},{20,4},{8,24},{24,8},{12,28},{28,12},{1,17},{... | collective-permute-start | bytes 393224 | tf_op jit(solution)/shard_map/ppermute | solution.py:16
  59.4 6.2 %collective-permute-done.3 = f32[128,4,64]{0,2,1:T(8,128)S(1)} collective-permute-done((f32[128,4,64]{0,2,1:T(8,128)S(1)}, f32[128,4,64]{0,2,1:T(8,128)S(1)}, u32[]{:S(2)}, u32[]{:S(2)}) %collective-permute-start.3) | collective-permute-done | bytes 131104 | tf_op jit(solution)/shard_map/ppermute | solution.py:16
  65.7 4.3 %collective-permute-done.4 = f32[128,2,64]{0,2,1:T(8,128)S(1)} collective-permute-done((f32[128,2,64]{0,2,1:T(8,128)S(1)}, f32[128,2,64]{0,2,1:T(8,128)S(1)}, u32[]{:S(2)}, u32[]{:S(2)}) %collective-permute-start.4) | collective-permute-done | bytes 65568 | tf_op jit(solution)/shard_map/ppermute | solution.py:16
  70.0 1.1 %collective-permute-start.5 = (f32[128,1,64]{0,2,1:T(8,128)S(1)}, f32[128,1,64]{0,2,1:T(8,128)S(1)}, u32[]{:S(2)}, u32[]{:S(2)}) collective-permute-start(f32[128,1,64]{0,2,1:T(8,128)S(1)} %slice_select_fusion.4), channel_id=1, source_target_pairs={{0,4},{4,0},{8,12},{12,8},{16,20},{20,16},{24,28},{28,24},{1,5},{5... | collective-permute-start | bytes 98312 | tf_op jit(solution)/shard_map/ppermute | solution.py:16
  71.0 0.6 slice.88
  71.7 0.6 slice.94
  72.3 1.7 %collective-permute-done.5 = f32[128,1,64]{0,2,1:T(8,128)S(1)} collective-permute-done((f32[128,1,64]{0,2,1:T(8,128)S(1)}, f32[128,1,64]{0,2,1:T(8,128)S(1)}, u32[]{:S(2)}, u32[]{:S(2)}) %collective-permute-start.5) | collective-permute-done | bytes 32800 | tf_op jit(solution)/shard_map/ppermute | solution.py:16
  74.0 0.6 fusion.20
  (52 shorter events, 3.2 us)
Async XLA Ops:
  7.2 32.8 %copy-start = (bf16[1,1024,256]{2,1,0:T(8,128)(2,1)S(1)}, bf16[1,1024,256]{2,1,0:T(8,128)(2,1)}, u32[]{:S(2)}) copy-start(bf16[1,1024,256]{2,1,0:T(8,128)(2,1)} %param.11) | copy-start | bytes 1572868
  7.2 9.9 %copy-start.7 = (s32[64]{0:T(128)S(1)}, s32[64]{0:T(128)}, u32[]{:S(2)}) copy-start(s32[64]{0:T(128)} %param.10) | copy-start | bytes 772
  9.0 16.2 %all-to-all-start = ((bf16[8,128,128]{2,1,0:T(8,128)(2,1)}), bf16[8,128,128]{2,1,0:T(8,128)(2,1)S(1)}, u32[]{:S(2)}, u32[]{:S(2)}) async-start(bf16[8,128,128]{2,1,0:T(8,128)(2,1)} %reshape.62), calls=%async_computation | async-start | bytes 524288 | tf_op jit(solution)/shard_map/all_to_all | solution.py:36
  16.3 24.4 %all-gather.2.cloned.1.call-start = ((), (), s32[]{:S(2)}) async-start(), calls=%async_computation.2 | async-start | bytes 1474560 | tf_op jit(solution)/shard_map/all_gather | solution.py:62
  26.7 13.3 %copy-start.4 = (bf16[1,256,256]{2,1,0:T(8,128)(2,1)S(1)}, bf16[1,256,256]{2,1,0:T(8,128)(2,1)}, u32[]{:S(2)}) copy-start(bf16[1,256,256]{2,1,0:T(8,128)(2,1)} %param.12) | copy-start | bytes 393220
  27.7 12.2 %all-to-all-start.1 = ((bf16[8,128,128]{2,1,0:T(8,128)(2,1)}), bf16[8,128,128]{2,1,0:T(8,128)(2,1)S(1)}, u32[]{:S(2)}, u32[]{:S(2)}) async-start(bf16[8,128,128]{2,1,0:T(8,128)(2,1)} %reshape.65), calls=%async_computation.1 | async-start | bytes 524288 | tf_op jit(solution)/shard_map/all_to_all | solution.py:43
  40.3 2.0 %copy-start.2 = (bf16[1,768,256]{2,1,0:T(8,128)(2,1)S(1)}, bf16[1,768,256]{2,1,0:T(8,128)(2,1)}, u32[]{:S(2)}) copy-start(bf16[1,768,256]{2,1,0:T(8,128)(2,1)} %param.14) | copy-start | bytes 1179652
  40.4 2.0 %copy-start.3 = (bf16[256,512]{1,0:T(8,128)(2,1)S(1)}, bf16[256,512]{1,0:T(8,128)(2,1)}, u32[]{:S(2)}) copy-start(bf16[256,512]{1,0:T(8,128)(2,1)} %param.15) | copy-start | bytes 786436
  42.3 0.8 %copy-start.1 = (bf16[128,768]{1,0:T(8,128)(2,1)}, bf16[128,768]{1,0:T(8,128)(2,1)S(1)}, u32[]{:S(2)}) copy-start(bf16[128,768]{1,0:T(8,128)(2,1)S(1)} %fusion.3) | copy-start | bytes 589828
  42.8 5.5 %copy-start.5 = (bf16[128,512]{1,0:T(8,128)(2,1)S(1)}, bf16[128,512]{1,0:T(8,128)(2,1)}, u32[]{:S(2)}) copy-start(bf16[128,512]{1,0:T(8,128)(2,1)} %param.16) | copy-start | bytes 393220
  43.2 5.0 %collective-permute-start = (f32[128,1,256]{2,0,1:T(8,128)S(1)}, f32[128,1,256]{2,0,1:T(8,128)S(1)}, u32[]{:S(2)}, u32[]{:S(2)}) collective-permute-start(f32[128,1,256]{2,0,1:T(8,128)S(1)} %copy_select_fusion), channel_id=1, source_target_pairs={{0,4},{4,0},{8,12},{12,8},{16,20},{20,16},{24,28},{28,24},{1,5},{5... | collective-permute-start | bytes 393224 | tf_op jit(solution)/shard_map/ppermute | solution.py:16
  44.7 13.2 %copy-start.6 = (bf16[64,512]{1,0:T(8,128)(2,1)S(1)}, bf16[64,512]{1,0:T(8,128)(2,1)}, u32[]{:S(2)}) copy-start(bf16[64,512]{1,0:T(8,128)(2,1)} %param.17) | copy-start | bytes 196612
  48.5 5.0 %collective-permute-start.1 = (f32[128,2,128]{0,2,1:T(8,128)S(1)}, f32[128,2,128]{0,2,1:T(8,128)S(1)}, u32[]{:S(2)}, u32[]{:S(2)}) collective-permute-start(f32[128,2,128]{0,2,1:T(8,128)S(1)} %slice_select_fusion.1), channel_id=1, source_target_pairs={{0,8},{8,0},{4,12},{12,4},{16,24},{24,16},{20,28},{28,20},{1,9},{9... | collective-permute-start | bytes 393224 | tf_op jit(solution)/shard_map/ppermute | solution.py:16
  53.6 4.3 %collective-permute-start.2 = (f32[128,1,128]{0,2,1:T(8,128)S(1)}, f32[128,1,128]{0,2,1:T(8,128)S(1)}, u32[]{:S(2)}, u32[]{:S(2)}) collective-permute-start(f32[128,1,128]{0,2,1:T(8,128)S(1)} %slice_select_fusion.3), channel_id=1, source_target_pairs={{0,4},{4,0},{8,12},{12,8},{16,20},{20,16},{24,28},{28,24},{1,5},{5... | collective-permute-start | bytes 196616 | tf_op jit(solution)/shard_map/ppermute | solution.py:16
  58.2 7.3 %collective-permute-start.3 = (f32[128,4,64]{0,2,1:T(8,128)S(1)}, f32[128,4,64]{0,2,1:T(8,128)S(1)}, u32[]{:S(2)}, u32[]{:S(2)}) collective-permute-start(f32[128,4,64]{0,2,1:T(8,128)S(1)} %slice_select_fusion), channel_id=1, source_target_pairs={{0,16},{16,0},{4,20},{20,4},{8,24},{24,8},{12,28},{28,12},{1,17},{... | collective-permute-start | bytes 393224 | tf_op jit(solution)/shard_map/ppermute | solution.py:16
  65.6 4.3 %collective-permute-start.4 = (f32[128,2,64]{0,2,1:T(8,128)S(1)}, f32[128,2,64]{0,2,1:T(8,128)S(1)}, u32[]{:S(2)}, u32[]{:S(2)}) collective-permute-start(f32[128,2,64]{0,2,1:T(8,128)S(1)} %slice_select_fusion.2), channel_id=1, source_target_pairs={{0,8},{8,0},{4,12},{12,4},{16,24},{24,16},{20,28},{28,20},{1,9},{9... | collective-permute-start | bytes 196616 | tf_op jit(solution)/shard_map/ppermute | solution.py:16
  70.0 4.0 %collective-permute-start.5 = (f32[128,1,64]{0,2,1:T(8,128)S(1)}, f32[128,1,64]{0,2,1:T(8,128)S(1)}, u32[]{:S(2)}, u32[]{:S(2)}) collective-permute-start(f32[128,1,64]{0,2,1:T(8,128)S(1)} %slice_select_fusion.4), channel_id=1, source_target_pairs={{0,4},{4,0},{8,12},{12,8},{16,20},{20,16},{24,28},{28,24},{1,5},{5... | collective-permute-start | bytes 98312 | tf_op jit(solution)/shard_map/ppermute | solution.py:16
Sparse Core Ops, SparseCore 0:
  18.7 18.8 all-gather.1
where the time goes:
time: 81.8 us; the launch traced here: 81.4 us
  waiting for transfers between devices  39.4 us (48%)
  starting transfers between devices  17.4 us (21%)
  between operations  14.4 us (18%)
  local copies, waits for them, and re-layouts  6.84 us (8%)
  matrix products  3.14 us (4%)
    ppermute x6, waiting for transfers between devices, swapped(): return lax.ppermute(block, axis, route)  22.3 us
    all_to_all x1, waiting for transfers between devices, shards(): lax.all_to_all(returning, 'leaf', split_axis=0, concat_axis=1, tiled=True)  8.57 us
    all_to_all x1, waiting for transfers between devices, shards(): lax.all_to_all(outgoing, 'leaf', split_axis=0, concat_axis=1, tiled=True)  7.89 us
    all_to_all x1, starting transfers between devices, shards(): lax.all_to_all(outgoing, 'leaf', split_axis=0, concat_axis=1, tiled=True)  7.28 us
    ppermute x6, starting transfers between devices, swapped(): return lax.ppermute(block, axis, route)  6.5 us
    all_to_all x1, starting transfers between devices, shards(): lax.all_to_all(returning, 'leaf', split_axis=0, concat_axis=1, tiled=True)  3.59 us
    reshape x1, local copies, waits for them, and re-layouts, shards(): right_sides.reshape(leaf_count, group_size // tile_width, tile_width)  1.84 us
  transfers between devices with their start and end apart: 9, of which 8 were waited for; matrix products, arithmetic and copies ran while one was open for 6% of the time, Pallas kernels for 0%

commit v1 on v0

v1 whole, which is shorter than its diff:
```python
import jax
import jax.numpy as jnp
from jax import lax
from jax.experimental import pallas as pl
from jax.experimental.pallas import tpu as pltpu
from jax.sharding import PartitionSpec as P

BLOCK = 128
NODE_LEAVES = 8


def partner_route(count, bit):
    return [(i, i ^ 1 << bit) for i in range(count) if i ^ 1 << bit < count]


def doubled(piece, axis, bit):
    upper = lax.axis_index(axis) >> bit & 1 == 1
    other = lax.ppermute(piece, axis, partner_route(lax.axis_size(axis), bit))
    first = jnp.where(upper, other, piece)
    second = jnp.where(upper, piece, other)
    return jnp.concatenate([first, second], axis=0)


def reorder_kernel(order_ref, rows_ref, out_ref):
    per_leaf = rows_ref.shape[2] // BLOCK
    for t in range(out_ref.shape[0] * per_leaf):
        source = order_ref[t]
        column = pl.multiple_of(lax.rem(source, per_leaf) * BLOCK, BLOCK)
        out_ref[t // per_leaf, :, pl.ds(t % per_leaf * BLOCK, BLOCK)] = rows_ref[
            lax.div(source, per_leaf), :, pl.ds(column, BLOCK)
        ]


def reorder(rows, block_order):
    leaf_count, per_group, row_count = rows.shape
    if per_group % 16 or leaf_count > 16:
        blocks = jnp.transpose(rows.reshape(leaf_count, per_group, -1, BLOCK), (0, 2, 1, 3))
        blocks = jnp.take(blocks.reshape(-1, per_group, BLOCK), block_order, axis=0)
        blocks = blocks.reshape(leaf_count, -1, per_group, BLOCK)
        return jnp.transpose(blocks, (0, 2, 1, 3)).reshape(leaf_count, per_group, row_count)
    return pl.pallas_call(
        reorder_kernel,
        out_shape=jax.ShapeDtypeStruct(rows.shape, rows.dtype),
        in_specs=[
            pl.BlockSpec(memory_space=pltpu.SMEM),
            pl.BlockSpec(memory_space=pltpu.VMEM),
        ],
        out_specs=pl.BlockSpec(memory_space=pltpu.VMEM),
    )(block_order, rows)


def shards(
    right_sides,
    block_order,
    leaf_basis,
    leaf_inner,
    leaf_inverse,
    leaf_coupling,
    merge_one,
    merge_two,
    merge_three,
):
    f32, bf16 = jnp.float32, jnp.bfloat16
    leaf_count = lax.axis_size("leaf")
    position = lax.axis_index("leaf")
    columns, row_count = right_sides.shape
    rank = merge_one.shape[0]

    inverse = leaf_inverse[0]
    for bit in reversed(range((lax.axis_size("rhs") - 1).bit_length())):
        upper = lax.axis_index("rhs") >> bit & 1 == 1
        other = lax.ppermute(inverse, "rhs", partner_route(lax.axis_size("rhs"), bit))
        first, second = jnp.where(upper, other, inverse), jnp.where(upper, inverse, other)
        span = leaf_inverse.shape[1]
        first = first.reshape(-1, 1, span, first.shape[1])
        second = second.reshape(-1, 1, span, second.shape[1])
        inverse = jnp.concatenate([first, second], axis=1).reshape(-1, first.shape[3])
    upper_rows = jnp.concatenate([merge_two, merge_three], axis=0)
    pair = lax.ppermute(upper_rows, "leaf", partner_route(leaf_count, 0))
    odd = position & 1 == 1
    low, high = jnp.where(odd, pair, upper_rows), jnp.where(odd, upper_rows, pair)
    cut = merge_two.shape[0]
    two_rows = jnp.concatenate([low[:cut], high[:cut]], axis=0)
    three_rows = doubled(jnp.concatenate([low[cut:], high[cut:]], axis=0), "leaf", 1)

    one_parts = merge_one.reshape(rank, 2, 2, rank // 2)
    one_eliminated = one_parts[:, :, 0].reshape(rank, rank)
    one_skeleton = one_parts[:, :, 1].reshape(rank, rank)
    through_two = lax.dot_general(
        two_rows, one_skeleton, (((0,), (1,)), ((), ())), preferred_element_type=f32
    ).astype(bf16)
    two_parts = through_two.reshape(4, 2, rank // 4, rank)
    through_three = lax.dot_general(
        three_rows,
        two_parts[:, 1].reshape(rank, rank),
        (((0,), (0,)), ((), ())),
        preferred_element_type=f32,
    ).astype(bf16)
    three_parts = through_three.reshape(NODE_LEAVES, rank // 4, rank)
    own_quad = position // 4 % 2
    two_eliminated = two_parts[:, 0]
    nothing = jnp.zeros_like(two_eliminated)
    two_spread = jnp.concatenate(
        [
            jnp.where(own_quad == 0, two_eliminated, nothing),
            jnp.where(own_quad == 1, two_eliminated, nothing),
        ],
        axis=0,
    )
    upper_table = jnp.concatenate([three_parts, two_spread], axis=1).reshape(-1, rank)

    outgoing = right_sides.reshape(leaf_count, columns // leaf_count, row_count)
    arrived = lax.all_to_all(outgoing, "leaf", split_axis=0, concat_axis=0, tiled=True)
    returning = reorder(arrived, block_order)
    placed = lax.all_to_all(returning, "leaf", split_axis=0, concat_axis=0, tiled=True).reshape(
        columns, row_count
    )

    basis = leaf_basis[0]
    projected = jnp.dot(placed, basis, preferred_element_type=f32).astype(bf16)
    middle = jnp.dot(projected, leaf_inner[0], preferred_element_type=f32).astype(bf16)
    correction = lax.dot_general(
        middle, basis, (((1,), (1,)), ((), ())), preferred_element_type=f32
    )
    reflected = (placed.astype(f32) - correction).astype(bf16)
    split_at = row_count - rank
    eliminated = jnp.dot(
        reflected[:, :split_at], inverse, preferred_element_type=f32
    ).astype(bf16)
    coupled = jnp.dot(eliminated, leaf_coupling[0], preferred_element_type=f32)
    skeleton = (reflected[:, split_at:].astype(f32) - coupled).astype(bf16)

    terms = lax.dot_general(
        upper_table, skeleton, (((1,), (1,)), ((), ())), preferred_element_type=f32
    ).astype(bf16)
    groups = None
    if leaf_count > NODE_LEAVES:
        groups = [
            list(range(i, i + NODE_LEAVES)) for i in range(0, leaf_count, NODE_LEAVES)
        ]
    received = lax.all_to_all(
        terms.reshape(NODE_LEAVES, -1, columns),
        "leaf",
        split_axis=0,
        concat_axis=0,
        tiled=True,
        axis_index_groups=groups,
    )
    one_terms = jnp.dot(skeleton, one_eliminated, preferred_element_type=f32)
    halves = one_terms[:, : rank // 2], one_terms[:, rank // 2 :]
    kept = jnp.where(odd, halves[1], halves[0])
    sent = jnp.where(odd, halves[0], halves[1])
    level_one = kept + lax.ppermute(sent, "leaf", partner_route(leaf_count, 0))
    total = jnp.sum(received.astype(f32), axis=0)
    eighth = rank // 8
    level_three = total[:eighth].T
    top_skeleton = total[eighth : 2 * eighth].T
    level_two = total[2 * eighth :].T
    return (eliminated, level_one, level_two, level_three, top_skeleton)


def solution(mesh):
    placed = (
        P("rhs", "leaf"),
        P(),
        P("leaf", None, None),
        P("leaf", None, None),
        P("leaf", "rhs", None),
        P("leaf", None, None),
        P("leaf", None),
        P("leaf", None),
        P("leaf", None),
    )
    return jax.shard_map(
        shards,
        mesh=mesh,
        in_specs=placed,
        out_specs=(P("rhs", "leaf"),) * 5,
        check_vma=False,
    )
```

time: 81.8 us -> 56.1 us (0.69)
  waiting for transfers between devices: 39.4 us -> 22.3 us
  between operations: 14.4 us -> 0.92 us
  starting transfers between devices: 17.4 us -> 22.1 us
  local copies, waits for them, and re-layouts: 6.84 us -> 4.24 us
  Pallas kernels: 0 us -> 1.93 us
  other arithmetic: 0.23 us -> 1.18 us
    ppermute x6 -> x5, waiting for transfers between devices: 22.3 us -> 12.3 us  [the longest x1 6.04 us: shards(): pair = lax.ppermute(upper_rows, 'leaf', partner_route(leaf_count, 0))]
    all_to_all x2 -> x3, waiting for transfers between devices: 16.5 us -> 10 us  [the longest x1 7.91 us: shards(): lax.all_to_all(returning, 'leaf', split_axis=0, concat_axis=0, tiled=True)]
    reshape x7 -> x0, local copies, waits for them, and re-layouts: 3.35 us -> none  [the longest x1 1.84 us: shards(): right_sides.reshape(leaf_count, group_size // tile_width, tile_width)]
    all_to_all x2 -> x3, starting transfers between devices: 10.9 us -> 13.3 us  [the longest x1 5.83 us: shards(): lax.all_to_all(outgoing, 'leaf', split_axis=0, concat_axis=0, tiled=True)]
    ppermute x6 -> x5, starting transfers between devices: 6.5 us -> 8.76 us  [the longest x2 3.07 us: shards(): lax.ppermute(inverse, 'rhs', partner_route(lax.axis_size('rhs'), bit))]
    unnamed x16, local copies, waits for them, and re-layouts: 0.05 us -> 2.11 us
    slice x4 -> x5, local copies, waits for them, and re-layouts: 2.07 us -> 0.05 us  [the longest x2 0.02 us: shards(): two_rows = jnp.concatenate([low[:cut], high[:cut]], axis=0)]
    pallas_call x0 -> x1, Pallas kernels: none -> 1.93 us  [reorder(): pl.pallas_call(reorder_kernel, out_shape=jax.ShapeDtypeStruct(rows.shape,...]
  transfers between devices with their start and end apart: 9 -> 8, of which waited for: 8 -> 5; matrix products, arithmetic and copies ran while one was open for 6% -> 7% of each run, Pallas kernels for 0% -> 3%
where the time goes in v1:
time: 56.1 us; the launch traced here: 55.6 us
  waiting for transfers between devices  22.3 us (40%)
  starting transfers between devices  22.1 us (39%)
  local copies, waits for them, and re-layouts  4.24 us (8%)
  matrix products  2.95 us (5%)
  Pallas kernels  1.93 us (3%)
  other arithmetic  1.18 us (2%)
  between operations  0.92 us (2%)
    all_to_all x1, waiting for transfers between devices, shards(): lax.all_to_all(returning, 'leaf', split_axis=0, concat_axis=0, tiled=True)  7.91 us
    ppermute x1, waiting for transfers between devices, shards(): pair = lax.ppermute(upper_rows, 'leaf', partner_route(leaf_count, 0))  6.04 us
    all_to_all x1, starting transfers between devices, shards(): lax.all_to_all(outgoing, 'leaf', split_axis=0, concat_axis=0, tiled=True)  5.83 us
    all_to_all x1, starting transfers between devices, shards(): lax.all_to_all(returning, 'leaf', split_axis=0, concat_axis=0, tiled=True)  4.06 us
    all_to_all x1, starting transfers between devices, shards(): lax.all_to_all(terms.reshape(NODE_LEAVES, -1, columns), 'leaf', split_axi...  3.41 us
    ppermute x1, waiting for transfers between devices, shards(): level_one = kept + lax.ppermute(sent, 'leaf', partner_route(leaf_count, 0))  3.41 us
    ppermute x2, starting transfers between devices, shards(): lax.ppermute(inverse, 'rhs', partner_route(lax.axis_size('rhs'), bit))  3.07 us
    ppermute x1, waiting for transfers between devices, doubled(): other = lax.ppermute(piece, axis, partner_route(lax.axis_size(axis), bit))  2.81 us
  transfers between devices with their start and end apart: 8, of which 5 were waited for; matrix products, arithmetic and copies ran while one was open for 7% of the time, Pallas kernels for 3%

profile of v1, /device:TPU:0, one launch (start us, length us, event | category | flops | bytes accessed | tf_op | source)
XLA Modules:
  0.0 55.6 jit_solution(9899995267720817104)
XLA Ops:
  0.7 3.0 %collective-permute-start = (bf16[192,768]{1,0:T(8,128)(2,1)}, bf16[192,768]{1,0:T(8,128)(2,1)S(1)}, u32[]{:S(2)}, u32[]{:S(2)}) collective-permute-start(bf16[192,768]{1,0:T(8,128)(2,1)} %bitcast.74), channel_id=1, source_target_pairs={{0,2},{1,3},{2,0},{3,1},{4,6},{5,7},{6,4},{7,5},{8,10},{9,11},{10,... | collective-permute-start | bytes 884744 | tf_op jit(solution)/shard_map/ppermute | solution.py:72
  3.7 5.8 %all-to-all-start = ((bf16[8,16,1024]{2,1,0:T(8,128)(2,1)}), bf16[8,16,1024]{2,1,0:T(8,128)(2,1)S(1)}, u32[]{:S(2)}, u32[]{:S(2)}) async-start(bf16[8,16,1024]{2,1,0:T(8,128)(2,1)} %bitcast.75), calls=%async_computation | async-start | bytes 524288 | tf_op jit(solution)/shard_map/all_to_all | solution.py:113
  9.5 0.9 %constant_dynamic-update-slice_fusion.1 = bf16[192,512]{1,0:T(8,128)(2,1)S(1)} fusion(bf16[128,512]{1,0:T(8,128)(2,1)} %param.16), kind=kLoop, calls=%fused_computation.44 | loop fusion | bytes 262144
  10.4 0.8 %constant_dynamic-update-slice_fusion = bf16[192,512]{1,0:T(8,128)(2,1)S(1)} fusion(bf16[192,512]{1,0:T(8,128)(2,1)S(1)} %constant_dynamic-update-slice_fusion.1, bf16[64,512]{1,0:T(8,128)(2,1)} %param.17), kind=kLoop, calls=%fused_computation.43 | loop fusion | bytes 131072 | tf_op jit(solution)/shard_map/concatenate | solution.py:78
  11.3 2.0 %collective-permute-start.3 = (bf16[192,512]{1,0:T(8,128)(2,1)S(1)}, bf16[192,512]{1,0:T(8,128)(2,1)S(1)}, u32[]{:S(2)}, u32[]{:S(2)}) collective-permute-start(bf16[192,512]{1,0:T(8,128)(2,1)S(1)} %constant_dynamic-update-slice_fusion), channel_id=1, source_target_pairs={{0,4},{4,0},{8,12},{12,8},{16,20},{20,16},{24,28},{28,24},{1,5},{5... | collective-permute-start | bytes 589832 | tf_op jit(solution)/shard_map/ppermute | solution.py:79
  13.5 6.0 %collective-permute-done.3 = bf16[192,512]{1,0:T(8,128)(2,1)S(1)} collective-permute-done((bf16[192,512]{1,0:T(8,128)(2,1)S(1)}, bf16[192,512]{1,0:T(8,128)(2,1)S(1)}, u32[]{:S(2)}, u32[]{:S(2)}) %collective-permute-start.3) | collective-permute-done | bytes 196640 | tf_op jit(solution)/shard_map/ppermute | solution.py:79
  19.6 1.7 %collective-permute-start.4 = (bf16[128,512]{1,0:T(8,128)(2,1)S(1)}, bf16[128,512]{1,0:T(8,128)(2,1)S(1)}, u32[]{:S(2)}, u32[]{:S(2)}) collective-permute-start(bf16[128,512]{1,0:T(8,128)(2,1)S(1)} %pad_maximum_fusion.2), channel_id=1, source_target_pairs={{0,8},{4,12},{8,0},{12,4},{16,24},{20,28},{24,16},{28,20},{1,9},{5... | collective-permute-start | bytes 393224 | tf_op jit(solution)/shard_map/ppermute | solution.py:18
  21.8 2.8 %collective-permute-done.4 = bf16[128,512]{1,0:T(8,128)(2,1)S(1)} collective-permute-done((bf16[128,512]{1,0:T(8,128)(2,1)S(1)}, bf16[128,512]{1,0:T(8,128)(2,1)S(1)}, u32[]{:S(2)}, u32[]{:S(2)}) %collective-permute-start.4) | collective-permute-done | bytes 131104 | tf_op jit(solution)/shard_map/ppermute | solution.py:18
  25.0 0.7 %copy-done.1 = bf16[8,16,1024]{2,1,0:T(8,128)(2,1)} copy-done((bf16[8,16,1024]{2,1,0:T(8,128)(2,1)}, bf16[8,16,1024]{2,1,0:T(8,128)(2,1)S(1)}, u32[]{:S(2)}) %copy-start.1) | copy-done | bytes 262168
  25.7 1.9 %shard_map.128 = bf16[8,16,1024]{2,1,0:T(8,128)(2,1)} custom-call(s32[64]{0:T(128)} %order_ref.1, bf16[8,16,1024]{2,1,0:T(8,128)(2,1)} %copy-done.1), custom_call_target="tpu_custom_call" | custom-call | tf_op jit(solution)/shard_map/pallas_call | solution.py:41
  27.6 4.1 %all-to-all-start.1 = ((bf16[8,16,1024]{2,1,0:T(8,128)(2,1)}), bf16[8,16,1024]{2,1,0:T(8,128)(2,1)S(1)}, u32[]{:S(2)}, u32[]{:S(2)}) async-start(bf16[8,16,1024]{2,1,0:T(8,128)(2,1)} %shard_map.128), calls=%async_computation.1 | async-start | bytes 524288 | tf_op jit(solution)/shard_map/all_to_all | solution.py:115
  32.0 7.9 %all-to-all-done.1 = bf16[8,16,1024]{2,1,0:T(8,128)(2,1)S(1)} async-done(((bf16[8,16,1024]{2,1,0:T(8,128)(2,1)}), bf16[8,16,1024]{2,1,0:T(8,128)(2,1)S(1)}, u32[]{:S(2)}, u32[]{:S(2)}) %all-to-all-start.1) | async-done | bytes 262176 | tf_op jit(solution)/shard_map/all_to_all | solution.py:115
  39.9 0.4 convolution_convert_fusion.5
  40.3 0.3 fusion
  40.6 0.3 convolution_convert_fusion.3
  40.9 0.3 copy-done.3
  41.7 1.0 %convolution_convert_fusion = bf16[1024,128]{1,0:T(8,128)(2,1)} fusion(bf16[1024,256]{1,0:T(8,128)(2,1)S(1)} %bitcast.69, bf16[128,256]{1,0:T(8,128)(2,1)S(1)} %fusion.1), kind=kOutput, calls=%fused_computation.1 | convolution fusion | flops 67239936 | bytes 851968 | tf_op jit(solution)/shard_map/dot_general | solution.py:133
  42.7 3.4 %all-to-all-start.2 = ((bf16[8,128,128]{2,1,0:T(8,128)(2,1)}), bf16[8,128,128]{2,1,0:T(8,128)(2,1)S(1)}, u32[]{:S(2)}, u32[]{:S(2)}) async-start(bf16[8,128,128]{2,1,0:T(8,128)(2,1)} %bitcast.23), calls=%async_computation.2 | async-start | bytes 524288 | tf_op jit(solution)/shard_map/all_to_all | solution.py:141
  46.2 2.0 %collective-permute-start.2 = (f32[128,128]{1,0:T(8,128)S(1)}, f32[128,128]{1,0:T(8,128)S(1)}, u32[]{:S(2)}, u32[]{:S(2)}) collective-permute-start(f32[128,128]{1,0:T(8,128)S(1)} %slice_select_fusion), channel_id=1, source_target_pairs={{0,4},{4,0},{8,12},{12,8},{16,20},{20,16},{24,28},{28,24},{1,5},{5... | collective-permute-start | bytes 196616 | tf_op jit(solution)/shard_map/ppermute | solution.py:153
  48.1 3.4 %collective-permute-done.2 = f32[128,128]{1,0:T(8,128)S(1)} collective-permute-done((f32[128,128]{1,0:T(8,128)S(1)}, f32[128,128]{1,0:T(8,128)S(1)}, u32[]{:S(2)}, u32[]{:S(2)}) %collective-permute-start.2) | collective-permute-done | bytes 65568 | tf_op jit(solution)/shard_map/ppermute | solution.py:153
  51.5 0.6 %select_add_fusion = f32[128,128]{1,0:T(8,128)} fusion(f32[128,128]{1,0:T(8,128)S(1)} %collective-permute-done.2, f32[128,256]{1,0:T(8,128)S(1)} %fusion.20, pred[]{:T(512)S(6)} %eq.22), kind=kLoop, calls=%fused_computation.38 | loop fusion | flops 32768 | bytes 262145 | tf_op jit(solution)/shard_map/add | solution.py:153
  52.2 2.1 %all-to-all-done.2 = bf16[8,128,128]{2,1,0:T(8,128)(2,1)S(1)} async-done(((bf16[8,128,128]{2,1,0:T(8,128)(2,1)}), bf16[8,128,128]{2,1,0:T(8,128)(2,1)S(1)}, u32[]{:S(2)}, u32[]{:S(2)}) %all-to-all-start.2) | async-done | bytes 262176 | tf_op jit(solution)/shard_map/all_to_all | solution.py:141
  54.3 0.6 %slice_bitcast_fusion = f32[128,64]{0,1:T(8,128)} fusion(f32[128,128]{1,0:T(8,128)S(1)} %convert_reduce_fusion), kind=kLoop, calls=%fused_computation.40 | loop fusion | bytes 65536 | tf_op jit(solution)/shard_map/transpose | solution.py:158
  55.0 0.6 %slice_bitcast_fusion.1 = (f32[128,32]{0,1:T(8,128)}, f32[128,32]{0,1:T(8,128)}) fusion(f32[128,128]{1,0:T(8,128)S(1)} %convert_reduce_fusion), kind=kLoop, calls=%fused_computation.41 | loop fusion | bytes 65536 | tf_op jit(solution)/shard_map/transpose | solution.py:157
  (38 shorter events, 1.8 us)
Async XLA Ops:
  0.6 39.3 %copy-start = (bf16[1,1024,256]{2,1,0:T(8,128)(2,1)S(1)}, bf16[1,1024,256]{2,1,0:T(8,128)(2,1)}, u32[]{:S(2)}) copy-start(bf16[1,1024,256]{2,1,0:T(8,128)(2,1)} %param.11) | copy-start | bytes 1572868
  0.6 12.6 %copy-start.5 = (bf16[256,512]{1,0:T(8,128)(2,1)S(1)}, bf16[256,512]{1,0:T(8,128)(2,1)}, u32[]{:S(2)}) copy-start(bf16[256,512]{1,0:T(8,128)(2,1)} %param.15) | copy-start | bytes 786436
  0.7 21.0 %collective-permute-start = (bf16[192,768]{1,0:T(8,128)(2,1)}, bf16[192,768]{1,0:T(8,128)(2,1)S(1)}, u32[]{:S(2)}, u32[]{:S(2)}) collective-permute-start(bf16[192,768]{1,0:T(8,128)(2,1)} %bitcast.74), channel_id=1, source_target_pairs={{0,2},{1,3},{2,0},{3,1},{4,6},{5,7},{6,4},{7,5},{8,10},{9,11},{10,... | collective-permute-start | bytes 884744 | tf_op jit(solution)/shard_map/ppermute | solution.py:72
  3.7 21.3 %all-to-all-start = ((bf16[8,16,1024]{2,1,0:T(8,128)(2,1)}), bf16[8,16,1024]{2,1,0:T(8,128)(2,1)S(1)}, u32[]{:S(2)}, u32[]{:S(2)}) async-start(bf16[8,16,1024]{2,1,0:T(8,128)(2,1)} %bitcast.75), calls=%async_computation | async-start | bytes 524288 | tf_op jit(solution)/shard_map/all_to_all | solution.py:113
  11.3 8.2 %collective-permute-start.3 = (bf16[192,512]{1,0:T(8,128)(2,1)S(1)}, bf16[192,512]{1,0:T(8,128)(2,1)S(1)}, u32[]{:S(2)}, u32[]{:S(2)}) collective-permute-start(bf16[192,512]{1,0:T(8,128)(2,1)S(1)} %constant_dynamic-update-slice_fusion), channel_id=1, source_target_pairs={{0,4},{4,0},{8,12},{12,8},{16,20},{20,16},{24,28},{28,24},{1,5},{5... | collective-permute-start | bytes 589832 | tf_op jit(solution)/shard_map/ppermute | solution.py:79
  19.5 2.1 %copy-start.4 = (bf16[1,192,768]{2,1,0:T(8,128)(2,1)S(1)}, bf16[1,192,768]{2,1,0:T(8,128)(2,1)}, u32[]{:S(2)}) copy-start(bf16[1,192,768]{2,1,0:T(8,128)(2,1)} %param.13) | copy-start | bytes 884740
  19.6 5.0 %collective-permute-start.4 = (bf16[128,512]{1,0:T(8,128)(2,1)S(1)}, bf16[128,512]{1,0:T(8,128)(2,1)S(1)}, u32[]{:S(2)}, u32[]{:S(2)}) collective-permute-start(bf16[128,512]{1,0:T(8,128)(2,1)S(1)} %pad_maximum_fusion.2), channel_id=1, source_target_pairs={{0,8},{4,12},{8,0},{12,4},{16,24},{20,28},{24,16},{28,20},{1,9},{5... | collective-permute-start | bytes 393224 | tf_op jit(solution)/shard_map/ppermute | solution.py:18
  21.8 10.0 %collective-permute-start.1 = (bf16[384,768]{1,0:T(8,128)(2,1)S(1)}, bf16[384,768]{1,0:T(8,128)(2,1)S(1)}, u32[]{:S(2)}, u32[]{:S(2)}) collective-permute-start(bf16[384,768]{1,0:T(8,128)(2,1)S(1)} %bitcast.64), channel_id=1, source_target_pairs={{0,1},{1,0},{2,3},{3,2},{4,5},{5,4},{6,7},{7,6},{8,9},{9,8},{10,11... | collective-permute-start | bytes 1769480 | tf_op jit(solution)/shard_map/ppermute | solution.py:72
  25.0 0.7 %copy-start.1 = (bf16[8,16,1024]{2,1,0:T(8,128)(2,1)}, bf16[8,16,1024]{2,1,0:T(8,128)(2,1)S(1)}, u32[]{:S(2)}) copy-start(bf16[8,16,1024]{2,1,0:T(8,128)(2,1)S(1)} %all-to-all-done.rows_ref) | copy-start | bytes 786436
  27.6 12.3 %all-to-all-start.1 = ((bf16[8,16,1024]{2,1,0:T(8,128)(2,1)}), bf16[8,16,1024]{2,1,0:T(8,128)(2,1)S(1)}, u32[]{:S(2)}, u32[]{:S(2)}) async-start(bf16[8,16,1024]{2,1,0:T(8,128)(2,1)} %shard_map.128), calls=%async_computation.1 | async-start | bytes 524288 | tf_op jit(solution)/shard_map/all_to_all | solution.py:115
  31.9 8.0 %copy-start.6 = (bf16[1,256,256]{2,1,0:T(8,128)(2,1)S(1)}, bf16[1,256,256]{2,1,0:T(8,128)(2,1)}, u32[]{:S(2)}) copy-start(bf16[1,256,256]{2,1,0:T(8,128)(2,1)} %param.12) | copy-start | bytes 393220
  40.3 1.0 %copy-start.3 = (bf16[1,768,256]{2,1,0:T(8,128)(2,1)S(1)}, bf16[1,768,256]{2,1,0:T(8,128)(2,1)}, u32[]{:S(2)}) copy-start(bf16[1,768,256]{2,1,0:T(8,128)(2,1)} %param.14) | copy-start | bytes 1179652
  41.3 1.4 %copy-start.2 = (bf16[128,768]{1,0:T(8,128)(2,1)}, bf16[128,768]{1,0:T(8,128)(2,1)S(1)}, u32[]{:S(2)}) copy-start(bf16[128,768]{1,0:T(8,128)(2,1)S(1)} %convolution_convert_fusion.3) | copy-start | bytes 589828
  42.7 11.6 %all-to-all-start.2 = ((bf16[8,128,128]{2,1,0:T(8,128)(2,1)}), bf16[8,128,128]{2,1,0:T(8,128)(2,1)S(1)}, u32[]{:S(2)}, u32[]{:S(2)}) async-start(bf16[8,128,128]{2,1,0:T(8,128)(2,1)} %bitcast.23), calls=%async_computation.2 | async-start | bytes 524288 | tf_op jit(solution)/shard_map/all_to_all | solution.py:141
  46.2 5.4 %collective-permute-start.2 = (f32[128,128]{1,0:T(8,128)S(1)}, f32[128,128]{1,0:T(8,128)S(1)}, u32[]{:S(2)}, u32[]{:S(2)}) collective-permute-start(f32[128,128]{1,0:T(8,128)S(1)} %slice_select_fusion), channel_id=1, source_target_pairs={{0,4},{4,0},{8,12},{12,8},{16,20},{20,16},{24,28},{28,24},{1,5},{5... | collective-permute-start | bytes 196616 | tf_op jit(solution)/shard_map/ppermute | solution.py:153

commit v2 on v1

v2 whole, which is shorter than its diff:
```python
import jax
import jax.numpy as jnp
from jax import lax
from jax.experimental import pallas as pl
from jax.experimental.pallas import tpu as pltpu
from jax.sharding import PartitionSpec as P

BLOCK = 128
NODE_LEAVES = 8
INSIDE = pl.BlockSpec(memory_space=pltpu.VMEM)


def exchanged(piece, axis, flip):
    count = lax.axis_size(axis)
    return lax.ppermute(piece, axis, [(i, i ^ flip) for i in range(count) if i ^ flip < count])


def product(left, right, over=((1,), (0,))):
    return lax.dot_general(left, right, (over, ((), ())), preferred_element_type=jnp.float32)


def reorder_kernel(order_ref, rows_ref, out_ref):
    per_leaf = rows_ref.shape[2] // BLOCK
    for t in range(out_ref.shape[0] * per_leaf):
        source = order_ref[t]
        column = pl.multiple_of(lax.rem(source, per_leaf) * BLOCK, BLOCK)
        out_ref[t // per_leaf, :, pl.ds(t % per_leaf * BLOCK, BLOCK)] = rows_ref[
            lax.div(source, per_leaf), :, pl.ds(column, BLOCK)
        ]


def reorder(rows, block_order):
    leaf_count, per_group, row_count = rows.shape
    if per_group % 16 or leaf_count > 16:
        blocks = jnp.transpose(rows.reshape(leaf_count, per_group, -1, BLOCK), (0, 2, 1, 3))
        blocks = jnp.take(blocks.reshape(-1, per_group, BLOCK), block_order, axis=0)
        blocks = blocks.reshape(leaf_count, -1, per_group, BLOCK)
        return jnp.transpose(blocks, (0, 2, 1, 3)).reshape(leaf_count, per_group, row_count)
    return pl.pallas_call(
        reorder_kernel,
        out_shape=pltpu.VMEM(rows.shape, rows.dtype),
        in_specs=[pl.BlockSpec(memory_space=pltpu.SMEM), INSIDE],
        out_specs=INSIDE,
        compiler_params=pltpu.CompilerParams(vmem_limit_bytes=2 << 20),
    )(block_order, pltpu.with_memory_space_constraint(rows, pltpu.VMEM))


def weights_kernel(
    inverse_ref,
    inverse_far_ref,
    inverse_near_ref,
    inverse_last_ref,
    upper_ref,
    upper_near_ref,
    one_ref,
    basis_ref,
    inner_ref,
    coupling_ref,
    inverse_out,
    table_out,
    narrow_out,
    one,
    two_rows,
    three_rows,
    arrivals,
):
    bf16 = jnp.bfloat16
    share = lax.axis_index("rhs")
    position = lax.axis_index("leaf")
    span = inverse_ref.shape[0]
    rank = one.shape[0]
    copies = [pltpu.make_async_copy(one_ref, one, arrivals.at[0])]
    start = pl.multiple_of(share * span, 16)
    copies.append(
        pltpu.make_async_copy(inverse_ref, inverse_out.at[pl.ds(start, span), :], arrivals.at[1])
    )
    at = 0
    for index, piece in enumerate((basis_ref, inner_ref, coupling_ref)):
        height = piece.shape[0]
        copies.append(
            pltpu.make_async_copy(
                piece, narrow_out.at[pl.ds(at, height), :], arrivals.at[2 + index]
            )
        )
        at += height
    for copy in copies:
        copy.start()

    for flip, piece in ((2, inverse_far_ref), (1, inverse_near_ref), (3, inverse_last_ref)):
        start = pl.multiple_of((share ^ flip) * span, 16)
        inverse_out[pl.ds(start, span), :] = piece[...]

    two_half, three_half = rank // 4, rank // 8
    for flip, piece in ((0, upper_ref), (1, upper_near_ref)):
        half = share & 1 ^ flip
        at = 0
        for other in range(4):
            if other < 2:
                start = (position & 1 ^ other) * 2 * two_half + half * two_half
                start = pl.multiple_of(start, 16)
                two_rows[pl.ds(start, two_half), :] = piece[pl.ds(at, two_half), :]
                at += two_half
            start = (position & 3 ^ other) * 2 * three_half + half * three_half
            start = pl.multiple_of(start, 16)
            three_rows[pl.ds(start, three_half), :] = piece[pl.ds(at, three_half), :]
            at += three_half

    copies[0].wait()
    half = rank // 2
    at = narrow_out.shape[0] - rank
    narrow_out[pl.ds(at, rank), :half] = one[:, :half]
    narrow_out[pl.ds(at, rank), half:] = one[:, 2 * half : 3 * half]
    one_skeleton = jnp.concatenate([one[:, half : 2 * half], one[:, 3 * half :]], axis=1)
    through_two = product(one_skeleton, two_rows[...]).astype(bf16)
    width = rank // 4
    two_skeleton = jnp.concatenate(
        [through_two[:, (2 * g + 1) * width : (2 * g + 2) * width] for g in range(4)], axis=1
    )
    through_three = product(two_skeleton, three_rows[...]).astype(bf16)
    own_quad = position // 4 % 2
    for leaf in range(NODE_LEAVES):
        group = leaf % 4
        two = through_two[:, 2 * group * width : (2 * group + 1) * width]
        two = jnp.where(own_quad == leaf // 4, two, jnp.zeros_like(two))
        three = through_three[:, leaf * width : (leaf + 1) * width]
        table_out[:, leaf * 2 * width : (leaf + 1) * 2 * width] = jnp.concatenate(
            [three, two], axis=1
        )
    for copy in copies[1:]:
        copy.wait()


def weights_stage(inverse, inverse_pieces, upper, upper_near, one, basis, inner, coupling):
    rank = one.shape[0]
    bf16 = jnp.bfloat16
    span, extent = inverse.shape
    height = basis.shape[0] + inner.shape[0] + coupling.shape[0] + rank
    shapes = [(4 * span, extent), (rank, 4 * rank), (height, rank)]
    outside = pl.BlockSpec(memory_space=pl.ANY)

    def near(array):
        return pltpu.with_memory_space_constraint(array, pltpu.VMEM)

    def far(array):
        return pltpu.with_memory_space_constraint(array, pltpu.HBM)

    return pl.pallas_call(
        weights_kernel,
        out_shape=[pltpu.VMEM(shape, bf16) for shape in shapes],
        in_specs=[outside] + [INSIDE] * 5 + [outside] * 4,
        out_specs=[INSIDE] * 3,
        scratch_shapes=[pltpu.VMEM((rank, 2 * rank), bf16)] * 3 + [pltpu.SemaphoreType.DMA((5,))],
        compiler_params=pltpu.CompilerParams(vmem_limit_bytes=6 << 20),
    )(
        far(inverse),
        *map(near, inverse_pieces),
        near(upper),
        near(upper_near),
        far(one),
        far(basis),
        far(inner),
        far(coupling),
    )


def leaf_kernel(
    placed_ref, inverse_ref, table_ref, narrow_ref, eliminated_ref, terms_ref, kept_ref, sent_ref
):
    bf16 = jnp.bfloat16
    row_count = placed_ref.shape[1]
    split_at = inverse_ref.shape[0]
    rank = narrow_ref.shape[1]
    placed = placed_ref[...]
    basis = narrow_ref[:row_count]
    inner = narrow_ref[pl.ds(row_count, rank)]
    coupling = narrow_ref[pl.ds(row_count + rank, split_at)]
    one_eliminated = narrow_ref[pl.ds(row_count + rank + split_at, rank)]
    projected = product(placed, basis).astype(bf16)
    middle = product(projected, inner).astype(bf16)
    correction = product(middle, basis, ((1,), (1,)))
    reflected = (placed.astype(jnp.float32) - correction).astype(bf16)
    eliminated = product(reflected[:, :split_at], inverse_ref[...]).astype(bf16)
    eliminated_ref[...] = eliminated
    coupled = product(eliminated, coupling)
    skeleton = (reflected[:, split_at:].astype(jnp.float32) - coupled).astype(bf16)
    terms = product(skeleton, table_ref[...]).astype(bf16)
    width = terms_ref.shape[2]
    for leaf in range(terms_ref.shape[0]):
        terms_ref[leaf] = terms[:, leaf * width : (leaf + 1) * width]
    one_terms = product(skeleton, one_eliminated)
    half = one_terms.shape[1] // 2
    odd = lax.axis_index("leaf") & 1 == 1
    kept_ref[...] = jnp.where(odd, one_terms[:, half:], one_terms[:, :half])
    sent_ref[...] = jnp.where(odd, one_terms[:, :half], one_terms[:, half:])


def leaf_stage(placed, inverse, table, narrow):
    columns = placed.shape[0]
    rank = narrow.shape[1]
    return pl.pallas_call(
        leaf_kernel,
        out_shape=(
            jax.ShapeDtypeStruct((columns, inverse.shape[1]), jnp.bfloat16),
            jax.ShapeDtypeStruct((NODE_LEAVES, columns, rank // 2), jnp.bfloat16),
            pltpu.VMEM((columns, rank // 2), jnp.float32),
            pltpu.VMEM((columns, rank // 2), jnp.float32),
        ),
        in_specs=[INSIDE] * 4,
        out_specs=(INSIDE,) * 4,
        compiler_params=pltpu.CompilerParams(vmem_limit_bytes=6 << 20),
    )(placed, inverse, table, narrow)


def tail_kernel(received_ref, three_ref, top_ref, two_ref):
    total = jnp.sum(received_ref[...].astype(jnp.float32), axis=0).T
    eighth = three_ref.shape[0]
    three_ref[...] = total[:eighth]
    top_ref[...] = total[eighth : 2 * eighth]
    two_ref[...] = total[2 * eighth :]


def tail_stage(received):
    _, columns, width = received.shape
    return pl.pallas_call(
        tail_kernel,
        out_shape=[
            jax.ShapeDtypeStruct((width * part // 4, columns), jnp.float32) for part in (1, 1, 2)
        ],
        in_specs=[INSIDE],
        out_specs=[INSIDE] * 3,
        compiler_params=pltpu.CompilerParams(vmem_limit_bytes=2 << 20),
    )(received)


def shards(
    right_sides,
    block_order,
    leaf_basis,
    leaf_inner,
    leaf_inverse,
    leaf_coupling,
    merge_one,
    merge_two,
    merge_three,
):
    leaf_count = lax.axis_size("leaf")
    columns, row_count = right_sides.shape

    outgoing = right_sides.reshape(leaf_count, columns // leaf_count, row_count)
    arrived = lax.all_to_all(outgoing, "leaf", split_axis=0, concat_axis=0, tiled=True)

    inverse = leaf_inverse[0]
    inverse_far = exchanged(inverse, "rhs", 2)
    half = lax.axis_index("rhs") & 1
    two_half, three_half = merge_two.shape[0] // 2, merge_three.shape[0] // 2
    two = lax.dynamic_slice_in_dim(merge_two, half * two_half, two_half)
    three = lax.dynamic_slice_in_dim(merge_three, half * three_half, three_half)
    upper_own = jnp.concatenate([two, three], axis=0)
    upper_pieces = [upper_own, exchanged(upper_own, "leaf", 1)]
    upper_pieces += [exchanged(three, "leaf", flip) for flip in (2, 3)]
    upper = jnp.concatenate(upper_pieces, axis=0)

    inverse, inverse_far, upper, _ = lax.optimization_barrier(
        (inverse, inverse_far, upper, arrived)
    )
    inverse_near = exchanged(inverse, "rhs", 1)
    inverse_last = exchanged(inverse_far, "rhs", 1)
    upper_near = exchanged(upper, "rhs", 1)
    inverse_whole, table, narrow = weights_stage(
        leaf_inverse[0],
        (inverse_far, inverse_near, inverse_last),
        upper,
        upper_near,
        merge_one,
        leaf_basis[0],
        leaf_inner[0],
        leaf_coupling[0],
    )

    returning = reorder(arrived, block_order)
    placed = lax.all_to_all(returning, "leaf", split_axis=0, concat_axis=0, tiled=True).reshape(
        columns, row_count
    )
    eliminated, terms, kept, sent = leaf_stage(placed, inverse_whole, table, narrow)

    groups = None
    if leaf_count > NODE_LEAVES:
        groups = [list(range(i, i + NODE_LEAVES)) for i in range(0, leaf_count, NODE_LEAVES)]
    received = lax.all_to_all(
        terms, "leaf", split_axis=0, concat_axis=0, tiled=True, axis_index_groups=groups
    )
    level_one = kept + exchanged(sent, "leaf", 1)
    level_three, top_skeleton, level_two = (part.T for part in tail_stage(received))
    return (eliminated, level_one, level_two, level_three, top_skeleton)


def solution(mesh):
    placed = (
        P("rhs", "leaf"),
        P(),
        P("leaf", None, None),
        P("leaf", None, None),
        P("leaf", "rhs", None),
        P("leaf", None, None),
        P("leaf", None),
        P("leaf", None),
        P("leaf", None),
    )
    return jax.shard_map(
        shards,
        mesh=mesh,
        in_specs=placed,
        out_specs=(P("rhs", "leaf"),) * 5,
        check_vma=False,
    )
```

time: 56.1 us -> 46.2 us (0.82)
  waiting for transfers between devices: 22.3 us -> 13 us
  Pallas kernels: 1.93 us -> 5.72 us
  matrix products: 2.95 us -> 0 us
  local copies, waits for them, and re-layouts: 4.24 us -> 3.32 us
    ppermute x5 -> x8, waiting for transfers between devices: 12.3 us -> 6.34 us  [exchanged(): lax.ppermute(piece, axis, [(i, i ^ flip) for i in range(count) if i ^ fli...]
    all_to_all x1, waiting for transfers between devices: 7.91 us -> 3.04 us  [shards(): lax.all_to_all(returning, 'leaf', split_axis=0, concat_axis=0, tiled=True)]
    pallas_call x1 -> x4, Pallas kernels: 1.93 us -> 5.72 us  [the longest x1 1.9 us: leaf_stage(): pl.pallas_call(leaf_kernel, out_shape=(jax.ShapeDtypeStruct((columns, inv...]
    dot_general x8 -> x0, matrix products: 2.95 us -> none  [the longest x1 1.01 us: shards(): lax.dot_general(upper_table, skeleton, (((1,), (1,)), ((), ())), preferre...]
    all_to_all x1, starting transfers between devices: 5.83 us -> 7.42 us  [shards(): lax.all_to_all(outgoing, 'leaf', split_axis=0, concat_axis=0, tiled=True)]
    transpose x2 -> x0, local copies, waits for them, and re-layouts: 1.23 us -> none  [the longest x1 0.62 us: shards(): level_two = total[2 * eighth:].T]
    unnamed x16 -> x12, local copies, waits for them, and re-layouts: 2.11 us -> 3.32 us
    all_to_all x1, waiting for transfers between devices: 0.01 us -> 1.19 us  [shards(): lax.all_to_all(outgoing, 'leaf', split_axis=0, concat_axis=0, tiled=True)]
  transfers between devices with their start and end apart: 8 -> 11, of which waited for: 5 -> 6; matrix products, arithmetic and copies ran while one was open for 7% -> 5% of each run, Pallas kernels for 3% -> 7%
where the time goes in v2:
time: 46.2 us; the launch traced here: 45.6 us
  starting transfers between devices  22.2 us (48%)
  waiting for transfers between devices  13 us (28%)
  Pallas kernels  5.72 us (12%)
  local copies, waits for them, and re-layouts  3.32 us (7%)
  between operations  0.75 us (2%)
  other arithmetic  0.65 us (1%)
    ppermute x8, starting transfers between devices, exchanged(): lax.ppermute(piece, axis, [(i, i ^ flip) for i in range(count) if i ^ fli...  7.79 us
    all_to_all x1, starting transfers between devices, shards(): lax.all_to_all(outgoing, 'leaf', split_axis=0, concat_axis=0, tiled=True)  7.42 us
    ppermute x8, waiting for transfers between devices, exchanged(): lax.ppermute(piece, axis, [(i, i ^ flip) for i in range(count) if i ^ fli...  6.34 us
    all_to_all x1, starting transfers between devices, shards(): lax.all_to_all(terms, 'leaf', split_axis=0, concat_axis=0, tiled=True, ax...  3.55 us
    all_to_all x1, starting transfers between devices, shards(): lax.all_to_all(returning, 'leaf', split_axis=0, concat_axis=0, tiled=True)  3.41 us
    unnamed x12, local copies, waits for them, and re-layouts  3.32 us
    all_to_all x1, waiting for transfers between devices, shards(): lax.all_to_all(returning, 'leaf', split_axis=0, concat_axis=0, tiled=True)  3.04 us
    all_to_all x1, waiting for transfers between devices, shards(): lax.all_to_all(terms, 'leaf', split_axis=0, concat_axis=0, tiled=True, ax...  2.47 us
  transfers between devices with their start and end apart: 11, of which 6 were waited for; matrix products, arithmetic and copies ran while one was open for 5% of the time, Pallas kernels for 7%

profile of v2, /device:TPU:0, one launch (start us, length us, event | category | flops | bytes accessed | tf_op | source)
XLA Modules:
  0.0 45.6 jit_solution(8467694043515351993)
XLA Ops:
  0.7 7.4 %all-to-all-start = ((bf16[8,16,1024]{2,1,0:T(8,128)(2,1)}), bf16[8,16,1024]{2,1,0:T(8,128)(2,1)S(1)}, u32[]{:S(2)}, u32[]{:S(2)}) async-start(bf16[8,16,1024]{2,1,0:T(8,128)(2,1)} %bitcast.15), calls=%async_computation | async-start | bytes 524288 | tf_op jit(solution)/shard_map/all_to_all | solution.py:250
  8.1 0.8 %constant_dynamic-update-slice_fusion.4 = (bf16[256,512]{1,0:T(8,128)(2,1)S(1)}, bf16[64,512]{1,0:T(8,128)(2,1)S(1)}) fusion(bf16[128,512]{1,0:T(8,128)(2,1)} %param.16, s32[]{:T(128)S(6)} %select_n.6), kind=kLoop, calls=%fused_computation.5 | loop fusion | bytes 196612
  8.9 0.8 %constant_dynamic-update-slice_fusion.3 = (bf16[256,512]{1,0:T(8,128)(2,1)S(1)}, bf16[32,512]{1,0:T(8,128)(2,1)S(1)}) fusion(bf16[256,512]{1,0:T(8,128)(2,1)S(1)} %get-tuple-element.33, bf16[64,512]{1,0:T(8,128)(2,1)} %param.17, s32[]{:T(128)S(6)} %select_n.7), kind=kLoop, calls=%fused_computation.4 | loop fusion | bytes 98308
  9.7 2.1 %collective-permute-start.1 = (bf16[96,512]{1,0:T(8,128)(2,1)S(1)}, bf16[96,512]{1,0:T(8,128)(2,1)S(1)}, u32[]{:S(2)}, u32[]{:S(2)}) collective-permute-start(bf16[96,512]{1,0:T(8,128)(2,1)S(1)} %pad_maximum_fusion), channel_id=1, source_target_pairs={{0,4},{4,0},{8,12},{12,8},{16,20},{20,16},{24,28},{28,24},{1,5},{5... | collective-permute-start | bytes 294920 | tf_op jit(solution)/shard_map/ppermute | solution.py:15
  11.8 1.5 %collective-permute-start.3 = (bf16[32,512]{1,0:T(8,128)(2,1)S(1)}, bf16[32,512]{1,0:T(8,128)(2,1)S(1)}, u32[]{:S(2)}, u32[]{:S(2)}) collective-permute-start(bf16[32,512]{1,0:T(8,128)(2,1)S(1)} %get-tuple-element.32), channel_id=1, source_target_pairs={{0,12},{4,8},{8,4},{12,0},{16,28},{20,24},{24,20},{28,16},{1,13},{... | collective-permute-start | bytes 98312 | tf_op jit(solution)/shard_map/ppermute | solution.py:15
  13.3 1.5 %collective-permute-start = (bf16[192,768]{1,0:T(8,128)(2,1)}, bf16[192,768]{1,0:T(8,128)(2,1)S(1)}, u32[]{:S(2)}, u32[]{:S(2)}) collective-permute-start(bf16[192,768]{1,0:T(8,128)(2,1)} %bitcast.12), channel_id=1, source_target_pairs={{0,2},{1,3},{2,0},{3,1},{4,6},{5,7},{6,4},{7,5},{8,10},{9,11},{10,... | collective-permute-start | bytes 884744 | tf_op jit(solution)/shard_map/ppermute | solution.py:15
  14.8 1.4 %collective-permute-done.1 = bf16[96,512]{1,0:T(8,128)(2,1)S(1)} collective-permute-done((bf16[96,512]{1,0:T(8,128)(2,1)S(1)}, bf16[96,512]{1,0:T(8,128)(2,1)S(1)}, u32[]{:S(2)}, u32[]{:S(2)}) %collective-permute-start.1) | collective-permute-done | bytes 98336 | tf_op jit(solution)/shard_map/ppermute | solution.py:15
  16.3 1.2 %all-to-all-done.rows_ref = bf16[8,16,1024]{2,1,0:T(8,128)(2,1)S(1)} async-done(((bf16[8,16,1024]{2,1,0:T(8,128)(2,1)}), bf16[8,16,1024]{2,1,0:T(8,128)(2,1)S(1)}, u32[]{:S(2)}, u32[]{:S(2)}) %all-to-all-start) | async-done | bytes 262176 | tf_op jit(solution)/shard_map/all_to_all | solution.py:250
  17.4 1.5 %shard_map.128 = bf16[8,16,1024]{2,1,0:T(8,128)(2,1)} custom-call(s32[64]{0:T(128)S(1)} %copy-done.2, bf16[8,16,1024]{2,1,0:T(8,128)(2,1)S(1)} %all-to-all-done.rows_ref), custom_call_target="tpu_custom_call" | custom-call | tf_op jit(solution)/shard_map/pallas_call | solution.py:39
  19.0 3.4 %all-to-all-start.1 = ((bf16[8,16,1024]{2,1,0:T(8,128)(2,1)}), bf16[8,16,1024]{2,1,0:T(8,128)(2,1)S(1)}, u32[]{:S(2)}, u32[]{:S(2)}) async-start(bf16[8,16,1024]{2,1,0:T(8,128)(2,1)} %shard_map.128), calls=%async_computation.1 | async-start | bytes 524288 | tf_op jit(solution)/shard_map/all_to_all | solution.py:281
  22.5 0.5 %collective-permute-start.5 = (bf16[192,768]{1,0:T(8,128)(2,1)S(1)}, bf16[192,768]{1,0:T(8,128)(2,1)S(1)}, u32[]{:S(2)}, u32[]{:S(2)}) collective-permute-start(bf16[192,768]{1,0:T(8,128)(2,1)S(1)} %collective-permute-done.inverse_far_ref), channel_id=1, source_target_pairs={{0,1},{1,0},{2,3},{3,2},{4,5},{5,4},{6,7},{7,6},{8,9},{9,8},{10,11... | collective-permute-start | bytes 884744 | tf_op jit(solution)/shard_map/ppermute | solution.py:15
  23.0 0.7 %copy-done = bf16[192,768]{1,0:T(8,128)(2,1)} copy-done((bf16[192,768]{1,0:T(8,128)(2,1)}, bf16[192,768]{1,0:T(8,128)(2,1)S(1)}, u32[]{:S(2)}) %copy-start) | copy-done | bytes 294936
  23.8 0.1 collective-permute-start.6
  23.8 1.5 %collective-permute-done.6.upper_near_ref = bf16[256,512]{1,0:T(8,128)(2,1)S(1)} collective-permute-done((bf16[256,512]{1,0:T(8,128)(2,1)S(1)}, bf16[256,512]{1,0:T(8,128)(2,1)S(1)}, u32[]{:S(2)}, u32[]{:S(2)}) %collective-permute-start.6) | collective-permute-done | bytes 262176 | tf_op jit(solution)/shard_map/ppermute | solution.py:15
  25.3 1.0 %copy-done.1 = bf16[192,768]{1,0:T(8,128)(2,1)S(1)} copy-done((bf16[192,768]{1,0:T(8,128)(2,1)S(1)}, bf16[192,768]{1,0:T(8,128)(2,1)}, u32[]{:S(2)}) %copy-start.1) | copy-done | bytes 294936
  26.3 1.6 %shard_map.129 = (bf16[768,768]{1,0:T(8,128)(2,1)S(1)}, bf16[256,1024]{1,0:T(8,128)(2,1)S(1)}, bf16[2304,256]{1,0:T(8,128)(2,1)S(1)}) custom-call(bf16[192,768]{1,0:T(8,128)(2,1)} %bitcast.13, bf16[192,768]{1,0:T(8,128)(2,1)S(1)} %copy-done.1, bf16[192,768]{1,0:T(8,128)(2,1)S(1)} %collective-permute-done.4.inverse_near_ref, ...), custom_call_target="tpu_custom_call" | custom-call | tf_op jit(solution)/shard_map/pallas_call | solution.py:147
  27.8 3.0 %all-to-all-done.1 = bf16[8,16,1024]{2,1,0:T(8,128)(2,1)S(1)} async-done(((bf16[8,16,1024]{2,1,0:T(8,128)(2,1)}), bf16[8,16,1024]{2,1,0:T(8,128)(2,1)S(1)}, u32[]{:S(2)}, u32[]{:S(2)}) %all-to-all-start.1) | async-done | bytes 262176 | tf_op jit(solution)/shard_map/all_to_all | solution.py:281
  30.9 1.9 %shard_map.130 = (bf16[128,768]{1,0:T(8,128)(2,1)}, bf16[8,128,128]{2,1,0:T(8,128)(2,1)}, f32[128,128]{1,0:T(8,128)S(1)}, f32[128,128]{1,0:T(8,128)S(1)}) custom-call(bf16[128,1024]{1,0:T(8,128)(2,1)S(1)} %bitcast.9, bf16[768,768]{1,0:T(8,128)(2,1)S(1)} %get-tuple-element.21.inverse_ref, bf16[256,1024]{1,0:T(8,128)(2,1)S(1)} %get-tuple-element.22.table_ref, ...), custom_call_target="tpu_custom_call" | custom-call | tf_op jit(solution)/shard_map/pallas_call | solution.py:200
  32.8 3.6 %all-to-all-start.2 = ((bf16[8,128,128]{2,1,0:T(8,128)(2,1)}), bf16[8,128,128]{2,1,0:T(8,128)(2,1)S(1)}, u32[]{:S(2)}, u32[]{:S(2)}) async-start(bf16[8,128,128]{2,1,0:T(8,128)(2,1)} %get-tuple-element.27), calls=%async_computation.2 | async-start | bytes 524288 | tf_op jit(solution)/shard_map/all_to_all | solution.py:289
  36.3 2.0 %collective-permute-start.7 = (f32[128,128]{1,0:T(8,128)S(1)}, f32[128,128]{1,0:T(8,128)S(1)}, u32[]{:S(2)}, u32[]{:S(2)}) collective-permute-start(f32[128,128]{1,0:T(8,128)S(1)} %get-tuple-element.26), channel_id=1, source_target_pairs={{0,4},{4,0},{8,12},{12,8},{16,20},{20,16},{24,28},{28,24},{1,5},{5... | collective-permute-start | bytes 196616 | tf_op jit(solution)/shard_map/ppermute | solution.py:15
  38.4 3.5 %collective-permute-done.7 = f32[128,128]{1,0:T(8,128)S(1)} collective-permute-done((f32[128,128]{1,0:T(8,128)S(1)}, f32[128,128]{1,0:T(8,128)S(1)}, u32[]{:S(2)}, u32[]{:S(2)}) %collective-permute-start.7) | collective-permute-done | bytes 65568 | tf_op jit(solution)/shard_map/ppermute | solution.py:15
  41.8 0.6 %add.11 = f32[128,128]{1,0:T(8,128)} add(f32[128,128]{1,0:T(8,128)S(1)} %get-tuple-element.25, f32[128,128]{1,0:T(8,128)S(1)} %collective-permute-done.7) | non-fusion elementwise | flops 16384 | bytes 196608 | tf_op jit(solution)/shard_map/add | solution.py:292
  42.5 2.5 %all-to-all-done.2.received_ref = bf16[8,128,128]{2,1,0:T(8,128)(2,1)S(1)} async-done(((bf16[8,128,128]{2,1,0:T(8,128)(2,1)}), bf16[8,128,128]{2,1,0:T(8,128)(2,1)S(1)}, u32[]{:S(2)}, u32[]{:S(2)}) %all-to-all-start.2) | async-done | bytes 262176 | tf_op jit(solution)/shard_map/all_to_all | solution.py:289
  44.9 0.7 %shard_map.131 = (f32[32,128]{1,0:T(8,128)}, f32[32,128]{1,0:T(8,128)}, f32[64,128]{1,0:T(8,128)}) custom-call(bf16[8,128,128]{2,1,0:T(8,128)(2,1)S(1)} %all-to-all-done.2.received_ref), custom_call_target="tpu_custom_call" | custom-call | tf_op jit(solution)/shard_map/pallas_call | solution.py:224
  (17 shorter events, 0.2 us)
Async XLA Ops:
  0.6 16.8 %copy-start.2 = (s32[64]{0:T(128)S(1)}, s32[64]{0:T(128)}, u32[]{:S(2)}) copy-start(s32[64]{0:T(128)} %order_ref.1) | copy-start | bytes 772
  0.6 21.8 %copy-start.3 = (bf16[1,192,768]{2,1,0:T(8,128)(2,1)S(1)}, bf16[1,192,768]{2,1,0:T(8,128)(2,1)}, u32[]{:S(2)}) copy-start(bf16[1,192,768]{2,1,0:T(8,128)(2,1)} %param.13) | copy-start | bytes 884740
  0.7 16.8 %all-to-all-start = ((bf16[8,16,1024]{2,1,0:T(8,128)(2,1)}), bf16[8,16,1024]{2,1,0:T(8,128)(2,1)S(1)}, u32[]{:S(2)}, u32[]{:S(2)}) async-start(bf16[8,16,1024]{2,1,0:T(8,128)(2,1)} %bitcast.15), calls=%async_computation | async-start | bytes 524288 | tf_op jit(solution)/shard_map/all_to_all | solution.py:250
  9.7 6.5 %collective-permute-start.1 = (bf16[96,512]{1,0:T(8,128)(2,1)S(1)}, bf16[96,512]{1,0:T(8,128)(2,1)S(1)}, u32[]{:S(2)}, u32[]{:S(2)}) collective-permute-start(bf16[96,512]{1,0:T(8,128)(2,1)S(1)} %pad_maximum_fusion), channel_id=1, source_target_pairs={{0,4},{4,0},{8,12},{12,8},{16,20},{20,16},{24,28},{28,24},{1,5},{5... | collective-permute-start | bytes 294920 | tf_op jit(solution)/shard_map/ppermute | solution.py:15
  11.8 10.6 %collective-permute-start.3 = (bf16[32,512]{1,0:T(8,128)(2,1)S(1)}, bf16[32,512]{1,0:T(8,128)(2,1)S(1)}, u32[]{:S(2)}, u32[]{:S(2)}) collective-permute-start(bf16[32,512]{1,0:T(8,128)(2,1)S(1)} %get-tuple-element.32), channel_id=1, source_target_pairs={{0,12},{4,8},{8,4},{12,0},{16,28},{20,24},{24,20},{28,16},{1,13},{... | collective-permute-start | bytes 98312 | tf_op jit(solution)/shard_map/ppermute | solution.py:15
  13.3 9.1 %collective-permute-start.2 = (bf16[32,512]{1,0:T(8,128)(2,1)S(1)}, bf16[32,512]{1,0:T(8,128)(2,1)S(1)}, u32[]{:S(2)}, u32[]{:S(2)}) collective-permute-start(bf16[32,512]{1,0:T(8,128)(2,1)S(1)} %get-tuple-element.32), channel_id=1, source_target_pairs={{0,8},{4,12},{8,0},{12,4},{16,24},{20,28},{24,16},{28,20},{1,9},{5... | collective-permute-start | bytes 98312 | tf_op jit(solution)/shard_map/ppermute | solution.py:15
  13.3 9.1 %collective-permute-start = (bf16[192,768]{1,0:T(8,128)(2,1)}, bf16[192,768]{1,0:T(8,128)(2,1)S(1)}, u32[]{:S(2)}, u32[]{:S(2)}) collective-permute-start(bf16[192,768]{1,0:T(8,128)(2,1)} %bitcast.12), channel_id=1, source_target_pairs={{0,2},{1,3},{2,0},{3,1},{4,6},{5,7},{6,4},{7,5},{8,10},{9,11},{10,... | collective-permute-start | bytes 884744 | tf_op jit(solution)/shard_map/ppermute | solution.py:15
  19.0 11.9 %all-to-all-start.1 = ((bf16[8,16,1024]{2,1,0:T(8,128)(2,1)}), bf16[8,16,1024]{2,1,0:T(8,128)(2,1)S(1)}, u32[]{:S(2)}, u32[]{:S(2)}) async-start(bf16[8,16,1024]{2,1,0:T(8,128)(2,1)} %shard_map.128), calls=%async_computation.1 | async-start | bytes 524288 | tf_op jit(solution)/shard_map/all_to_all | solution.py:281
  22.5 2.8 %collective-permute-start.4 = (bf16[192,768]{1,0:T(8,128)(2,1)S(1)}, bf16[192,768]{1,0:T(8,128)(2,1)S(1)}, u32[]{:S(2)}, u32[]{:S(2)}) collective-permute-start(bf16[192,768]{1,0:T(8,128)(2,1)S(1)} %bitcast.14), channel_id=1, source_target_pairs={{0,1},{1,0},{2,3},{3,2},{4,5},{5,4},{6,7},{7,6},{8,9},{9,8},{10,11... | collective-permute-start | bytes 884744 | tf_op jit(solution)/shard_map/ppermute | solution.py:15
  22.5 2.8 %collective-permute-start.5 = (bf16[192,768]{1,0:T(8,128)(2,1)S(1)}, bf16[192,768]{1,0:T(8,128)(2,1)S(1)}, u32[]{:S(2)}, u32[]{:S(2)}) collective-permute-start(bf16[192,768]{1,0:T(8,128)(2,1)S(1)} %collective-permute-done.inverse_far_ref), channel_id=1, source_target_pairs={{0,1},{1,0},{2,3},{3,2},{4,5},{5,4},{6,7},{7,6},{8,9},{9,8},{10,11... | collective-permute-start | bytes 884744 | tf_op jit(solution)/shard_map/ppermute | solution.py:15
  23.0 0.7 %copy-start = (bf16[192,768]{1,0:T(8,128)(2,1)}, bf16[192,768]{1,0:T(8,128)(2,1)S(1)}, u32[]{:S(2)}) copy-start(bf16[192,768]{1,0:T(8,128)(2,1)S(1)} %collective-permute-done.inverse_far_ref) | copy-start | bytes 884740
  23.8 1.5 %collective-permute-start.6 = (bf16[256,512]{1,0:T(8,128)(2,1)S(1)}, bf16[256,512]{1,0:T(8,128)(2,1)S(1)}, u32[]{:S(2)}, u32[]{:S(2)}) collective-permute-start(bf16[256,512]{1,0:T(8,128)(2,1)S(1)} %constant_dynamic-update-slice_fusion.upper_ref), channel_id=1, source_target_pairs={{0,1},{1,0},{2,3},{3,2},{4,5},{5,4},{6,7},{7,6},{8,9},{9,8},{10,11... | collective-permute-start | bytes 786440 | tf_op jit(solution)/shard_map/ppermute | solution.py:15
  25.3 1.0 %copy-start.1 = (bf16[192,768]{1,0:T(8,128)(2,1)S(1)}, bf16[192,768]{1,0:T(8,128)(2,1)}, u32[]{:S(2)}) copy-start(bf16[192,768]{1,0:T(8,128)(2,1)} %copy-done) | copy-start | bytes 884740
  32.8 12.1 %all-to-all-start.2 = ((bf16[8,128,128]{2,1,0:T(8,128)(2,1)}), bf16[8,128,128]{2,1,0:T(8,128)(2,1)S(1)}, u32[]{:S(2)}, u32[]{:S(2)}) async-start(bf16[8,128,128]{2,1,0:T(8,128)(2,1)} %get-tuple-element.27), calls=%async_computation.2 | async-start | bytes 524288 | tf_op jit(solution)/shard_map/all_to_all | solution.py:289
  36.3 5.5 %collective-permute-start.7 = (f32[128,128]{1,0:T(8,128)S(1)}, f32[128,128]{1,0:T(8,128)S(1)}, u32[]{:S(2)}, u32[]{:S(2)}) collective-permute-start(f32[128,128]{1,0:T(8,128)S(1)} %get-tuple-element.26), channel_id=1, source_target_pairs={{0,4},{4,0},{8,12},{12,8},{16,20},{20,16},{24,28},{28,24},{1,5},{5... | collective-permute-start | bytes 196616 | tf_op jit(solution)/shard_map/ppermute | solution.py:15

commit v3 on v2

v3 whole, which is shorter than its diff:
```python
import jax
import jax.numpy as jnp
from jax import lax
from jax.experimental import pallas as pl
from jax.experimental.pallas import tpu as pltpu
from jax.sharding import PartitionSpec as P

BLOCK = 128
NODE_LEAVES = 8
INSIDE = pl.BlockSpec(memory_space=pltpu.VMEM)
SCALARS = pl.BlockSpec(memory_space=pltpu.SMEM)
OUTSIDE = pl.BlockSpec(memory_space=pl.ANY)


def near(array):
    return pltpu.with_memory_space_constraint(array, pltpu.VMEM)


def far(array):
    return pltpu.with_memory_space_constraint(array, pltpu.HBM)


def exchanged(piece, axis, flip):
    count = lax.axis_size(axis)
    return lax.ppermute(piece, axis, [(i, i ^ flip) for i in range(count) if i ^ flip < count])


def product(left, right, over=((1,), (0,))):
    return lax.dot_general(left, right, (over, ((), ())), preferred_element_type=jnp.float32)


def reorder_kernel(order_ref, rows_ref, out_ref, staged, leaving):
    per_leaf = rows_ref.shape[2] // BLOCK
    copies = []
    for leaf in range(out_ref.shape[0]):
        for t in range(per_leaf):
            source = order_ref[leaf * per_leaf + t]
            column = pl.multiple_of(lax.rem(source, per_leaf) * BLOCK, BLOCK)
            staged[leaf, :, pl.ds(t * BLOCK, BLOCK)] = rows_ref[
                lax.div(source, per_leaf), :, pl.ds(column, BLOCK)
            ]
        copies.append(pltpu.make_async_copy(staged.at[leaf], out_ref.at[leaf], leaving.at[leaf]))
        copies[-1].start()
    for copy in copies:
        copy.wait()


def reorder(rows, block_order):
    leaf_count, per_group, row_count = rows.shape
    if per_group % 16 or leaf_count > 16:
        blocks = jnp.transpose(rows.reshape(leaf_count, per_group, -1, BLOCK), (0, 2, 1, 3))
        blocks = jnp.take(blocks.reshape(-1, per_group, BLOCK), block_order, axis=0)
        blocks = blocks.reshape(leaf_count, -1, per_group, BLOCK)
        return jnp.transpose(blocks, (0, 2, 1, 3)).reshape(leaf_count, per_group, row_count)
    return pl.pallas_call(
        reorder_kernel,
        out_shape=pltpu.HBM(rows.shape, rows.dtype),
        in_specs=[SCALARS, INSIDE],
        out_specs=OUTSIDE,
        scratch_shapes=[
            pltpu.VMEM(rows.shape, rows.dtype),
            pltpu.SemaphoreType.DMA((leaf_count,)),
        ],
        compiler_params=pltpu.CompilerParams(vmem_limit_bytes=2 << 20),
    )(pltpu.with_memory_space_constraint(block_order, pltpu.SMEM), near(rows))


def order_kernel(order_ref, order_out):
    def keep(t, carry):
        order_out[t] = order_ref[t]
        return carry

    lax.fori_loop(0, order_ref.shape[0], keep, 0, unroll=8)


def kept_order(block_order):
    return pl.pallas_call(
        order_kernel,
        out_shape=pltpu.SMEM(block_order.shape, block_order.dtype),
        in_specs=[SCALARS],
        out_specs=SCALARS,
        compiler_params=pltpu.CompilerParams(vmem_limit_bytes=1 << 20),
    )(block_order)


def halves_kernel(two_ref, three_ref, upper_out, three_out, arrivals):
    half = lax.axis_index("rhs") & 1
    two_half, three_half = two_ref.shape[0] // 2, three_ref.shape[0] // 2
    two = two_ref.at[pl.ds(pl.multiple_of(half * two_half, 16), two_half), :]
    three = three_ref.at[pl.ds(pl.multiple_of(half * three_half, 16), three_half), :]
    copies = [
        pltpu.make_async_copy(two, upper_out.at[pl.ds(0, two_half), :], arrivals.at[0]),
        pltpu.make_async_copy(three, upper_out.at[pl.ds(two_half, three_half), :], arrivals.at[1]),
        pltpu.make_async_copy(three, three_out, arrivals.at[2]),
    ]
    for copy in copies:
        copy.start()

    for copy in copies:
        copy.wait()


def halves(two, three):
    two_half, three_half, width = two.shape[0] // 2, three.shape[0] // 2, two.shape[1]
    return pl.pallas_call(
        halves_kernel,
        out_shape=[
            pltpu.VMEM((two_half + three_half, width), two.dtype),
            pltpu.VMEM((three_half, width), two.dtype),
        ],
        in_specs=[OUTSIDE] * 2,
        out_specs=[INSIDE] * 2,
        scratch_shapes=[pltpu.SemaphoreType.DMA((3,))],
        compiler_params=pltpu.CompilerParams(vmem_limit_bytes=1 << 20),
    )(far(two), far(three))


def weights_kernel(
    inverse_ref,
    inverse_far_ref,
    inverse_near_ref,
    inverse_last_ref,
    upper_ref,
    upper_near_ref,
    one_ref,
    basis_ref,
    inner_ref,
    coupling_ref,
    inverse_out,
    three_out,
    two_out,
    narrow_out,
    one,
    two_rows,
    three_rows,
    arrivals,
):
    bf16 = jnp.bfloat16
    share = lax.axis_index("rhs")
    position = lax.axis_index("leaf")
    span = inverse_ref.shape[0]
    rank = one.shape[0]
    copies = [pltpu.make_async_copy(one_ref, one, arrivals.at[0])]
    start = pl.multiple_of(share * span, 16)
    copies.append(
        pltpu.make_async_copy(inverse_ref, inverse_out.at[pl.ds(start, span), :], arrivals.at[1])
    )
    at = 0
    for index, piece in enumerate((basis_ref, inner_ref, coupling_ref)):
        height = piece.shape[0]
        copies.append(
            pltpu.make_async_copy(
                piece, narrow_out.at[pl.ds(at, height), :], arrivals.at[2 + index]
            )
        )
        at += height
    for copy in copies:
        copy.start()

    for flip, piece in ((2, inverse_far_ref), (1, inverse_near_ref), (3, inverse_last_ref)):
        start = pl.multiple_of((share ^ flip) * span, 16)
        inverse_out[pl.ds(start, span), :] = piece[...]

    two_half, three_half = rank // 4, rank // 8
    for flip, piece in ((0, upper_ref), (1, upper_near_ref)):
        half = share & 1 ^ flip
        at = 0
        for other in range(4):
            if other < 2:
                start = (position & 1 ^ other) * 2 * two_half + half * two_half
                start = pl.multiple_of(start, 16)
                two_rows[pl.ds(start, two_half), :] = piece[pl.ds(at, two_half), :]
                at += two_half
            start = (position & 3 ^ other) * 2 * three_half + half * three_half
            start = pl.multiple_of(start, 16)
            three_rows[pl.ds(start, three_half), :] = piece[pl.ds(at, three_half), :]
            at += three_half

    copies[0].wait()
    half = rank // 2
    at = narrow_out.shape[0] - rank
    narrow_out[pl.ds(at, rank), :half] = one[:, :half]
    narrow_out[pl.ds(at, rank), half:] = one[:, 2 * half : 3 * half]
    one_skeleton = jnp.concatenate([one[:, half : 2 * half], one[:, 3 * half :]], axis=1)
    through_two = product(one_skeleton, two_rows[...])
    width = rank // 4
    two_skeleton = jnp.concatenate(
        [through_two[:, (2 * g + 1) * width : (2 * g + 2) * width] for g in range(4)], axis=1
    ).astype(bf16)
    through_two = through_two.T.astype(bf16)
    for group in range(4):
        two_out[pl.ds(group * width, width), :] = through_two[
            2 * group * width : (2 * group + 1) * width
        ]
    three_out[...] = product(two_skeleton, three_rows[...]).T.astype(bf16)
    for copy in copies[1:]:
        copy.wait()


def weights_stage(inverse, inverse_pieces, upper, upper_near, one, basis, inner, coupling):
    rank = one.shape[0]
    bf16 = jnp.bfloat16
    span, extent = inverse.shape
    height = basis.shape[0] + inner.shape[0] + coupling.shape[0] + rank
    shapes = [(4 * span, extent), (2 * rank, rank), (rank, rank), (height, rank)]
    return pl.pallas_call(
        weights_kernel,
        out_shape=[pltpu.VMEM(shape, bf16) for shape in shapes],
        in_specs=[OUTSIDE] + [INSIDE] * 5 + [OUTSIDE] * 4,
        out_specs=[INSIDE] * 4,
        scratch_shapes=[pltpu.VMEM((rank, 2 * rank), bf16)] * 3 + [pltpu.SemaphoreType.DMA((5,))],
        cost_estimate=pl.CostEstimate(
            flops=10**9, bytes_accessed=6 * 10**6, transcendentals=0
        ),
        compiler_params=pltpu.CompilerParams(vmem_limit_bytes=6 << 20),
    )(
        far(inverse),
        *map(near, inverse_pieces),
        near(upper),
        near(upper_near),
        far(one),
        far(basis),
        far(inner),
        far(coupling),
    )


def leaf_kernel(
    placed_ref,
    inverse_ref,
    three_ref,
    two_ref,
    narrow_ref,
    eliminated_ref,
    terms_ref,
    near_ref,
    far_ref,
    last_ref,
    kept_one_ref,
    kept_two_ref,
    eliminated_staged,
    terms_staged,
    two_staged,
    leaving,
):
    bf16 = jnp.bfloat16
    row_count = placed_ref.shape[1]
    split_at = inverse_ref.shape[0]
    rank = narrow_ref.shape[1]
    placed = placed_ref[...]
    basis = narrow_ref[:row_count]
    inner = narrow_ref[pl.ds(row_count, rank)]
    coupling = narrow_ref[pl.ds(row_count + rank, split_at)]
    one_eliminated = narrow_ref[pl.ds(row_count + rank + split_at, rank)]
    projected = product(placed, basis).astype(bf16)
    middle = product(projected, inner).astype(bf16)
    correction = product(middle, basis, ((1,), (1,)))
    reflected = (placed.astype(jnp.float32) - correction).astype(bf16)
    eliminated = product(reflected[:, :split_at], inverse_ref[...]).astype(bf16)
    eliminated_staged[...] = eliminated
    copies = [pltpu.make_async_copy(eliminated_staged, eliminated_ref, leaving.at[0])]
    copies[0].start()
    coupled = product(eliminated, coupling)
    skeleton = (reflected[:, split_at:].astype(jnp.float32) - coupled).astype(bf16)
    terms = product(three_ref[...], skeleton, ((1,), (1,))).astype(bf16)
    terms_staged[...] = terms.reshape(terms_staged.shape)
    copies.append(pltpu.make_async_copy(terms_staged, terms_ref, leaving.at[1]))
    copies[1].start()

    position = lax.axis_index("leaf")
    one_terms = product(skeleton, one_eliminated)
    half = rank // 2
    odd = position & 1 == 1
    kept_one_ref[...] = jnp.where(odd, one_terms[:, half:], one_terms[:, :half])
    sent_one = jnp.where(odd, one_terms[:, :half], one_terms[:, half:]).astype(bf16)
    near_ref[pl.ds(0, sent_one.shape[0]), :] = sent_one
    two_staged[...] = product(two_ref[...], skeleton, ((1,), (1,))).reshape(two_staged.shape)
    own = position & 3
    kept_two_ref[...] = two_staged[own]
    near_ref[pl.ds(sent_one.shape[0], rank // 4), :] = two_staged[own ^ 1].astype(bf16)
    far_ref[...] = two_staged[own ^ 2].astype(bf16)
    last_ref[...] = two_staged[own ^ 3].astype(bf16)
    for copy in copies:
        copy.wait()


def leaf_stage(placed, inverse, three, two, narrow):
    columns = placed.shape[0]
    rank = narrow.shape[1]
    half, width = rank // 2, rank // 4
    f32, bf16 = jnp.float32, jnp.bfloat16
    return pl.pallas_call(
        leaf_kernel,
        out_shape=(
            pltpu.HBM((columns, inverse.shape[1]), bf16),
            pltpu.HBM((NODE_LEAVES, width, columns), bf16),
            pltpu.VMEM((columns + width, columns), bf16),
            pltpu.VMEM((width, columns), bf16),
            pltpu.VMEM((width, columns), bf16),
            pltpu.VMEM((columns, half), f32),
            pltpu.VMEM((width, columns), f32),
        ),
        in_specs=[INSIDE] * 5,
        out_specs=(OUTSIDE,) * 2 + (INSIDE,) * 5,
        scratch_shapes=[
            pltpu.VMEM((columns, inverse.shape[1]), bf16),
            pltpu.VMEM((NODE_LEAVES, width, columns), bf16),
            pltpu.VMEM((4, width, columns), f32),
            pltpu.SemaphoreType.DMA((2,)),
        ],
        compiler_params=pltpu.CompilerParams(vmem_limit_bytes=6 << 20),
    )(near(placed), near(inverse), near(three), near(two), near(narrow))


def tail_kernel(
    received_ref,
    near_ref,
    far_ref,
    last_ref,
    kept_one_ref,
    kept_two_ref,
    one_ref,
    two_ref,
    three_ref,
    top_ref,
):
    f32 = jnp.float32
    columns = kept_one_ref.shape[0]
    one_ref[...] = kept_one_ref[...] + near_ref[pl.ds(0, columns), :].astype(f32)
    two = kept_two_ref[...] + near_ref[pl.ds(columns, two_ref.shape[0]), :].astype(f32)
    two_ref[...] = two + far_ref[...].astype(f32) + last_ref[...].astype(f32)
    total = jnp.sum(received_ref[...].astype(f32), axis=0)
    three_ref[...] = total[: three_ref.shape[0]]
    top_ref[...] = total[three_ref.shape[0] :]


def tail_stage(received, *others):
    _, height, columns = received.shape
    kept_one, kept_two = others[-2:]
    shapes = [kept_one.shape, kept_two.shape] + [(height // 2, columns)] * 2
    return pl.pallas_call(
        tail_kernel,
        out_shape=[jax.ShapeDtypeStruct(shape, jnp.float32) for shape in shapes],
        in_specs=[INSIDE] * 6,
        out_specs=[INSIDE] * 4,
        compiler_params=pltpu.CompilerParams(vmem_limit_bytes=2 << 20),
    )(received, *others)


def shards(
    right_sides,
    block_order,
    leaf_basis,
    leaf_inner,
    leaf_inverse,
    leaf_coupling,
    merge_one,
    merge_two,
    merge_three,
):
    leaf_count = lax.axis_size("leaf")
    columns, row_count = right_sides.shape

    outgoing = right_sides.reshape(leaf_count, columns // leaf_count, row_count)
    arrived = lax.all_to_all(outgoing, "leaf", split_axis=0, concat_axis=0, tiled=True)

    upper_own, three = halves(merge_two, merge_three)
    upper_pieces = [upper_own, exchanged(upper_own, "leaf", 1)]
    upper_pieces += [exchanged(three, "leaf", flip) for flip in (2, 3)]
    inverse, block_order, _ = lax.optimization_barrier((leaf_inverse[0], block_order, upper_own))
    inverse_far = exchanged(inverse, "rhs", 2)
    order = kept_order(block_order)
    upper = jnp.concatenate(upper_pieces, axis=0)

    inverse, inverse_far, upper, _ = lax.optimization_barrier(
        (inverse, inverse_far, upper, arrived)
    )
    inverse_near = exchanged(inverse, "rhs", 1)
    inverse_last = exchanged(inverse_far, "rhs", 1)
    upper_near = exchanged(upper, "rhs", 1)
    inverse_whole, three_table, two_table, narrow = weights_stage(
        leaf_inverse[0],
        (inverse_far, inverse_near, inverse_last),
        upper,
        upper_near,
        merge_one,
        leaf_basis[0],
        leaf_inner[0],
        leaf_coupling[0],
    )

    returning = reorder(arrived, order)
    placed = lax.all_to_all(returning, "leaf", split_axis=0, concat_axis=0, tiled=True).reshape(
        columns, row_count
    )
    eliminated, terms, near_sent, far_sent, last_sent, kept_one, kept_two = leaf_stage(
        placed, inverse_whole, three_table, two_table, narrow
    )

    groups = None
    if leaf_count > NODE_LEAVES:
        groups = [list(range(i, i + NODE_LEAVES)) for i in range(0, leaf_count, NODE_LEAVES)]
    received = lax.all_to_all(
        terms, "leaf", split_axis=0, concat_axis=0, tiled=True, axis_index_groups=groups
    )
    level_one, level_two, level_three, top_skeleton = tail_stage(
        received,
        exchanged(near_sent, "leaf", 1),
        exchanged(far_sent, "leaf", 2),
        exchanged(last_sent, "leaf", 3),
        kept_one,
        kept_two,
    )
    return (eliminated, level_one, level_two.T, level_three.T, top_skeleton.T)


def solution(mesh):
    placed = (
        P("rhs", "leaf"),
        P(),
        P("leaf", None, None),
        P("leaf", None, None),
        P("leaf", "rhs", None),
        P("leaf", None, None),
        P("leaf", None),
        P("leaf", None),
        P("leaf", None),
    )
    return jax.shard_map(
        shards,
        mesh=mesh,
        in_specs=placed,
        out_specs=(P("rhs", "leaf"),) * 5,
        check_vma=False,
    )
```

time: 46.2 us -> 45 us (0.974)
  local copies, waits for them, and re-layouts: 3.32 us -> 0.66 us
  starting transfers between devices: 22.2 us -> 24 us
  Pallas kernels: 5.72 us -> 6.57 us
  other arithmetic: 0.65 us -> 0.02 us
  waiting for transfers between devices: 13 us -> 12.5 us
    unnamed x12 -> x4, local copies, waits for them, and re-layouts: 3.32 us -> 0.66 us
    all_to_all x1, waiting for transfers between devices: 2.47 us -> 0.01 us  [shards(): lax.all_to_all(terms, 'leaf', split_axis=0, concat_axis=0, tiled=True, ax...]
    ppermute x8 -> x10, starting transfers between devices: 7.79 us -> 9.24 us  [exchanged(): lax.ppermute(piece, axis, [(i, i ^ flip) for i in range(count) if i ^ fli...]
    all_to_all x1, waiting for transfers between devices: 3.04 us -> 4.14 us  [shards(): lax.all_to_all(returning, 'leaf', split_axis=0, concat_axis=0, tiled=True)]
    pallas_call x3 -> x5, Pallas kernels: 4.14 us -> 5.02 us  [the longest x1 1.91 us: leaf_stage(): pl.pallas_call(leaf_kernel, out_shape=(pltpu.HBM((columns, inverse.shape[...]
    all_to_all x1, waiting for transfers between devices: 1.19 us -> 2.05 us  [shards(): lax.all_to_all(outgoing, 'leaf', split_axis=0, concat_axis=0, tiled=True)]
    add x1 -> x0, other arithmetic: 0.64 us -> none  [shards(): level_one = kept + exchanged(sent, 'leaf', 1)]
    all_to_all x1, starting transfers between devices: 3.41 us -> 4 us  [shards(): lax.all_to_all(returning, 'leaf', split_axis=0, concat_axis=0, tiled=True)]
  transfers between devices with their start and end apart: 11 -> 13, of which waited for: 6 -> 5; matrix products, arithmetic and copies ran while one was open for 5% -> 0% of each run, Pallas kernels for 7% -> 9%
where the time goes in v3:
time: 45 us; the launch traced here: 44.5 us
  starting transfers between devices  24 us (53%)
  waiting for transfers between devices  12.5 us (28%)
  Pallas kernels  6.57 us (15%)
  between operations  0.75 us (2%)
  local copies, waits for them, and re-layouts  0.66 us (1%)
    ppermute x10, starting transfers between devices, exchanged(): lax.ppermute(piece, axis, [(i, i ^ flip) for i in range(count) if i ^ fli...  9.24 us
    all_to_all x1, starting transfers between devices, shards(): lax.all_to_all(outgoing, 'leaf', split_axis=0, concat_axis=0, tiled=True)  7.42 us
    ppermute x10, waiting for transfers between devices, exchanged(): lax.ppermute(piece, axis, [(i, i ^ flip) for i in range(count) if i ^ fli...  6.29 us
    all_to_all x1, waiting for transfers between devices, shards(): lax.all_to_all(returning, 'leaf', split_axis=0, concat_axis=0, tiled=True)  4.14 us
    all_to_all x1, starting transfers between devices, shards(): lax.all_to_all(returning, 'leaf', split_axis=0, concat_axis=0, tiled=True)  4 us
    all_to_all x1, starting transfers between devices, shards(): lax.all_to_all(terms, 'leaf', split_axis=0, concat_axis=0, tiled=True, ax...  3.38 us
    all_to_all x1, waiting for transfers between devices, shards(): lax.all_to_all(outgoing, 'leaf', split_axis=0, concat_axis=0, tiled=True)  2.05 us
    pallas_call x1, Pallas kernels, leaf_stage(): pl.pallas_call(leaf_kernel, out_shape=(pltpu.HBM((columns, inverse.shape[...  1.91 us
  transfers between devices with their start and end apart: 13, of which 5 were waited for; matrix products, arithmetic and copies ran while one was open for 0% of the time, Pallas kernels for 9%

profile of v3, /device:TPU:0, one launch (start us, length us, event | category | flops | bytes accessed | tf_op | source)
XLA Modules:
  0.0 44.5 jit_solution(12172261609448299977)
XLA Ops:
  0.6 7.4 %all-to-all-start = ((bf16[8,16,1024]{2,1,0:T(8,128)(2,1)}), bf16[8,16,1024]{2,1,0:T(8,128)(2,1)S(1)}, u32[]{:S(2)}, u32[]{:S(2)}) async-start(bf16[8,16,1024]{2,1,0:T(8,128)(2,1)} %bitcast.10), calls=%async_computation | async-start | bytes 524288 | tf_op jit(solution)/shard_map/all_to_all | solution.py:365
  8.1 0.9 %shard_map.128 = (bf16[96,512]{1,0:T(8,128)(2,1)S(1)}, bf16[32,512]{1,0:T(8,128)(2,1)S(1)}) custom-call(bf16[128,512]{1,0:T(8,128)(2,1)} %two_ref.1, bf16[64,512]{1,0:T(8,128)(2,1)} %three_ref.1), custom_call_target="tpu_custom_call" | custom-call | tf_op jit(solution)/shard_map/pallas_call | solution.py:105
  8.9 1.6 %collective-permute-start = (bf16[192,768]{1,0:T(8,128)(2,1)}, bf16[192,768]{1,0:T(8,128)(2,1)S(1)}, u32[]{:S(2)}, u32[]{:S(2)}) collective-permute-start(bf16[192,768]{1,0:T(8,128)(2,1)} %bitcast.13), channel_id=1, source_target_pairs={{0,2},{1,3},{2,0},{3,1},{4,6},{5,7},{6,4},{7,5},{8,10},{9,11},{10,... | collective-permute-start | bytes 884744 | tf_op jit(solution)/shard_map/ppermute | solution.py:25
  10.5 2.0 %collective-permute-start.1 = (bf16[96,512]{1,0:T(8,128)(2,1)S(1)}, bf16[96,512]{1,0:T(8,128)(2,1)S(1)}, u32[]{:S(2)}, u32[]{:S(2)}) collective-permute-start(bf16[96,512]{1,0:T(8,128)(2,1)S(1)} %get-tuple-element.27), channel_id=1, source_target_pairs={{0,4},{4,0},{8,12},{12,8},{16,20},{20,16},{24,28},{28,24},{1,5},{5... | collective-permute-start | bytes 294920 | tf_op jit(solution)/shard_map/ppermute | solution.py:25
  12.5 1.5 %collective-permute-start.3 = (bf16[32,512]{1,0:T(8,128)(2,1)S(1)}, bf16[32,512]{1,0:T(8,128)(2,1)S(1)}, u32[]{:S(2)}, u32[]{:S(2)}) collective-permute-start(bf16[32,512]{1,0:T(8,128)(2,1)S(1)} %get-tuple-element.30), channel_id=1, source_target_pairs={{0,12},{4,8},{8,4},{12,0},{16,28},{20,24},{24,20},{28,16},{1,13},{... | collective-permute-start | bytes 98312 | tf_op jit(solution)/shard_map/ppermute | solution.py:25
  14.0 0.7 %copy-done = s32[64]{0:T(128)S(1)} copy-done((s32[64]{0:T(128)S(1)}, s32[64]{0:T(128)}, u32[]{:S(2)}) %copy-start) | copy-done | bytes 280
  14.6 0.6 %shard_map.129.order_ref = s32[64]{0:T(128)S(4)} custom-call(s32[64]{0:T(128)S(1)} %copy-done), custom_call_target="tpu_custom_call" | custom-call | tf_op jit(solution)/shard_map/pallas_call | solution.py:77
  15.3 2.0 %all-to-all-done.rows_ref = bf16[8,16,1024]{2,1,0:T(8,128)(2,1)S(1)} async-done(((bf16[8,16,1024]{2,1,0:T(8,128)(2,1)}), bf16[8,16,1024]{2,1,0:T(8,128)(2,1)S(1)}, u32[]{:S(2)}, u32[]{:S(2)}) %all-to-all-start) | async-done | bytes 262176 | tf_op jit(solution)/shard_map/all_to_all | solution.py:365
  17.3 0.9 %shard_map.130 = bf16[8,16,1024]{2,1,0:T(8,128)(2,1)} custom-call(s32[64]{0:T(128)S(4)} %shard_map.129.order_ref, bf16[8,16,1024]{2,1,0:T(8,128)(2,1)S(1)} %all-to-all-done.rows_ref), custom_call_target="tpu_custom_call" | custom-call | tf_op jit(solution)/shard_map/pallas_call | solution.py:55
  18.3 4.0 %all-to-all-start.1 = ((bf16[8,16,1024]{2,1,0:T(8,128)(2,1)}), bf16[8,16,1024]{2,1,0:T(8,128)(2,1)S(1)}, u32[]{:S(2)}, u32[]{:S(2)}) async-start(bf16[8,16,1024]{2,1,0:T(8,128)(2,1)} %shard_map.130), calls=%async_computation.1 | async-start | bytes 524288 | tf_op jit(solution)/shard_map/all_to_all | solution.py:393
  22.4 0.1 collective-permute-start.4
  22.4 0.5 %collective-permute-start.5 = (bf16[192,768]{1,0:T(8,128)(2,1)S(1)}, bf16[192,768]{1,0:T(8,128)(2,1)S(1)}, u32[]{:S(2)}, u32[]{:S(2)}) collective-permute-start(bf16[192,768]{1,0:T(8,128)(2,1)S(1)} %collective-permute-done.inverse_far_ref), channel_id=1, source_target_pairs={{0,1},{1,0},{2,3},{3,2},{4,5},{5,4},{6,7},{7,6},{8,9},{9,8},{10,11... | collective-permute-start | bytes 884744 | tf_op jit(solution)/shard_map/ppermute | solution.py:25
  22.9 0.1 collective-permute-start.6
  23.0 1.8 %collective-permute-done.6.upper_near_ref = bf16[256,512]{1,0:T(8,128)(2,1)S(1)} collective-permute-done((bf16[256,512]{1,0:T(8,128)(2,1)S(1)}, bf16[256,512]{1,0:T(8,128)(2,1)S(1)}, u32[]{:S(2)}, u32[]{:S(2)}) %collective-permute-start.6) | collective-permute-done | bytes 262176 | tf_op jit(solution)/shard_map/ppermute | solution.py:25
  24.8 1.5 %shard_map.131 = (bf16[768,768]{1,0:T(8,128)(2,1)S(1)}, bf16[512,256]{1,0:T(8,128)(2,1)S(1)}, bf16[256,256]{1,0:T(8,128)(2,1)S(1)}, bf16[2304,256]{1,0:T(8,128)(2,1)S(1)}) custom-call(bf16[192,768]{1,0:T(8,128)(2,1)} %bitcast.14, bf16[192,768]{1,0:T(8,128)(2,1)S(1)} %collective-permute-done.inverse_far_ref, ...), custom_call_target="tpu_custom_call" | custom-call | flops 1000000000 | bytes 6000000 | tf_op jit(solution)/shard_map/pallas_call | solution.py:206
  26.4 4.1 %all-to-all-done.1 = bf16[8,16,1024]{2,1,0:T(8,128)(2,1)S(1)} async-done(((bf16[8,16,1024]{2,1,0:T(8,128)(2,1)}), bf16[8,16,1024]{2,1,0:T(8,128)(2,1)S(1)}, u32[]{:S(2)}, u32[]{:S(2)}) %all-to-all-start.1) | async-done | bytes 262176 | tf_op jit(solution)/shard_map/all_to_all | solution.py:393
  30.5 1.9 %shard_map.132 = (bf16[128,768]{1,0:T(8,128)(2,1)}, bf16[8,64,128]{2,1,0:T(8,128)(2,1)}, bf16[192,128]{1,0:T(8,128)(2,1)S(1)}, bf16[64,128]{1,0:T(8,128)(2,1)S(1...) custom-call(bf16[128,1024]{1,0:T(8,128)(2,1)S(1)} %bitcast.9, ...), custom_call_target="tpu_custom_call" | custom-call | tf_op jit(solution)/shard_map/pallas_call | solution.py:292
  32.4 3.4 %all-to-all-start.2 = ((bf16[8,64,128]{2,1,0:T(8,128)(2,1)}), bf16[8,64,128]{2,1,0:T(8,128)(2,1)S(1)}, u32[]{:S(2)}, u32[]{:S(2)}) async-start(bf16[8,64,128]{2,1,0:T(8,128)(2,1)} %get-tuple-element.39), calls=%async_computation.2 | async-start | bytes 262144 | tf_op jit(solution)/shard_map/all_to_all | solution.py:403
  35.8 1.9 %collective-permute-start.7 = (bf16[192,128]{1,0:T(8,128)(2,1)S(1)}, bf16[192,128]{1,0:T(8,128)(2,1)S(1)}, u32[]{:S(2)}, u32[]{:S(2)}) collective-permute-start(bf16[192,128]{1,0:T(8,128)(2,1)S(1)} %get-tuple-element.40), channel_id=1, source_target_pairs={{0,4},{4,0},{8,12},{12,8},{16,20},{20,16},{24,28},{28,24},{1,5},{5... | collective-permute-start | bytes 147464 | tf_op jit(solution)/shard_map/ppermute | solution.py:25
  37.7 1.5 %collective-permute-start.8 = (bf16[64,128]{1,0:T(8,128)(2,1)S(1)}, bf16[64,128]{1,0:T(8,128)(2,1)S(1)}, u32[]{:S(2)}, u32[]{:S(2)}) collective-permute-start(bf16[64,128]{1,0:T(8,128)(2,1)S(1)} %get-tuple-element.41), channel_id=1, source_target_pairs={{0,8},{4,12},{8,0},{12,4},{16,24},{20,28},{24,16},{28,20},{1,9},{5... | collective-permute-start | bytes 49160 | tf_op jit(solution)/shard_map/ppermute | solution.py:25
  39.2 0.2 collective-permute-start.9
  39.4 2.1 %collective-permute-done.8.far_ref = bf16[64,128]{1,0:T(8,128)(2,1)S(1)} collective-permute-done((bf16[64,128]{1,0:T(8,128)(2,1)S(1)}, bf16[64,128]{1,0:T(8,128)(2,1)S(1)}, u32[]{:S(2)}, u32[]{:S(2)}) %collective-permute-start.8) | collective-permute-done | bytes 16416 | tf_op jit(solution)/shard_map/ppermute | solution.py:25
  41.5 2.4 %collective-permute-done.9.last_ref = bf16[64,128]{1,0:T(8,128)(2,1)S(1)} collective-permute-done((bf16[64,128]{1,0:T(8,128)(2,1)S(1)}, bf16[64,128]{1,0:T(8,128)(2,1)S(1)}, u32[]{:S(2)}, u32[]{:S(2)}) %collective-permute-start.9) | collective-permute-done | bytes 16416 | tf_op jit(solution)/shard_map/ppermute | solution.py:25
  43.9 0.7 %shard_map.133 = (f32[128,128]{1,0:T(8,128)}, f32[64,128]{1,0:T(8,128)}, f32[32,128]{1,0:T(8,128)}, f32[32,128]{1,0:T(8,128)}) custom-call(bf16[8,64,128]{2,1,0:T(8,128)(2,1)S(1)} %all-to-all-done.2.received_ref, bf16[192,128]{1,0:T(8,128)(2,1)S(1)} %collective-permute-done.7.near_ref, bf16[64,128]{1,0:T(8,128)(2,1)S(1)} %collective-permute-done.8.far_ref, ...), custom_call_target="tpu_custom_call" | custom-call | tf_op jit(solution)/shard_map/pallas_call | solution.py:341
  (13 shorter events, 0.1 us)
Async XLA Ops:
  0.6 21.7 %copy-start.1 = (bf16[1,192,768]{2,1,0:T(8,128)(2,1)S(1)}, bf16[1,192,768]{2,1,0:T(8,128)(2,1)}, u32[]{:S(2)}) copy-start(bf16[1,192,768]{2,1,0:T(8,128)(2,1)} %param.13) | copy-start | bytes 884740
  0.6 16.7 %all-to-all-start = ((bf16[8,16,1024]{2,1,0:T(8,128)(2,1)}), bf16[8,16,1024]{2,1,0:T(8,128)(2,1)S(1)}, u32[]{:S(2)}, u32[]{:S(2)}) async-start(bf16[8,16,1024]{2,1,0:T(8,128)(2,1)} %bitcast.10), calls=%async_computation | async-start | bytes 524288 | tf_op jit(solution)/shard_map/all_to_all | solution.py:365
  8.9 13.4 %collective-permute-start = (bf16[192,768]{1,0:T(8,128)(2,1)}, bf16[192,768]{1,0:T(8,128)(2,1)S(1)}, u32[]{:S(2)}, u32[]{:S(2)}) collective-permute-start(bf16[192,768]{1,0:T(8,128)(2,1)} %bitcast.13), channel_id=1, source_target_pairs={{0,2},{1,3},{2,0},{3,1},{4,6},{5,7},{6,4},{7,5},{8,10},{9,11},{10,... | collective-permute-start | bytes 884744 | tf_op jit(solution)/shard_map/ppermute | solution.py:25
  10.5 11.8 %collective-permute-start.1 = (bf16[96,512]{1,0:T(8,128)(2,1)S(1)}, bf16[96,512]{1,0:T(8,128)(2,1)S(1)}, u32[]{:S(2)}, u32[]{:S(2)}) collective-permute-start(bf16[96,512]{1,0:T(8,128)(2,1)S(1)} %get-tuple-element.27), channel_id=1, source_target_pairs={{0,4},{4,0},{8,12},{12,8},{16,20},{20,16},{24,28},{28,24},{1,5},{5... | collective-permute-start | bytes 294920 | tf_op jit(solution)/shard_map/ppermute | solution.py:25
  12.5 9.8 %collective-permute-start.3 = (bf16[32,512]{1,0:T(8,128)(2,1)S(1)}, bf16[32,512]{1,0:T(8,128)(2,1)S(1)}, u32[]{:S(2)}, u32[]{:S(2)}) collective-permute-start(bf16[32,512]{1,0:T(8,128)(2,1)S(1)} %get-tuple-element.30), channel_id=1, source_target_pairs={{0,12},{4,8},{8,4},{12,0},{16,28},{20,24},{24,20},{28,16},{1,13},{... | collective-permute-start | bytes 98312 | tf_op jit(solution)/shard_map/ppermute | solution.py:25
  14.0 8.3 %collective-permute-start.2 = (bf16[32,512]{1,0:T(8,128)(2,1)S(1)}, bf16[32,512]{1,0:T(8,128)(2,1)S(1)}, u32[]{:S(2)}, u32[]{:S(2)}) collective-permute-start(bf16[32,512]{1,0:T(8,128)(2,1)S(1)} %get-tuple-element.30), channel_id=1, source_target_pairs={{0,8},{4,12},{8,0},{12,4},{16,24},{20,28},{24,16},{28,20},{1,9},{5... | collective-permute-start | bytes 98312 | tf_op jit(solution)/shard_map/ppermute | solution.py:25
  14.0 0.7 %copy-start = (s32[64]{0:T(128)S(1)}, s32[64]{0:T(128)}, u32[]{:S(2)}) copy-start(s32[64]{0:T(128)} %order_ref) | copy-start | bytes 772
  18.3 12.2 %all-to-all-start.1 = ((bf16[8,16,1024]{2,1,0:T(8,128)(2,1)}), bf16[8,16,1024]{2,1,0:T(8,128)(2,1)S(1)}, u32[]{:S(2)}, u32[]{:S(2)}) async-start(bf16[8,16,1024]{2,1,0:T(8,128)(2,1)} %shard_map.130), calls=%async_computation.1 | async-start | bytes 524288 | tf_op jit(solution)/shard_map/all_to_all | solution.py:393
  22.4 2.4 %collective-permute-start.4 = (bf16[192,768]{1,0:T(8,128)(2,1)S(1)}, bf16[192,768]{1,0:T(8,128)(2,1)S(1)}, u32[]{:S(2)}, u32[]{:S(2)}) collective-permute-start(bf16[192,768]{1,0:T(8,128)(2,1)S(1)} %bitcast.15), channel_id=1, source_target_pairs={{0,1},{1,0},{2,3},{3,2},{4,5},{5,4},{6,7},{7,6},{8,9},{9,8},{10,11... | collective-permute-start | bytes 884744 | tf_op jit(solution)/shard_map/ppermute | solution.py:25
  22.4 2.4 %collective-permute-start.5 = (bf16[192,768]{1,0:T(8,128)(2,1)S(1)}, bf16[192,768]{1,0:T(8,128)(2,1)S(1)}, u32[]{:S(2)}, u32[]{:S(2)}) collective-permute-start(bf16[192,768]{1,0:T(8,128)(2,1)S(1)} %collective-permute-done.inverse_far_ref), channel_id=1, source_target_pairs={{0,1},{1,0},{2,3},{3,2},{4,5},{5,4},{6,7},{7,6},{8,9},{9,8},{10,11... | collective-permute-start | bytes 884744 | tf_op jit(solution)/shard_map/ppermute | solution.py:25
  22.9 1.9 %collective-permute-start.6 = (bf16[256,512]{1,0:T(8,128)(2,1)S(1)}, bf16[256,512]{1,0:T(8,128)(2,1)S(1)}, u32[]{:S(2)}, u32[]{:S(2)}) collective-permute-start(bf16[256,512]{1,0:T(8,128)(2,1)S(1)} %pad_maximum_fusion.upper_ref), channel_id=1, source_target_pairs={{0,1},{1,0},{2,3},{3,2},{4,5},{5,4},{6,7},{7,6},{8,9},{9,8},{10,11... | collective-permute-start | bytes 786440 | tf_op jit(solution)/shard_map/ppermute | solution.py:25
  32.4 11.4 %all-to-all-start.2 = ((bf16[8,64,128]{2,1,0:T(8,128)(2,1)}), bf16[8,64,128]{2,1,0:T(8,128)(2,1)S(1)}, u32[]{:S(2)}, u32[]{:S(2)}) async-start(bf16[8,64,128]{2,1,0:T(8,128)(2,1)} %get-tuple-element.39), calls=%async_computation.2 | async-start | bytes 262144 | tf_op jit(solution)/shard_map/all_to_all | solution.py:403
  35.8 8.0 %collective-permute-start.7 = (bf16[192,128]{1,0:T(8,128)(2,1)S(1)}, bf16[192,128]{1,0:T(8,128)(2,1)S(1)}, u32[]{:S(2)}, u32[]{:S(2)}) collective-permute-start(bf16[192,128]{1,0:T(8,128)(2,1)S(1)} %get-tuple-element.40), channel_id=1, source_target_pairs={{0,4},{4,0},{8,12},{12,8},{16,20},{20,16},{24,28},{28,24},{1,5},{5... | collective-permute-start | bytes 147464 | tf_op jit(solution)/shard_map/ppermute | solution.py:25
  37.7 3.7 %collective-permute-start.8 = (bf16[64,128]{1,0:T(8,128)(2,1)S(1)}, bf16[64,128]{1,0:T(8,128)(2,1)S(1)}, u32[]{:S(2)}, u32[]{:S(2)}) collective-permute-start(bf16[64,128]{1,0:T(8,128)(2,1)S(1)} %get-tuple-element.41), channel_id=1, source_target_pairs={{0,8},{4,12},{8,0},{12,4},{16,24},{20,28},{24,16},{28,20},{1,9},{5... | collective-permute-start | bytes 49160 | tf_op jit(solution)/shard_map/ppermute | solution.py:25
  39.2 4.6 %collective-permute-start.9 = (bf16[64,128]{1,0:T(8,128)(2,1)S(1)}, bf16[64,128]{1,0:T(8,128)(2,1)S(1)}, u32[]{:S(2)}, u32[]{:S(2)}) collective-permute-start(bf16[64,128]{1,0:T(8,128)(2,1)S(1)} %get-tuple-element.42), channel_id=1, source_target_pairs={{0,12},{4,8},{8,4},{12,0},{16,28},{20,24},{24,20},{28,16},{1,13},{... | collective-permute-start | bytes 49160 | tf_op jit(solution)/shard_map/ppermute | solution.py:25

commit v4 on v3

v4 whole, which is shorter than its diff:
```python
import jax
import jax.numpy as jnp
from jax import lax
from jax.experimental import pallas as pl
from jax.experimental.pallas import tpu as pltpu
from jax.sharding import PartitionSpec as P

BLOCK = 128
NODE_LEAVES = 8
MEMBERS = (4, 5, 1, 0, 7, 3, 6, 2)
LAST_MEMBERS = (4, 5, 1, 0, 7, 3, 6, 2)
INSIDE = pl.BlockSpec(memory_space=pltpu.VMEM)
SCALARS = pl.BlockSpec(memory_space=pltpu.SMEM)
OUTSIDE = pl.BlockSpec(memory_space=pl.ANY)


def near(array):
    return pltpu.with_memory_space_constraint(array, pltpu.VMEM)


def far(array):
    return pltpu.with_memory_space_constraint(array, pltpu.HBM)


def exchanged(piece, axis, flip):
    count = lax.axis_size(axis)
    return lax.ppermute(piece, axis, [(i, i ^ flip) for i in range(count) if i ^ flip < count])


def product(left, right, over=((1,), (0,))):
    return lax.dot_general(left, right, (over, ((), ())), preferred_element_type=jnp.float32)


def reorder_kernel(order_ref, rows_ref, out_ref, staged, leaving):
    per_leaf = rows_ref.shape[2] // BLOCK
    copies = []
    for slot, leaf in enumerate(MEMBERS):
        for t in range(per_leaf):
            source = order_ref[leaf * per_leaf + t]
            column = pl.multiple_of(lax.rem(source, per_leaf) * BLOCK, BLOCK)
            staged[slot, :, pl.ds(t * BLOCK, BLOCK)] = rows_ref[
                lax.div(source, per_leaf), :, pl.ds(column, BLOCK)
            ]
        copies.append(pltpu.make_async_copy(staged.at[slot], out_ref.at[slot], leaving.at[slot]))
        copies[-1].start()
    for copy in copies:
        copy.wait()


def reorder_anywhere(rows, block_order):
    leaf_count, per_group, row_count = rows.shape
    blocks = jnp.transpose(rows.reshape(leaf_count, per_group, -1, BLOCK), (0, 2, 1, 3))
    blocks = jnp.take(blocks.reshape(-1, per_group, BLOCK), block_order, axis=0)
    blocks = blocks.reshape(leaf_count, -1, per_group, BLOCK)
    return jnp.transpose(blocks, (0, 2, 1, 3)).reshape(leaf_count, per_group, row_count)


def reorder(rows, places):
    leaf_count = rows.shape[0]
    return pl.pallas_call(
        reorder_kernel,
        out_shape=pltpu.HBM(rows.shape, rows.dtype),
        in_specs=[SCALARS, INSIDE],
        out_specs=OUTSIDE,
        scratch_shapes=[
            pltpu.VMEM(rows.shape, rows.dtype),
            pltpu.SemaphoreType.DMA((leaf_count,)),
        ],
        compiler_params=pltpu.CompilerParams(vmem_limit_bytes=2 << 20),
    )(pltpu.with_memory_space_constraint(places, pltpu.SMEM), near(rows))


def early_kernel(order_ref, two_ref, three_ref, places_out, upper_out, three_out, arrivals):
    half = lax.axis_index("rhs") & 1
    two_half, three_half = two_ref.shape[0] // 2, three_ref.shape[0] // 2
    two = two_ref.at[pl.ds(pl.multiple_of(half * two_half, 16), two_half), :]
    three = three_ref.at[pl.ds(pl.multiple_of(half * three_half, 16), three_half), :]
    copies = [
        pltpu.make_async_copy(order_ref, places_out, arrivals.at[0]),
        pltpu.make_async_copy(two, upper_out.at[pl.ds(0, two_half), :], arrivals.at[1]),
        pltpu.make_async_copy(three, upper_out.at[pl.ds(two_half, three_half), :], arrivals.at[2]),
        pltpu.make_async_copy(three, three_out, arrivals.at[3]),
    ]
    for copy in copies:
        copy.start()
    copies[0].wait()
    leaves = len(MEMBERS)
    per_leaf = places_out.shape[0] // leaves
    slots = sum(slot << 3 * leaf for slot, leaf in enumerate(MEMBERS))

    def place(t, carry):
        source = places_out[t]
        leaf = lax.div(source, per_leaf)
        slot = lax.shift_right_logical(jnp.int32(slots), 3 * leaf) & 7
        places_out[t] = slot * per_leaf + lax.rem(source, per_leaf)
        return carry

    if per_leaf * leaves < 128:
        lax.fori_loop(0, per_leaf * leaves, place, 0, unroll=8)
    for copy in copies[1:]:
        copy.wait()


def early_stage(block_order, two, three):
    two_half, three_half, width = two.shape[0] // 2, three.shape[0] // 2, two.shape[1]
    return pl.pallas_call(
        early_kernel,
        out_shape=[
            pltpu.SMEM(block_order.shape, block_order.dtype),
            pltpu.VMEM((two_half + three_half, width), two.dtype),
            pltpu.VMEM((three_half, width), two.dtype),
        ],
        in_specs=[OUTSIDE] * 3,
        out_specs=[SCALARS] + [INSIDE] * 2,
        scratch_shapes=[pltpu.SemaphoreType.DMA((4,))],
        compiler_params=pltpu.CompilerParams(vmem_limit_bytes=1 << 20),
    )(far(block_order), far(two), far(three))


def weights_kernel(
    inverse_ref,
    inverse_far_ref,
    inverse_near_ref,
    inverse_last_ref,
    upper_ref,
    upper_near_ref,
    one_ref,
    basis_ref,
    inner_ref,
    coupling_ref,
    inverse_out,
    table_out,
    narrow_out,
    one,
    two_rows,
    three_rows,
    arrivals,
):
    bf16 = jnp.bfloat16
    share = lax.axis_index("rhs")
    position = lax.axis_index("leaf")
    span = inverse_ref.shape[0]
    rank = one.shape[0]
    copies = [pltpu.make_async_copy(one_ref, one, arrivals.at[0])]
    start = pl.multiple_of(share * span, 16)
    copies.append(
        pltpu.make_async_copy(inverse_ref, inverse_out.at[pl.ds(start, span), :], arrivals.at[1])
    )
    at = 0
    for index, piece in enumerate((basis_ref, inner_ref, coupling_ref)):
        height = piece.shape[0]
        copies.append(
            pltpu.make_async_copy(
                piece, narrow_out.at[pl.ds(at, height), :], arrivals.at[2 + index]
            )
        )
        at += height
    for copy in copies:
        copy.start()

    for flip, piece in ((2, inverse_far_ref), (1, inverse_near_ref), (3, inverse_last_ref)):
        start = pl.multiple_of((share ^ flip) * span, 16)
        inverse_out[pl.ds(start, span), :] = piece[...]

    two_half, three_half = rank // 4, rank // 8
    for flip, piece in ((0, upper_ref), (1, upper_near_ref)):
        half = share & 1 ^ flip
        at = 0
        for other in range(4):
            if other < 2:
                start = (position & 1 ^ other) * 2 * two_half + half * two_half
                start = pl.multiple_of(start, 16)
                two_rows[pl.ds(start, two_half), :] = piece[pl.ds(at, two_half), :]
                at += two_half
            start = (position & 3 ^ other) * 2 * three_half + half * three_half
            start = pl.multiple_of(start, 16)
            three_rows[pl.ds(start, three_half), :] = piece[pl.ds(at, three_half), :]
            at += three_half

    copies[0].wait()
    half = rank // 2
    at = narrow_out.shape[0] - rank
    narrow_out[pl.ds(at, rank), :half] = one[:, :half]
    narrow_out[pl.ds(at, rank), half:] = one[:, 2 * half : 3 * half]
    one_skeleton = jnp.concatenate([one[:, half : 2 * half], one[:, 3 * half :]], axis=1)
    through_two = product(one_skeleton, two_rows[...])
    width = rank // 4
    two_skeleton = jnp.concatenate(
        [through_two[:, (2 * g + 1) * width : (2 * g + 2) * width] for g in range(4)], axis=1
    ).astype(bf16)
    through_two = through_two.T.astype(bf16)
    through_three = product(two_skeleton, three_rows[...]).T.astype(bf16)
    own_quad = position // 4 % 2
    for slot, leaf in enumerate(LAST_MEMBERS):
        at = 2 * slot * width
        table_out[pl.ds(at, width), :] = through_three[leaf * width : (leaf + 1) * width]
        group = leaf % 4
        two = through_two[2 * group * width : (2 * group + 1) * width]
        two = jnp.where(own_quad == leaf // 4, two, jnp.zeros_like(two))
        table_out[pl.ds(at + width, width), :] = two
    for copy in copies[1:]:
        copy.wait()


def weights_stage(inverse, inverse_pieces, upper, upper_near, one, basis, inner, coupling):
    rank = one.shape[0]
    bf16 = jnp.bfloat16
    span, extent = inverse.shape
    height = basis.shape[0] + inner.shape[0] + coupling.shape[0] + rank
    shapes = [(4 * span, extent), (4 * rank, rank), (height, rank)]
    return pl.pallas_call(
        weights_kernel,
        out_shape=[pltpu.VMEM(shape, bf16) for shape in shapes],
        in_specs=[OUTSIDE] + [INSIDE] * 5 + [OUTSIDE] * 4,
        out_specs=[INSIDE] * 3,
        scratch_shapes=[pltpu.VMEM((rank, 2 * rank), bf16)] * 3 + [pltpu.SemaphoreType.DMA((5,))],
        cost_estimate=pl.CostEstimate(
            flops=10**9, bytes_accessed=6 * 10**6, transcendentals=0
        ),
        compiler_params=pltpu.CompilerParams(vmem_limit_bytes=6 << 20),
    )(
        far(inverse),
        *map(near, inverse_pieces),
        near(upper),
        near(upper_near),
        far(one),
        far(basis),
        far(inner),
        far(coupling),
    )


def leaf_kernel(
    placed_ref,
    inverse_ref,
    table_ref,
    narrow_ref,
    eliminated_ref,
    terms_ref,
    sent_one_ref,
    kept_one_ref,
    eliminated_staged,
    terms_staged,
    leaving,
):
    bf16 = jnp.bfloat16
    row_count = placed_ref.shape[1]
    split_at = inverse_ref.shape[0]
    rank = narrow_ref.shape[1]
    placed = placed_ref[...]
    basis = narrow_ref[:row_count]
    inner = narrow_ref[pl.ds(row_count, rank)]
    coupling = narrow_ref[pl.ds(row_count + rank, split_at)]
    one_eliminated = narrow_ref[pl.ds(row_count + rank + split_at, rank)]
    projected = product(placed, basis).astype(bf16)
    middle = product(projected, inner).astype(bf16)
    correction = product(middle, basis, ((1,), (1,)))
    reflected = (placed.astype(jnp.float32) - correction).astype(bf16)
    eliminated = product(reflected[:, :split_at], inverse_ref[...]).astype(bf16)
    eliminated_staged[...] = eliminated
    copies = [pltpu.make_async_copy(eliminated_staged, eliminated_ref, leaving.at[0])]
    copies[0].start()
    coupled = product(eliminated, coupling)
    skeleton = (reflected[:, split_at:].astype(jnp.float32) - coupled).astype(bf16)
    terms = product(table_ref[...], skeleton, ((1,), (1,))).astype(bf16)
    terms_staged[...] = terms.reshape(terms_staged.shape)
    copies.append(pltpu.make_async_copy(terms_staged, terms_ref, leaving.at[1]))
    copies[1].start()

    one_terms = product(skeleton, one_eliminated)
    half = rank // 2
    odd = lax.axis_index("leaf") & 1 == 1
    kept_one_ref[...] = jnp.where(odd, one_terms[:, half:], one_terms[:, :half])
    sent_one_ref[...] = jnp.where(odd, one_terms[:, :half], one_terms[:, half:]).astype(bf16)
    for copy in copies:
        copy.wait()


def leaf_stage(placed, inverse, table, narrow):
    columns = placed.shape[0]
    rank = narrow.shape[1]
    half = rank // 2
    bf16 = jnp.bfloat16
    return pl.pallas_call(
        leaf_kernel,
        out_shape=(
            pltpu.HBM((columns, inverse.shape[1]), bf16),
            pltpu.HBM((NODE_LEAVES, half, columns), bf16),
            pltpu.VMEM((columns, half), bf16),
            pltpu.VMEM((columns, half), jnp.float32),
        ),
        in_specs=[INSIDE] * 4,
        out_specs=(OUTSIDE,) * 2 + (INSIDE,) * 2,
        scratch_shapes=[
            pltpu.VMEM((columns, inverse.shape[1]), bf16),
            pltpu.VMEM((NODE_LEAVES, half, columns), bf16),
            pltpu.SemaphoreType.DMA((2,)),
        ],
        compiler_params=pltpu.CompilerParams(vmem_limit_bytes=6 << 20),
    )(near(placed), near(inverse), near(table), near(narrow))


def tail_kernel(
    received_ref, received_one_ref, kept_one_ref, one_ref, two_ref, three_ref, top_ref
):
    f32 = jnp.float32
    one_ref[...] = kept_one_ref[...] + received_one_ref[...].astype(f32)
    total = jnp.sum(received_ref[...].astype(f32), axis=0)
    eighth = three_ref.shape[0]
    three_ref[...] = total[:eighth]
    top_ref[...] = total[eighth : 2 * eighth]
    two_ref[...] = total[2 * eighth :]


def tail_stage(received, received_one, kept_one):
    _, height, columns = received.shape
    shapes = [kept_one.shape] + [(height // part, columns) for part in (2, 4, 4)]
    return pl.pallas_call(
        tail_kernel,
        out_shape=[jax.ShapeDtypeStruct(shape, jnp.float32) for shape in shapes],
        in_specs=[INSIDE] * 3,
        out_specs=[INSIDE] * 4,
        compiler_params=pltpu.CompilerParams(vmem_limit_bytes=2 << 20),
    )(received, received_one, kept_one)


def shards(
    right_sides,
    block_order,
    leaf_basis,
    leaf_inner,
    leaf_inverse,
    leaf_coupling,
    merge_one,
    merge_two,
    merge_three,
):
    leaf_count = lax.axis_size("leaf")
    columns, row_count = right_sides.shape

    one_node = leaf_count == NODE_LEAVES
    members = [list(MEMBERS)] if one_node else None

    def spread(pieces, groups):
        return lax.all_to_all(
            pieces, "leaf", split_axis=0, concat_axis=0, tiled=True, axis_index_groups=groups
        )

    arrived = spread(right_sides.reshape(leaf_count, columns // leaf_count, row_count), members)

    places, upper_own, three = early_stage(block_order, merge_two, merge_three)
    upper_pieces = [upper_own, exchanged(upper_own, "leaf", 1)]
    upper_pieces += [exchanged(three, "leaf", flip) for flip in (2, 3)]
    inverse, _ = lax.optimization_barrier((leaf_inverse[0], upper_own))
    inverse_far = exchanged(inverse, "rhs", 2)
    upper = jnp.concatenate(upper_pieces, axis=0)

    inverse, inverse_far, upper, _ = lax.optimization_barrier(
        (inverse, inverse_far, upper, arrived)
    )
    inverse_near = exchanged(inverse, "rhs", 1)
    inverse_last = exchanged(inverse_far, "rhs", 1)
    upper_near = exchanged(upper, "rhs", 1)
    inverse_whole, table, narrow = weights_stage(
        leaf_inverse[0],
        (inverse_far, inverse_near, inverse_last),
        upper,
        upper_near,
        merge_one,
        leaf_basis[0],
        leaf_inner[0],
        leaf_coupling[0],
    )

    if one_node:
        returning = reorder(arrived, places)
    else:
        returning = reorder_anywhere(arrived, block_order)
    placed = spread(returning, members).reshape(columns, row_count)
    eliminated, terms, sent_one, kept_one = leaf_stage(placed, inverse_whole, table, narrow)

    starts = range(0, leaf_count, NODE_LEAVES)
    received = spread(terms, [[start + leaf for leaf in LAST_MEMBERS] for start in starts])
    level_one, level_two, level_three, top_skeleton = tail_stage(
        received, exchanged(sent_one, "leaf", 1), kept_one
    )
    return (eliminated, level_one, level_two.T, level_three.T, top_skeleton.T)


def solution(mesh):
    placed = (
        P("rhs", "leaf"),
        P(),
        P("leaf", None, None),
        P("leaf", None, None),
        P("leaf", "rhs", None),
        P("leaf", None, None),
        P("leaf", None),
        P("leaf", None),
        P("leaf", None),
    )
    return jax.shard_map(
        shards,
        mesh=mesh,
        in_specs=placed,
        out_specs=(P("rhs", "leaf"),) * 5,
        check_vma=False,
    )
```

time: 45 us -> 40.3 us (0.90)
  waiting for transfers between devices: 12.5 us -> 7 us
  starting transfers between devices: 24 us -> 25.6 us
  local copies, waits for them, and re-layouts: 0.66 us -> 0.01 us
    all_to_all x3, waiting for transfers between devices: 6.19 us -> 1.91 us  [spread(): lax.all_to_all(pieces, 'leaf', split_axis=0, concat_axis=0, tiled=True, a...]
    all_to_all x3, starting transfers between devices: 14.8 us -> 18.4 us  [spread(): lax.all_to_all(pieces, 'leaf', split_axis=0, concat_axis=0, tiled=True, a...]
    ppermute x10 -> x8, starting transfers between devices: 9.24 us -> 7.15 us  [exchanged(): lax.ppermute(piece, axis, [(i, i ^ flip) for i in range(count) if i ^ fli...]
    ppermute x10 -> x8, waiting for transfers between devices: 6.29 us -> 5.09 us  [exchanged(): lax.ppermute(piece, axis, [(i, i ^ flip) for i in range(count) if i ^ fli...]
    unnamed x4 -> x2, local copies, waits for them, and re-layouts: 0.66 us -> 0.01 us
    pallas_call x2 -> x1, Pallas kernels: 1.5 us -> 1.31 us  [early_stage(): pl.pallas_call(early_kernel, out_shape=[pltpu.SMEM(block_order.shape, blo...]
  transfers between devices with their start and end apart: 13 -> 11, of which waited for: 5 -> 5; matrix products, arithmetic and copies ran while one was open for 0% -> 0% of each run, Pallas kernels for 9% -> 10%
where the time goes in v4:
time: 40.3 us; the launch traced here: 39.8 us
  starting transfers between devices  25.6 us (64%)
  waiting for transfers between devices  7 us (17%)
  Pallas kernels  6.5 us (16%)
  between operations  0.72 us (2%)
    all_to_all x3, starting transfers between devices, spread(): lax.all_to_all(pieces, 'leaf', split_axis=0, concat_axis=0, tiled=True, a...  18.4 us
    ppermute x8, starting transfers between devices, exchanged(): lax.ppermute(piece, axis, [(i, i ^ flip) for i in range(count) if i ^ fli...  7.15 us
    ppermute x8, waiting for transfers between devices, exchanged(): lax.ppermute(piece, axis, [(i, i ^ flip) for i in range(count) if i ^ fli...  5.09 us
    pallas_call x1, Pallas kernels, leaf_stage(): pl.pallas_call(leaf_kernel, out_shape=(pltpu.HBM((columns, inverse.shape[...  2.01 us
    all_to_all x3, waiting for transfers between devices, spread(): lax.all_to_all(pieces, 'leaf', split_axis=0, concat_axis=0, tiled=True, a...  1.91 us
    pallas_call x1, Pallas kernels, weights_stage(): pl.pallas_call(weights_kernel, out_shape=[pltpu.VMEM(shape, bf16) for sha...  1.55 us
    pallas_call x1, Pallas kernels, early_stage(): pl.pallas_call(early_kernel, out_shape=[pltpu.SMEM(block_order.shape, blo...  1.31 us
    pallas_call x1, Pallas kernels, reorder(): pl.pallas_call(reorder_kernel, out_shape=pltpu.HBM(rows.shape, rows.dtype...  0.96 us
  transfers between devices with their start and end apart: 11, of which 5 were waited for; matrix products, arithmetic and copies ran while one was open for 0% of the time, Pallas kernels for 10%

profile of v4, /device:TPU:0, one launch (start us, length us, event | category | flops | bytes accessed | tf_op | source)
XLA Modules:
  0.0 39.8 jit_solution(86155119758311166)
XLA Ops:
  0.6 0.0 copy-start
  0.6 8.0 %all-to-all-start = ((bf16[8,16,1024]{2,1,0:T(8,128)(2,1)}), bf16[8,16,1024]{2,1,0:T(8,128)(2,1)S(1)}, u32[]{:S(2)}, u32[]{:S(2)}) async-start(bf16[8,16,1024]{2,1,0:T(8,128)(2,1)} %bitcast.10), calls=%async_computation | async-start | bytes 524288 | tf_op jit(solution)/shard_map/all_to_all | solution.py:345
  8.6 1.3 %shard_map.128 = (s32[64]{0:T(128)S(4)}, bf16[96,512]{1,0:T(8,128)(2,1)S(1)}, bf16[32,512]{1,0:T(8,128)(2,1)S(1)}) custom-call(s32[64]{0:T(128)} %order_ref.1, bf16[128,512]{1,0:T(8,128)(2,1)} %two_ref.1, bf16[64,512]{1,0:T(8,128)(2,1)} %three_ref.1), custom_call_target="tpu_custom_call" | custom-call | tf_op jit(solution)/shard_map/pallas_call | solution.py:106
  9.9 1.6 %collective-permute-start = (bf16[192,768]{1,0:T(8,128)(2,1)}, bf16[192,768]{1,0:T(8,128)(2,1)S(1)}, u32[]{:S(2)}, u32[]{:S(2)}) collective-permute-start(bf16[192,768]{1,0:T(8,128)(2,1)} %bitcast.13), channel_id=1, source_target_pairs={{0,2},{1,3},{2,0},{3,1},{4,6},{5,7},{6,4},{7,5},{8,10},{9,11},{10,... | collective-permute-start | bytes 884744 | tf_op jit(solution)/shard_map/ppermute | solution.py:27
  11.5 1.5 %collective-permute-start.1 = (bf16[96,512]{1,0:T(8,128)(2,1)S(1)}, bf16[96,512]{1,0:T(8,128)(2,1)S(1)}, u32[]{:S(2)}, u32[]{:S(2)}) collective-permute-start(bf16[96,512]{1,0:T(8,128)(2,1)S(1)} %get-tuple-element.24), channel_id=1, source_target_pairs={{0,4},{4,0},{8,12},{12,8},{16,20},{20,16},{24,28},{28,24},{1,5},{5... | collective-permute-start | bytes 294920 | tf_op jit(solution)/shard_map/ppermute | solution.py:27
  13.0 0.6 %collective-permute-start.3 = (bf16[32,512]{1,0:T(8,128)(2,1)S(1)}, bf16[32,512]{1,0:T(8,128)(2,1)S(1)}, u32[]{:S(2)}, u32[]{:S(2)}) collective-permute-start(bf16[32,512]{1,0:T(8,128)(2,1)S(1)} %get-tuple-element.26), channel_id=1, source_target_pairs={{0,12},{4,8},{8,4},{12,0},{16,28},{20,24},{24,20},{28,16},{1,13},{... | collective-permute-start | bytes 98312 | tf_op jit(solution)/shard_map/ppermute | solution.py:27
  13.5 1.5 %collective-permute-start.2 = (bf16[32,512]{1,0:T(8,128)(2,1)S(1)}, bf16[32,512]{1,0:T(8,128)(2,1)S(1)}, u32[]{:S(2)}, u32[]{:S(2)}) collective-permute-start(bf16[32,512]{1,0:T(8,128)(2,1)S(1)} %get-tuple-element.26), channel_id=1, source_target_pairs={{0,8},{4,12},{8,0},{12,4},{16,24},{20,28},{24,16},{28,20},{1,9},{5... | collective-permute-start | bytes 98312 | tf_op jit(solution)/shard_map/ppermute | solution.py:27
  15.0 0.6 %all-to-all-done.rows_ref = bf16[8,16,1024]{2,1,0:T(8,128)(2,1)S(1)} async-done(((bf16[8,16,1024]{2,1,0:T(8,128)(2,1)}), bf16[8,16,1024]{2,1,0:T(8,128)(2,1)S(1)}, u32[]{:S(2)}, u32[]{:S(2)}) %all-to-all-start) | async-done | bytes 262176 | tf_op jit(solution)/shard_map/all_to_all | solution.py:345
  15.6 1.0 %shard_map.129 = bf16[8,16,1024]{2,1,0:T(8,128)(2,1)} custom-call(s32[64]{0:T(128)S(4)} %get-tuple-element.23.order_ref, bf16[8,16,1024]{2,1,0:T(8,128)(2,1)S(1)} %all-to-all-done.rows_ref), custom_call_target="tpu_custom_call" | custom-call | tf_op jit(solution)/shard_map/pallas_call | solution.py:60
  16.6 4.7 %all-to-all-start.1 = ((bf16[8,16,1024]{2,1,0:T(8,128)(2,1)}), bf16[8,16,1024]{2,1,0:T(8,128)(2,1)S(1)}, u32[]{:S(2)}, u32[]{:S(2)}) async-start(bf16[8,16,1024]{2,1,0:T(8,128)(2,1)} %shard_map.129), calls=%async_computation.1 | async-start | bytes 524288 | tf_op jit(solution)/shard_map/all_to_all | solution.py:345
  21.2 0.0 collective-permute-done.3
  21.3 0.0 collective-permute-done.1
  21.3 0.1 collective-permute-start.4
  21.4 0.5 %collective-permute-start.5 = (bf16[192,768]{1,0:T(8,128)(2,1)S(1)}, bf16[192,768]{1,0:T(8,128)(2,1)S(1)}, u32[]{:S(2)}, u32[]{:S(2)}) collective-permute-start(bf16[192,768]{1,0:T(8,128)(2,1)S(1)} %collective-permute-done.inverse_far_ref), channel_id=1, source_target_pairs={{0,1},{1,0},{2,3},{3,2},{4,5},{5,4},{6,7},{7,6},{8,9},{9,8},{10,11... | collective-permute-start | bytes 884744 | tf_op jit(solution)/shard_map/ppermute | solution.py:27
  21.9 0.1 collective-permute-start.6
  22.0 1.8 %collective-permute-done.6.upper_near_ref = bf16[256,512]{1,0:T(8,128)(2,1)S(1)} collective-permute-done((bf16[256,512]{1,0:T(8,128)(2,1)S(1)}, bf16[256,512]{1,0:T(8,128)(2,1)S(1)}, u32[]{:S(2)}, u32[]{:S(2)}) %collective-permute-start.6) | collective-permute-done | bytes 262176 | tf_op jit(solution)/shard_map/ppermute | solution.py:27
  23.8 1.5 %shard_map.130 = (bf16[768,768]{1,0:T(8,128)(2,1)S(1)}, bf16[1024,256]{1,0:T(8,128)(2,1)S(1)}, bf16[2304,256]{1,0:T(8,128)(2,1)S(1)}) custom-call(bf16[192,768]{1,0:T(8,128)(2,1)} %bitcast.14, bf16[192,768]{1,0:T(8,128)(2,1)S(1)} %collective-permute-done.inverse_far_ref, bf16[192,768]{1,0:T(8,128)(2,1)S(1)} %collective-permute-done.4.inverse_near_ref, ...), custom_call_target="tpu_custom_call" | custom-call | flops 1000000000 | bytes 6000000 | tf_op jit(solution)/shard_map/pallas_call | solution.py:211
  25.3 0.6 %all-to-all-done.1 = bf16[8,16,1024]{2,1,0:T(8,128)(2,1)S(1)} async-done(((bf16[8,16,1024]{2,1,0:T(8,128)(2,1)}), bf16[8,16,1024]{2,1,0:T(8,128)(2,1)S(1)}, u32[]{:S(2)}, u32[]{:S(2)}) %all-to-all-start.1) | async-done | bytes 262176 | tf_op jit(solution)/shard_map/all_to_all | solution.py:345
  25.9 2.0 %shard_map.131 = (bf16[128,768]{1,0:T(8,128)(2,1)}, bf16[8,128,128]{2,1,0:T(8,128)(2,1)}, bf16[128,128]{1,0:T(8,128)(2,1)S(1)}, f32[128,128]{1,0:T(8,128)S(1)}) custom-call(bf16[128,1024]{1,0:T(8,128)(2,1)S(1)} %bitcast.9, bf16[768,768]{1,0:T(8,128)(2,1)S(1)} %get-tuple-element.30.inverse_ref, bf16[1024,256]{1,0:T(8,128)(2,1)S(1)} %get-tuple-element.31.table_ref, ...), custom_call_target="tpu_custom_call" | custom-call | tf_op jit(solution)/shard_map/pallas_call | solution.py:284
  27.9 5.8 %all-to-all-start.2 = ((bf16[8,128,128]{2,1,0:T(8,128)(2,1)}), bf16[8,128,128]{2,1,0:T(8,128)(2,1)S(1)}, u32[]{:S(2)}, u32[]{:S(2)}) async-start(bf16[8,128,128]{2,1,0:T(8,128)(2,1)} %get-tuple-element.34), calls=%async_computation.2 | async-start | bytes 524288 | tf_op jit(solution)/shard_map/all_to_all | solution.py:345
  33.7 1.5 %collective-permute-start.7 = (bf16[128,128]{1,0:T(8,128)(2,1)S(1)}, bf16[128,128]{1,0:T(8,128)(2,1)S(1)}, u32[]{:S(2)}, u32[]{:S(2)}) collective-permute-start(bf16[128,128]{1,0:T(8,128)(2,1)S(1)} %get-tuple-element.35), channel_id=1, source_target_pairs={{0,4},{4,0},{8,12},{12,8},{16,20},{20,16},{24,28},{28,24},{1,5},{5... | collective-permute-start | bytes 98312 | tf_op jit(solution)/shard_map/ppermute | solution.py:27
  35.2 3.3 %collective-permute-done.7.received_one_ref = bf16[128,128]{1,0:T(8,128)(2,1)S(1)} collective-permute-done((bf16[128,128]{1,0:T(8,128)(2,1)S(1)}, bf16[128,128]{1,0:T(8,128)(2,1)S(1)}, u32[]{:S(2)}, u32[]{:S(2)}) %collective-permute-start.7) | collective-permute-done | bytes 32800 | tf_op jit(solution)/shard_map/ppermute | solution.py:27
  38.4 0.7 %all-to-all-done.2.received_ref = bf16[8,128,128]{2,1,0:T(8,128)(2,1)S(1)} async-done(((bf16[8,128,128]{2,1,0:T(8,128)(2,1)}), bf16[8,128,128]{2,1,0:T(8,128)(2,1)S(1)}, u32[]{:S(2)}, u32[]{:S(2)}) %all-to-all-start.2) | async-done | bytes 262176 | tf_op jit(solution)/shard_map/all_to_all | solution.py:345
  39.2 0.7 %shard_map.132 = (f32[128,128]{1,0:T(8,128)}, f32[64,128]{1,0:T(8,128)}, f32[32,128]{1,0:T(8,128)}, f32[32,128]{1,0:T(8,128)}) custom-call(bf16[8,128,128]{2,1,0:T(8,128)(2,1)S(1)} %all-to-all-done.2.received_ref, bf16[128,128]{1,0:T(8,128)(2,1)S(1)} %collective-permute-done.7.received_one_ref, f32[128,128]{1,0:T(8,128)S(1)} %get-tuple-element.36.kept_one_ref), custom_call_target="tpu_custom_call" | custom-call | tf_op jit(solution)/shard_map/pallas_call | solution.py:318
  (6 shorter events, 0.0 us)
Async XLA Ops:
  0.6 20.7 %copy-start = (bf16[1,192,768]{2,1,0:T(8,128)(2,1)S(1)}, bf16[1,192,768]{2,1,0:T(8,128)(2,1)}, u32[]{:S(2)}) copy-start(bf16[1,192,768]{2,1,0:T(8,128)(2,1)} %param.13) | copy-start | bytes 884740
  0.6 14.9 %all-to-all-start = ((bf16[8,16,1024]{2,1,0:T(8,128)(2,1)}), bf16[8,16,1024]{2,1,0:T(8,128)(2,1)S(1)}, u32[]{:S(2)}, u32[]{:S(2)}) async-start(bf16[8,16,1024]{2,1,0:T(8,128)(2,1)} %bitcast.10), calls=%async_computation | async-start | bytes 524288 | tf_op jit(solution)/shard_map/all_to_all | solution.py:345
  9.9 11.3 %collective-permute-start = (bf16[192,768]{1,0:T(8,128)(2,1)}, bf16[192,768]{1,0:T(8,128)(2,1)S(1)}, u32[]{:S(2)}, u32[]{:S(2)}) collective-permute-start(bf16[192,768]{1,0:T(8,128)(2,1)} %bitcast.13), channel_id=1, source_target_pairs={{0,2},{1,3},{2,0},{3,1},{4,6},{5,7},{6,4},{7,5},{8,10},{9,11},{10,... | collective-permute-start | bytes 884744 | tf_op jit(solution)/shard_map/ppermute | solution.py:27
  11.5 9.8 %collective-permute-start.1 = (bf16[96,512]{1,0:T(8,128)(2,1)S(1)}, bf16[96,512]{1,0:T(8,128)(2,1)S(1)}, u32[]{:S(2)}, u32[]{:S(2)}) collective-permute-start(bf16[96,512]{1,0:T(8,128)(2,1)S(1)} %get-tuple-element.24), channel_id=1, source_target_pairs={{0,4},{4,0},{8,12},{12,8},{16,20},{20,16},{24,28},{28,24},{1,5},{5... | collective-permute-start | bytes 294920 | tf_op jit(solution)/shard_map/ppermute | solution.py:27
  13.0 8.3 %collective-permute-start.3 = (bf16[32,512]{1,0:T(8,128)(2,1)S(1)}, bf16[32,512]{1,0:T(8,128)(2,1)S(1)}, u32[]{:S(2)}, u32[]{:S(2)}) collective-permute-start(bf16[32,512]{1,0:T(8,128)(2,1)S(1)} %get-tuple-element.26), channel_id=1, source_target_pairs={{0,12},{4,8},{8,4},{12,0},{16,28},{20,24},{24,20},{28,16},{1,13},{... | collective-permute-start | bytes 98312 | tf_op jit(solution)/shard_map/ppermute | solution.py:27
  13.5 7.7 %collective-permute-start.2 = (bf16[32,512]{1,0:T(8,128)(2,1)S(1)}, bf16[32,512]{1,0:T(8,128)(2,1)S(1)}, u32[]{:S(2)}, u32[]{:S(2)}) collective-permute-start(bf16[32,512]{1,0:T(8,128)(2,1)S(1)} %get-tuple-element.26), channel_id=1, source_target_pairs={{0,8},{4,12},{8,0},{12,4},{16,24},{20,28},{24,16},{28,20},{1,9},{5... | collective-permute-start | bytes 98312 | tf_op jit(solution)/shard_map/ppermute | solution.py:27
  16.6 9.3 %all-to-all-start.1 = ((bf16[8,16,1024]{2,1,0:T(8,128)(2,1)}), bf16[8,16,1024]{2,1,0:T(8,128)(2,1)S(1)}, u32[]{:S(2)}, u32[]{:S(2)}) async-start(bf16[8,16,1024]{2,1,0:T(8,128)(2,1)} %shard_map.129), calls=%async_computation.1 | async-start | bytes 524288 | tf_op jit(solution)/shard_map/all_to_all | solution.py:345
  21.3 2.4 %collective-permute-start.4 = (bf16[192,768]{1,0:T(8,128)(2,1)S(1)}, bf16[192,768]{1,0:T(8,128)(2,1)S(1)}, u32[]{:S(2)}, u32[]{:S(2)}) collective-permute-start(bf16[192,768]{1,0:T(8,128)(2,1)S(1)} %bitcast.15), channel_id=1, source_target_pairs={{0,1},{1,0},{2,3},{3,2},{4,5},{5,4},{6,7},{7,6},{8,9},{9,8},{10,11... | collective-permute-start | bytes 884744 | tf_op jit(solution)/shard_map/ppermute | solution.py:27
  21.4 2.4 %collective-permute-start.5 = (bf16[192,768]{1,0:T(8,128)(2,1)S(1)}, bf16[192,768]{1,0:T(8,128)(2,1)S(1)}, u32[]{:S(2)}, u32[]{:S(2)}) collective-permute-start(bf16[192,768]{1,0:T(8,128)(2,1)S(1)} %collective-permute-done.inverse_far_ref), channel_id=1, source_target_pairs={{0,1},{1,0},{2,3},{3,2},{4,5},{5,4},{6,7},{7,6},{8,9},{9,8},{10,11... | collective-permute-start | bytes 884744 | tf_op jit(solution)/shard_map/ppermute | solution.py:27
  21.9 1.9 %collective-permute-start.6 = (bf16[256,512]{1,0:T(8,128)(2,1)S(1)}, bf16[256,512]{1,0:T(8,128)(2,1)S(1)}, u32[]{:S(2)}, u32[]{:S(2)}) collective-permute-start(bf16[256,512]{1,0:T(8,128)(2,1)S(1)} %pad_maximum_fusion.upper_ref), channel_id=1, source_target_pairs={{0,1},{1,0},{2,3},{3,2},{4,5},{5,4},{6,7},{7,6},{8,9},{9,8},{10,11... | collective-permute-start | bytes 786440 | tf_op jit(solution)/shard_map/ppermute | solution.py:27
  27.9 11.2 %all-to-all-start.2 = ((bf16[8,128,128]{2,1,0:T(8,128)(2,1)}), bf16[8,128,128]{2,1,0:T(8,128)(2,1)S(1)}, u32[]{:S(2)}, u32[]{:S(2)}) async-start(bf16[8,128,128]{2,1,0:T(8,128)(2,1)} %get-tuple-element.34), calls=%async_computation.2 | async-start | bytes 524288 | tf_op jit(solution)/shard_map/all_to_all | solution.py:345
  33.7 4.8 %collective-permute-start.7 = (bf16[128,128]{1,0:T(8,128)(2,1)S(1)}, bf16[128,128]{1,0:T(8,128)(2,1)S(1)}, u32[]{:S(2)}, u32[]{:S(2)}) collective-permute-start(bf16[128,128]{1,0:T(8,128)(2,1)S(1)} %get-tuple-element.35), channel_id=1, source_target_pairs={{0,4},{4,0},{8,12},{12,8},{16,20},{20,16},{24,28},{28,24},{1,5},{5... | collective-permute-start | bytes 98312 | tf_op jit(solution)/shard_map/ppermute | solution.py:27

commit v5 on v4

--- a/solution.py
+++ b/solution.py
@@ -7,8 +7,9 @@
 
 BLOCK = 128
 NODE_LEAVES = 8
-MEMBERS = (4, 5, 1, 0, 7, 3, 6, 2)
-LAST_MEMBERS = (4, 5, 1, 0, 7, 3, 6, 2)
+FIRST_MEMBERS = (4, 5, 6, 7, 0, 1, 2, 3)
+MEMBERS = (4, 7, 3, 1, 0, 2, 6, 5)
+LAST_MEMBERS = (5, 4, 1, 0, 7, 6, 3, 2)
 INSIDE = pl.BlockSpec(memory_space=pltpu.VMEM)
 SCALARS = pl.BlockSpec(memory_space=pltpu.SMEM)
 OUTSIDE = pl.BlockSpec(memory_space=pl.ANY)
@@ -84,9 +85,9 @@
     for copy in copies:
         copy.start()
     copies[0].wait()
-    leaves = len(MEMBERS)
+    leaves = len(FIRST_MEMBERS)
     per_leaf = places_out.shape[0] // leaves
-    slots = sum(slot << 3 * leaf for slot, leaf in enumerate(MEMBERS))
+    slots = sum(slot << 3 * leaf for slot, leaf in enumerate(FIRST_MEMBERS))
 
     def place(t, carry):
         source = places_out[t]
@@ -132,6 +133,7 @@
     table_out,
     narrow_out,
     one,
+    coupling,
     two_rows,
     three_rows,
     arrivals,
@@ -147,7 +149,7 @@
         pltpu.make_async_copy(inverse_ref, inverse_out.at[pl.ds(start, span), :], arrivals.at[1])
     )
     at = 0
-    for index, piece in enumerate((basis_ref, inner_ref, coupling_ref)):
+    for index, piece in enumerate((basis_ref, inner_ref)):
         height = piece.shape[0]
         copies.append(
             pltpu.make_async_copy(
@@ -155,6 +157,7 @@
             )
         )
         at += height
+    copies.append(pltpu.make_async_copy(coupling_ref, coupling, arrivals.at[4]))
     for copy in copies:
         copy.start()
 
@@ -200,6 +203,9 @@
         table_out[pl.ds(at + width, width), :] = two
     for copy in copies[1:]:
         copy.wait()
+    height = coupling.shape[0]
+    at = narrow_out.shape[0] - rank - height
+    narrow_out[pl.ds(at, height), :] = product(inverse_out[...], coupling[...]).astype(bf16)
 
 
 def weights_stage(inverse, inverse_pieces, upper, upper_near, one, basis, inner, coupling):
@@ -213,7 +219,13 @@
         out_shape=[pltpu.VMEM(shape, bf16) for shape in shapes],
         in_specs=[OUTSIDE] + [INSIDE] * 5 + [OUTSIDE] * 4,
         out_specs=[INSIDE] * 3,
-        scratch_shapes=[pltpu.VMEM((rank, 2 * rank), bf16)] * 3 + [pltpu.SemaphoreType.DMA((5,))],
+        scratch_shapes=[
+            pltpu.VMEM((rank, 2 * rank), bf16),
+            pltpu.VMEM(coupling.shape, bf16),
+            pltpu.VMEM((rank, 2 * rank), bf16),
+            pltpu.VMEM((rank, 2 * rank), bf16),
+            pltpu.SemaphoreType.DMA((5,)),
+        ],
         cost_estimate=pl.CostEstimate(
             flops=10**9, bytes_accessed=6 * 10**6, transcendentals=0
         ),
@@ -232,40 +244,47 @@
 
 def leaf_kernel(
     placed_ref,
-    inverse_ref,
     table_ref,
     narrow_ref,
-    eliminated_ref,
+    leading_ref,
     terms_ref,
     sent_one_ref,
     kept_one_ref,
-    eliminated_staged,
     terms_staged,
     leaving,
 ):
     bf16 = jnp.bfloat16
-    row_count = placed_ref.shape[1]
-    split_at = inverse_ref.shape[0]
+    row_count = placed_ref.shape[2]
     rank = narrow_ref.shape[1]
-    placed = placed_ref[...]
+    split_at = row_count - rank
+    slots = range(placed_ref.shape[0])
+    if len(slots) == NODE_LEAVES:
+        slots = [MEMBERS.index(leaf) for leaf in FIRST_MEMBERS]
+    placed = jnp.concatenate([placed_ref[slot] for slot in slots], axis=0)
     basis = narrow_ref[:row_count]
     inner = narrow_ref[pl.ds(row_count, rank)]
-    coupling = narrow_ref[pl.ds(row_count + rank, split_at)]
+    through = narrow_ref[pl.ds(row_count + rank, split_at)]
     one_eliminated = narrow_ref[pl.ds(row_count + rank + split_at, rank)]
     projected = product(placed, basis).astype(bf16)
     middle = product(projected, inner).astype(bf16)
     correction = product(middle, basis, ((1,), (1,)))
     reflected = (placed.astype(jnp.float32) - correction).astype(bf16)
-    eliminated = product(reflected[:, :split_at], inverse_ref[...]).astype(bf16)
-    eliminated_staged[...] = eliminated
-    copies = [pltpu.make_async_copy(eliminated_staged, eliminated_ref, leaving.at[0])]
-    copies[0].start()
-    coupled = product(eliminated, coupling)
+    leading = reflected[:, :split_at]
+    leading_ref[...] = leading
+    coupled = product(leading, through)
     skeleton = (reflected[:, split_at:].astype(jnp.float32) - coupled).astype(bf16)
-    terms = product(table_ref[...], skeleton, ((1,), (1,))).astype(bf16)
-    terms_staged[...] = terms.reshape(terms_staged.shape)
-    copies.append(pltpu.make_async_copy(terms_staged, terms_ref, leaving.at[1]))
-    copies[1].start()
+    copies = []
+    share = NODE_LEAVES // leaving.shape[0]
+    height = terms_staged.shape[1]
+    for part in range(leaving.shape[0]):
+        table = table_ref[pl.ds(part * share * height, share * height), :]
+        terms = product(table, skeleton, ((1,), (1,))).astype(bf16)
+        some = pl.ds(part * share, share)
+        terms_staged[some] = terms.reshape((share,) + terms_staged.shape[1:])
+        copies.append(
+            pltpu.make_async_copy(terms_staged.at[some], terms_ref.at[some], leaving.at[part])
+        )
+        copies[-1].start()
 
     one_terms = product(skeleton, one_eliminated)
     half = rank // 2
@@ -276,28 +295,44 @@
         copy.wait()
 
 
-def leaf_stage(placed, inverse, table, narrow):
-    columns = placed.shape[0]
+def leaf_stage(placed, table, narrow):
+    columns = placed.shape[0] * placed.shape[1]
     rank = narrow.shape[1]
     half = rank // 2
     bf16 = jnp.bfloat16
     return pl.pallas_call(
         leaf_kernel,
         out_shape=(
-            pltpu.HBM((columns, inverse.shape[1]), bf16),
+            pltpu.VMEM((columns, placed.shape[2] - rank), bf16),
             pltpu.HBM((NODE_LEAVES, half, columns), bf16),
             pltpu.VMEM((columns, half), bf16),
             pltpu.VMEM((columns, half), jnp.float32),
         ),
-        in_specs=[INSIDE] * 4,
-        out_specs=(OUTSIDE,) * 2 + (INSIDE,) * 2,
+        in_specs=[INSIDE] * 3,
+        out_specs=(INSIDE, OUTSIDE, INSIDE, INSIDE),
         scratch_shapes=[
-            pltpu.VMEM((columns, inverse.shape[1]), bf16),
             pltpu.VMEM((NODE_LEAVES, half, columns), bf16),
             pltpu.SemaphoreType.DMA((2,)),
         ],
         compiler_params=pltpu.CompilerParams(vmem_limit_bytes=6 << 20),
-    )(near(placed), near(inverse), near(table), near(narrow))
+    )(near(placed), near(table), near(narrow))
+
+
+def eliminate_kernel(leading_ref, inverse_ref, eliminated_ref):
+    eliminated_ref[...] = product(leading_ref[...], inverse_ref[...]).astype(jnp.bfloat16)
+
+
+def eliminate_stage(leading, inverse):
+    return pl.pallas_call(
+        eliminate_kernel,
+        out_shape=jax.ShapeDtypeStruct(leading.shape, jnp.bfloat16),
+        in_specs=[INSIDE] * 2,
+        out_specs=INSIDE,
+        cost_estimate=pl.CostEstimate(
+            flops=10**9, bytes_accessed=6 * 10**6, transcendentals=0
+        ),
+        compiler_params=pltpu.CompilerParams(vmem_limit_bytes=6 << 20),
+    )(near(leading), near(inverse))
 
 
 def tail_kernel(
@@ -339,14 +374,14 @@
     columns, row_count = right_sides.shape
 
     one_node = leaf_count == NODE_LEAVES
-    members = [list(MEMBERS)] if one_node else None
+    first_members, members = ([list(FIRST_MEMBERS)], [list(MEMBERS)]) if one_node else (None, None)
 
     def spread(pieces, groups):
         return lax.all_to_all(
             pieces, "leaf", split_axis=0, concat_axis=0, tiled=True, axis_index_groups=groups
         )
 
-    arrived = spread(right_sides.reshape(leaf_count, columns // leaf_count, row_count), members)
+    arrived = spread(right_sides.reshape(leaf_count, columns // leaf_count, row_count), first_members)
 
     places, upper_own, three = early_stage(block_order, merge_two, merge_three)
     upper_pieces = [upper_own, exchanged(upper_own, "leaf", 1)]
@@ -376,11 +411,12 @@
         returning = reorder(arrived, places)
     else:
         returning = reorder_anywhere(arrived, block_order)
-    placed = spread(returning, members).reshape(columns, row_count)
-    eliminated, terms, sent_one, kept_one = leaf_stage(placed, inverse_whole, table, narrow)
+    placed = spread(returning, members)
+    leading, terms, sent_one, kept_one = leaf_stage(placed, table, narrow)
 
     starts = range(0, leaf_count, NODE_LEAVES)
     received = spread(terms, [[start + leaf for leaf in LAST_MEMBERS] for start in starts])
+    eliminated = eliminate_stage(leading, inverse_whole)
     level_one, level_two, level_three, top_skeleton = tail_stage(
         received, exchanged(sent_one, "leaf", 1), kept_one
     )

time: 40.3 us -> 39.3 us (0.975)
  waiting for transfers between devices: 7 us -> 4.85 us
  Pallas kernels: 6.5 us -> 7.72 us
    all_to_all x3, waiting for transfers between devices: 1.91 us -> 0.55 us  [spread(): lax.all_to_all(pieces, 'leaf', split_axis=0, concat_axis=0, tiled=True, a...]
    ppermute x8, starting transfers between devices: 7.15 us -> 6.25 us  [exchanged(): lax.ppermute(piece, axis, [(i, i ^ flip) for i in range(count) if i ^ fli...]
    all_to_all x3, starting transfers between devices: 18.4 us -> 19.3 us  [spread(): lax.all_to_all(pieces, 'leaf', split_axis=0, concat_axis=0, tiled=True, a...]
    ppermute x8, waiting for transfers between devices: 5.09 us -> 4.3 us  [exchanged(): lax.ppermute(piece, axis, [(i, i ^ flip) for i in range(count) if i ^ fli...]
    pallas_call x1 -> x2, Pallas kernels: 2.01 us -> 2.76 us  [the longest x1 1.75 us: leaf_stage(): pl.pallas_call(leaf_kernel, out_shape=(pltpu.VMEM((columns, placed.shape[...]
    pallas_call x1, Pallas kernels: 1.55 us -> 2.02 us  [weights_stage(): pl.pallas_call(weights_kernel, out_shape=[pltpu.VMEM(shape, bf16) for sha...]
  transfers between devices with their start and end apart: 11 -> 11, of which waited for: 5 -> 4; matrix products, arithmetic and copies ran while one was open for 0% -> 0% of each run, Pallas kernels for 10% -> 14%
where the time goes in v5:
time: 39.3 us; the launch traced here: 38.8 us
  starting transfers between devices  25.5 us (65%)
  Pallas kernels  7.72 us (20%)
  waiting for transfers between devices  4.85 us (12%)
  between operations  0.72 us (2%)
    all_to_all x3, starting transfers between devices, spread(): lax.all_to_all(pieces, 'leaf', split_axis=0, concat_axis=0, tiled=True, a...  19.3 us
    ppermute x8, starting transfers between devices, exchanged(): lax.ppermute(piece, axis, [(i, i ^ flip) for i in range(count) if i ^ fli...  6.25 us
    ppermute x8, waiting for transfers between devices, exchanged(): lax.ppermute(piece, axis, [(i, i ^ flip) for i in range(count) if i ^ fli...  4.3 us
    pallas_call x1, Pallas kernels, weights_stage(): pl.pallas_call(weights_kernel, out_shape=[pltpu.VMEM(shape, bf16) for sha...  2.02 us
    pallas_call x1, Pallas kernels, leaf_stage(): pl.pallas_call(leaf_kernel, out_shape=(pltpu.VMEM((columns, placed.shape[...  1.75 us
    pallas_call x1, Pallas kernels, early_stage(): pl.pallas_call(early_kernel, out_shape=[pltpu.SMEM(block_order.shape, blo...  1.31 us
    pallas_call x1, Pallas kernels, eliminate_stage(): pl.pallas_call(eliminate_kernel, out_shape=jax.ShapeDtypeStruct(leading.s...  1.01 us
    pallas_call x1, Pallas kernels, reorder(): pl.pallas_call(reorder_kernel, out_shape=pltpu.HBM(rows.shape, rows.dtype...  0.96 us
  transfers between devices with their start and end apart: 11, of which 4 were waited for; matrix products, arithmetic and copies ran while one was open for 0% of the time, Pallas kernels for 14%

profile of v5, /device:TPU:0, one launch (start us, length us, event | category | flops | bytes accessed | tf_op | source)
XLA Modules:
  0.0 38.8 jit_solution(13194270603087713427)
XLA Ops:
  0.6 0.0 copy-start
  0.6 8.0 %all-to-all-start = ((bf16[8,16,1024]{2,1,0:T(8,128)(2,1)}), bf16[8,16,1024]{2,1,0:T(8,128)(2,1)S(1)}, u32[]{:S(2)}, u32[]{:S(2)}) async-start(bf16[8,16,1024]{2,1,0:T(8,128)(2,1)} %bitcast.8), calls=%async_computation | async-start | bytes 524288 | tf_op jit(solution)/shard_map/all_to_all | solution.py:380
  8.6 1.3 %shard_map.128 = (s32[64]{0:T(128)S(4)}, bf16[96,512]{1,0:T(8,128)(2,1)S(1)}, bf16[32,512]{1,0:T(8,128)(2,1)S(1)}) custom-call(s32[64]{0:T(128)} %order_ref.1, bf16[128,512]{1,0:T(8,128)(2,1)} %two_ref.1, bf16[64,512]{1,0:T(8,128)(2,1)} %three_ref.1), custom_call_target="tpu_custom_call" | custom-call | tf_op jit(solution)/shard_map/pallas_call | solution.py:107
  9.9 1.6 %collective-permute-start = (bf16[192,768]{1,0:T(8,128)(2,1)}, bf16[192,768]{1,0:T(8,128)(2,1)S(1)}, u32[]{:S(2)}, u32[]{:S(2)}) collective-permute-start(bf16[192,768]{1,0:T(8,128)(2,1)} %bitcast.11), channel_id=1, source_target_pairs={{0,2},{1,3},{2,0},{3,1},{4,6},{5,7},{6,4},{7,5},{8,10},{9,11},{10,... | collective-permute-start | bytes 884744 | tf_op jit(solution)/shard_map/ppermute | solution.py:28
  11.5 1.5 %collective-permute-start.1 = (bf16[96,512]{1,0:T(8,128)(2,1)S(1)}, bf16[96,512]{1,0:T(8,128)(2,1)S(1)}, u32[]{:S(2)}, u32[]{:S(2)}) collective-permute-start(bf16[96,512]{1,0:T(8,128)(2,1)S(1)} %get-tuple-element.24), channel_id=1, source_target_pairs={{0,4},{4,0},{8,12},{12,8},{16,20},{20,16},{24,28},{28,24},{1,5},{5... | collective-permute-start | bytes 294920 | tf_op jit(solution)/shard_map/ppermute | solution.py:28
  13.0 0.6 %collective-permute-start.3 = (bf16[32,512]{1,0:T(8,128)(2,1)S(1)}, bf16[32,512]{1,0:T(8,128)(2,1)S(1)}, u32[]{:S(2)}, u32[]{:S(2)}) collective-permute-start(bf16[32,512]{1,0:T(8,128)(2,1)S(1)} %get-tuple-element.26), channel_id=1, source_target_pairs={{0,12},{4,8},{8,4},{12,0},{16,28},{20,24},{24,20},{28,16},{1,13},{... | collective-permute-start | bytes 98312 | tf_op jit(solution)/shard_map/ppermute | solution.py:28
  13.5 1.5 %collective-permute-start.2 = (bf16[32,512]{1,0:T(8,128)(2,1)S(1)}, bf16[32,512]{1,0:T(8,128)(2,1)S(1)}, u32[]{:S(2)}, u32[]{:S(2)}) collective-permute-start(bf16[32,512]{1,0:T(8,128)(2,1)S(1)} %get-tuple-element.26), channel_id=1, source_target_pairs={{0,8},{4,12},{8,0},{12,4},{16,24},{20,28},{24,16},{28,20},{1,9},{5... | collective-permute-start | bytes 98312 | tf_op jit(solution)/shard_map/ppermute | solution.py:28
  15.0 0.2 all-to-all-done.rows_ref
  15.2 1.0 %shard_map.129 = bf16[8,16,1024]{2,1,0:T(8,128)(2,1)} custom-call(s32[64]{0:T(128)S(4)} %get-tuple-element.23.order_ref, bf16[8,16,1024]{2,1,0:T(8,128)(2,1)S(1)} %all-to-all-done.rows_ref), custom_call_target="tpu_custom_call" | custom-call | tf_op jit(solution)/shard_map/pallas_call | solution.py:61
  16.2 5.2 %all-to-all-start.1 = ((bf16[8,16,1024]{2,1,0:T(8,128)(2,1)}), bf16[8,16,1024]{2,1,0:T(8,128)(2,1)S(1)}, u32[]{:S(2)}, u32[]{:S(2)}) async-start(bf16[8,16,1024]{2,1,0:T(8,128)(2,1)} %shard_map.129), calls=%async_computation.1 | async-start | bytes 524288 | tf_op jit(solution)/shard_map/all_to_all | solution.py:380
  21.3 0.0 collective-permute-done.1
  21.4 0.0 collective-permute-done.inverse_far_ref
  21.4 0.1 collective-permute-start.4
  21.5 0.5 %collective-permute-start.5 = (bf16[192,768]{1,0:T(8,128)(2,1)S(1)}, bf16[192,768]{1,0:T(8,128)(2,1)S(1)}, u32[]{:S(2)}, u32[]{:S(2)}) collective-permute-start(bf16[192,768]{1,0:T(8,128)(2,1)S(1)} %collective-permute-done.inverse_far_ref), channel_id=1, source_target_pairs={{0,1},{1,0},{2,3},{3,2},{4,5},{5,4},{6,7},{7,6},{8,9},{9,8},{10,11... | collective-permute-start | bytes 884744 | tf_op jit(solution)/shard_map/ppermute | solution.py:28
  22.0 0.1 collective-permute-start.6
  22.1 1.8 %collective-permute-done.6.upper_near_ref = bf16[256,512]{1,0:T(8,128)(2,1)S(1)} collective-permute-done((bf16[256,512]{1,0:T(8,128)(2,1)S(1)}, bf16[256,512]{1,0:T(8,128)(2,1)S(1)}, u32[]{:S(2)}, u32[]{:S(2)}) %collective-permute-start.6) | collective-permute-done | bytes 262176 | tf_op jit(solution)/shard_map/ppermute | solution.py:28
  23.9 2.0 %shard_map.130 = (bf16[768,768]{1,0:T(8,128)(2,1)S(1)}, bf16[1024,256]{1,0:T(8,128)(2,1)S(1)}, bf16[2304,256]{1,0:T(8,128)(2,1)S(1)}) custom-call(bf16[192,768]{1,0:T(8,128)(2,1)} %bitcast.12, bf16[192,768]{1,0:T(8,128)(2,1)S(1)} %collective-permute-done.inverse_far_ref, bf16[192,768]{1,0:T(8,128)(2,1)S(1)} %collective-permute-done.4.inverse_near_ref, ...), custom_call_target="tpu_custom_call" | custom-call | flops 1000000000 | bytes 6000000 | tf_op jit(solution)/shard_map/pallas_call | solution.py:217
  25.9 0.3 all-to-all-done.1.placed_ref
  26.2 1.8 %shard_map.131 = (bf16[128,768]{1,0:T(8,128)(2,1)S(1)}, bf16[8,128,128]{2,1,0:T(8,128)(2,1)}, bf16[128,128]{1,0:T(8,128)(2,1)S(1)}, f32[128,128]{1,0:T(8,128)S(1)}) custom-call(bf16[8,16,1024]{2,1,0:T(8,128)(2,1)S(1)} %all-to-all-done.1.placed_ref, bf16[1024,256]{1,0:T(8,128)(2,1)S(1)} %get-tuple-element.30.table_ref, ...), custom_call_target="tpu_custom_call" | custom-call | tf_op jit(solution)/shard_map/pallas_call | solution.py:303
  28.0 6.1 %all-to-all-start.2 = ((bf16[8,128,128]{2,1,0:T(8,128)(2,1)}), bf16[8,128,128]{2,1,0:T(8,128)(2,1)S(1)}, u32[]{:S(2)}, u32[]{:S(2)}) async-start(bf16[8,128,128]{2,1,0:T(8,128)(2,1)} %get-tuple-element.34), calls=%async_computation.2 | async-start | bytes 524288 | tf_op jit(solution)/shard_map/all_to_all | solution.py:380
  34.1 0.6 %collective-permute-start.7 = (bf16[128,128]{1,0:T(8,128)(2,1)S(1)}, bf16[128,128]{1,0:T(8,128)(2,1)S(1)}, u32[]{:S(2)}, u32[]{:S(2)}) collective-permute-start(bf16[128,128]{1,0:T(8,128)(2,1)S(1)} %get-tuple-element.35), channel_id=1, source_target_pairs={{0,4},{4,0},{8,12},{12,8},{16,20},{20,16},{24,28},{28,24},{1,5},{5... | collective-permute-start | bytes 98312 | tf_op jit(solution)/shard_map/ppermute | solution.py:28
  34.7 1.0 %shard_map.132 = bf16[128,768]{1,0:T(8,128)(2,1)} custom-call(bf16[128,768]{1,0:T(8,128)(2,1)S(1)} %get-tuple-element.32.leading_ref, bf16[768,768]{1,0:T(8,128)(2,1)S(1)} %get-tuple-element.33.inverse_ref), custom_call_target="tpu_custom_call" | custom-call | flops 1000000000 | bytes 6000000 | tf_op jit(solution)/shard_map/pallas_call | solution.py:326
  35.7 2.5 %collective-permute-done.7.received_one_ref = bf16[128,128]{1,0:T(8,128)(2,1)S(1)} collective-permute-done((bf16[128,128]{1,0:T(8,128)(2,1)S(1)}, bf16[128,128]{1,0:T(8,128)(2,1)S(1)}, u32[]{:S(2)}, u32[]{:S(2)}) %collective-permute-start.7) | collective-permute-done | bytes 32800 | tf_op jit(solution)/shard_map/ppermute | solution.py:28
  38.2 0.7 %shard_map.133 = (f32[128,128]{1,0:T(8,128)}, f32[64,128]{1,0:T(8,128)}, f32[32,128]{1,0:T(8,128)}, f32[32,128]{1,0:T(8,128)}) custom-call(bf16[8,128,128]{2,1,0:T(8,128)(2,1)S(1)} %all-to-all-done.2.received_ref, bf16[128,128]{1,0:T(8,128)(2,1)S(1)} %collective-permute-done.7.received_one_ref, f32[128,128]{1,0:T(8,128)S(1)} %get-tuple-element.36.kept_one_ref), custom_call_target="tpu_custom_call" | custom-call | tf_op jit(solution)/shard_map/pallas_call | solution.py:353
  (7 shorter events, 0.0 us)
Async XLA Ops:
  0.6 20.8 %copy-start = (bf16[1,192,768]{2,1,0:T(8,128)(2,1)S(1)}, bf16[1,192,768]{2,1,0:T(8,128)(2,1)}, u32[]{:S(2)}) copy-start(bf16[1,192,768]{2,1,0:T(8,128)(2,1)} %param.13) | copy-start | bytes 884740
  0.6 14.6 %all-to-all-start = ((bf16[8,16,1024]{2,1,0:T(8,128)(2,1)}), bf16[8,16,1024]{2,1,0:T(8,128)(2,1)S(1)}, u32[]{:S(2)}, u32[]{:S(2)}) async-start(bf16[8,16,1024]{2,1,0:T(8,128)(2,1)} %bitcast.8), calls=%async_computation | async-start | bytes 524288 | tf_op jit(solution)/shard_map/all_to_all | solution.py:380
  9.9 11.4 %collective-permute-start = (bf16[192,768]{1,0:T(8,128)(2,1)}, bf16[192,768]{1,0:T(8,128)(2,1)S(1)}, u32[]{:S(2)}, u32[]{:S(2)}) collective-permute-start(bf16[192,768]{1,0:T(8,128)(2,1)} %bitcast.11), channel_id=1, source_target_pairs={{0,2},{1,3},{2,0},{3,1},{4,6},{5,7},{6,4},{7,5},{8,10},{9,11},{10,... | collective-permute-start | bytes 884744 | tf_op jit(solution)/shard_map/ppermute | solution.py:28
  11.5 9.8 %collective-permute-start.1 = (bf16[96,512]{1,0:T(8,128)(2,1)S(1)}, bf16[96,512]{1,0:T(8,128)(2,1)S(1)}, u32[]{:S(2)}, u32[]{:S(2)}) collective-permute-start(bf16[96,512]{1,0:T(8,128)(2,1)S(1)} %get-tuple-element.24), channel_id=1, source_target_pairs={{0,4},{4,0},{8,12},{12,8},{16,20},{20,16},{24,28},{28,24},{1,5},{5... | collective-permute-start | bytes 294920 | tf_op jit(solution)/shard_map/ppermute | solution.py:28
  13.0 8.4 %collective-permute-start.3 = (bf16[32,512]{1,0:T(8,128)(2,1)S(1)}, bf16[32,512]{1,0:T(8,128)(2,1)S(1)}, u32[]{:S(2)}, u32[]{:S(2)}) collective-permute-start(bf16[32,512]{1,0:T(8,128)(2,1)S(1)} %get-tuple-element.26), channel_id=1, source_target_pairs={{0,12},{4,8},{8,4},{12,0},{16,28},{20,24},{24,20},{28,16},{1,13},{... | collective-permute-start | bytes 98312 | tf_op jit(solution)/shard_map/ppermute | solution.py:28
  13.5 7.8 %collective-permute-start.2 = (bf16[32,512]{1,0:T(8,128)(2,1)S(1)}, bf16[32,512]{1,0:T(8,128)(2,1)S(1)}, u32[]{:S(2)}, u32[]{:S(2)}) collective-permute-start(bf16[32,512]{1,0:T(8,128)(2,1)S(1)} %get-tuple-element.26), channel_id=1, source_target_pairs={{0,8},{4,12},{8,0},{12,4},{16,24},{20,28},{24,16},{28,20},{1,9},{5... | collective-permute-start | bytes 98312 | tf_op jit(solution)/shard_map/ppermute | solution.py:28
  16.2 10.1 %all-to-all-start.1 = ((bf16[8,16,1024]{2,1,0:T(8,128)(2,1)}), bf16[8,16,1024]{2,1,0:T(8,128)(2,1)S(1)}, u32[]{:S(2)}, u32[]{:S(2)}) async-start(bf16[8,16,1024]{2,1,0:T(8,128)(2,1)} %shard_map.129), calls=%async_computation.1 | async-start | bytes 524288 | tf_op jit(solution)/shard_map/all_to_all | solution.py:380
  21.4 2.4 %collective-permute-start.4 = (bf16[192,768]{1,0:T(8,128)(2,1)S(1)}, bf16[192,768]{1,0:T(8,128)(2,1)S(1)}, u32[]{:S(2)}, u32[]{:S(2)}) collective-permute-start(bf16[192,768]{1,0:T(8,128)(2,1)S(1)} %bitcast.13), channel_id=1, source_target_pairs={{0,1},{1,0},{2,3},{3,2},{4,5},{5,4},{6,7},{7,6},{8,9},{9,8},{10,11... | collective-permute-start | bytes 884744 | tf_op jit(solution)/shard_map/ppermute | solution.py:28
  21.5 2.4 %collective-permute-start.5 = (bf16[192,768]{1,0:T(8,128)(2,1)S(1)}, bf16[192,768]{1,0:T(8,128)(2,1)S(1)}, u32[]{:S(2)}, u32[]{:S(2)}) collective-permute-start(bf16[192,768]{1,0:T(8,128)(2,1)S(1)} %collective-permute-done.inverse_far_ref), channel_id=1, source_target_pairs={{0,1},{1,0},{2,3},{3,2},{4,5},{5,4},{6,7},{7,6},{8,9},{9,8},{10,11... | collective-permute-start | bytes 884744 | tf_op jit(solution)/shard_map/ppermute | solution.py:28
  22.0 1.9 %collective-permute-start.6 = (bf16[256,512]{1,0:T(8,128)(2,1)S(1)}, bf16[256,512]{1,0:T(8,128)(2,1)S(1)}, u32[]{:S(2)}, u32[]{:S(2)}) collective-permute-start(bf16[256,512]{1,0:T(8,128)(2,1)S(1)} %pad_maximum_fusion.upper_ref), channel_id=1, source_target_pairs={{0,1},{1,0},{2,3},{3,2},{4,5},{5,4},{6,7},{7,6},{8,9},{9,8},{10,11... | collective-permute-start | bytes 786440 | tf_op jit(solution)/shard_map/ppermute | solution.py:28
  28.0 10.2 %all-to-all-start.2 = ((bf16[8,128,128]{2,1,0:T(8,128)(2,1)}), bf16[8,128,128]{2,1,0:T(8,128)(2,1)S(1)}, u32[]{:S(2)}, u32[]{:S(2)}) async-start(bf16[8,128,128]{2,1,0:T(8,128)(2,1)} %get-tuple-element.34), calls=%async_computation.2 | async-start | bytes 524288 | tf_op jit(solution)/shard_map/all_to_all | solution.py:380
  34.1 4.1 %collective-permute-start.7 = (bf16[128,128]{1,0:T(8,128)(2,1)S(1)}, bf16[128,128]{1,0:T(8,128)(2,1)S(1)}, u32[]{:S(2)}, u32[]{:S(2)}) collective-permute-start(bf16[128,128]{1,0:T(8,128)(2,1)S(1)} %get-tuple-element.35), channel_id=1, source_target_pairs={{0,4},{4,0},{8,12},{12,8},{16,20},{20,16},{24,28},{28,24},{1,5},{5... | collective-permute-start | bytes 98312 | tf_op jit(solution)/shard_map/ppermute | solution.py:28

commit v6 on v5

--- a/solution.py
+++ b/solution.py
@@ -35,12 +35,16 @@
 def reorder_kernel(order_ref, rows_ref, out_ref, staged, leaving):
     per_leaf = rows_ref.shape[2] // BLOCK
     copies = []
+    arrived_slots = sum(slot << 3 * leaf for slot, leaf in enumerate(FIRST_MEMBERS))
     for slot, leaf in enumerate(MEMBERS):
         for t in range(per_leaf):
             source = order_ref[leaf * per_leaf + t]
             column = pl.multiple_of(lax.rem(source, per_leaf) * BLOCK, BLOCK)
+            from_slot = lax.shift_right_logical(
+                jnp.int32(arrived_slots), 3 * lax.div(source, per_leaf)
+            )
             staged[slot, :, pl.ds(t * BLOCK, BLOCK)] = rows_ref[
-                lax.div(source, per_leaf), :, pl.ds(column, BLOCK)
+                from_slot & 7, :, pl.ds(column, BLOCK)
             ]
         copies.append(pltpu.make_async_copy(staged.at[slot], out_ref.at[slot], leaving.at[slot]))
         copies[-1].start()
@@ -56,7 +60,7 @@
     return jnp.transpose(blocks, (0, 2, 1, 3)).reshape(leaf_count, per_group, row_count)
 
 
-def reorder(rows, places):
+def reorder(rows, order_kept):
     leaf_count = rows.shape[0]
     return pl.pallas_call(
         reorder_kernel,
@@ -68,37 +72,23 @@
             pltpu.SemaphoreType.DMA((leaf_count,)),
         ],
         compiler_params=pltpu.CompilerParams(vmem_limit_bytes=2 << 20),
-    )(pltpu.with_memory_space_constraint(places, pltpu.SMEM), near(rows))
-
-
-def early_kernel(order_ref, two_ref, three_ref, places_out, upper_out, three_out, arrivals):
+    )(pltpu.with_memory_space_constraint(order_kept, pltpu.SMEM), near(rows))
+
+
+def early_kernel(order_ref, two_ref, three_ref, order_kept_out, upper_out, three_out, arrivals):
     half = lax.axis_index("rhs") & 1
     two_half, three_half = two_ref.shape[0] // 2, three_ref.shape[0] // 2
     two = two_ref.at[pl.ds(pl.multiple_of(half * two_half, 16), two_half), :]
     three = three_ref.at[pl.ds(pl.multiple_of(half * three_half, 16), three_half), :]
     copies = [
-        pltpu.make_async_copy(order_ref, places_out, arrivals.at[0]),
+        pltpu.make_async_copy(order_ref, order_kept_out, arrivals.at[0]),
         pltpu.make_async_copy(two, upper_out.at[pl.ds(0, two_half), :], arrivals.at[1]),
         pltpu.make_async_copy(three, upper_out.at[pl.ds(two_half, three_half), :], arrivals.at[2]),
         pltpu.make_async_copy(three, three_out, arrivals.at[3]),
     ]
     for copy in copies:
         copy.start()
-    copies[0].wait()
-    leaves = len(FIRST_MEMBERS)
-    per_leaf = places_out.shape[0] // leaves
-    slots = sum(slot << 3 * leaf for slot, leaf in enumerate(FIRST_MEMBERS))
-
-    def place(t, carry):
-        source = places_out[t]
-        leaf = lax.div(source, per_leaf)
-        slot = lax.shift_right_logical(jnp.int32(slots), 3 * leaf) & 7
-        places_out[t] = slot * per_leaf + lax.rem(source, per_leaf)
-        return carry
-
-    if per_leaf * leaves < 128:
-        lax.fori_loop(0, per_leaf * leaves, place, 0, unroll=8)
-    for copy in copies[1:]:
+    for copy in copies:
         copy.wait()
 
 
@@ -143,21 +133,17 @@
     position = lax.axis_index("leaf")
     span = inverse_ref.shape[0]
     rank = one.shape[0]
-    copies = [pltpu.make_async_copy(one_ref, one, arrivals.at[0])]
     start = pl.multiple_of(share * span, 16)
-    copies.append(
-        pltpu.make_async_copy(inverse_ref, inverse_out.at[pl.ds(start, span), :], arrivals.at[1])
-    )
+    copies = [
+        pltpu.make_async_copy(one_ref, one, arrivals.at[0]),
+        pltpu.make_async_copy(coupling_ref, coupling, arrivals.at[1]),
+        pltpu.make_async_copy(inverse_ref, inverse_out.at[pl.ds(start, span), :], arrivals.at[2]),
+    ]
     at = 0
     for index, piece in enumerate((basis_ref, inner_ref)):
-        height = piece.shape[0]
-        copies.append(
-            pltpu.make_async_copy(
-                piece, narrow_out.at[pl.ds(at, height), :], arrivals.at[2 + index]
-            )
-        )
-        at += height
-    copies.append(pltpu.make_async_copy(coupling_ref, coupling, arrivals.at[4]))
+        place = narrow_out.at[pl.ds(at, piece.shape[0]), :]
+        copies.append(pltpu.make_async_copy(piece, place, arrivals.at[3 + index]))
+        at += piece.shape[0]
     for copy in copies:
         copy.start()
 
@@ -190,9 +176,12 @@
     width = rank // 4
     two_skeleton = jnp.concatenate(
         [through_two[:, (2 * g + 1) * width : (2 * g + 2) * width] for g in range(4)], axis=1
-    ).astype(bf16)
+    )
+    two_high = two_skeleton.astype(bf16)
+    two_low = (two_skeleton - two_high.astype(jnp.float32)).astype(bf16)
     through_two = through_two.T.astype(bf16)
-    through_three = product(two_skeleton, three_rows[...]).T.astype(bf16)
+    three = three_rows[...]
+    through_three = (product(two_high, three) + product(two_low, three)).T.astype(bf16)
     own_quad = position // 4 % 2
     for slot, leaf in enumerate(LAST_MEMBERS):
         at = 2 * slot * width
@@ -201,11 +190,13 @@
         two = through_two[2 * group * width : (2 * group + 1) * width]
         two = jnp.where(own_quad == leaf // 4, two, jnp.zeros_like(two))
         table_out[pl.ds(at + width, width), :] = two
-    for copy in copies[1:]:
+    for copy in copies[1:3]:
         copy.wait()
     height = coupling.shape[0]
     at = narrow_out.shape[0] - rank - height
     narrow_out[pl.ds(at, height), :] = product(inverse_out[...], coupling[...]).astype(bf16)
+    for copy in copies[3:]:
+        copy.wait()
 
 
 def weights_stage(inverse, inverse_pieces, upper, upper_near, one, basis, inner, coupling):
@@ -312,7 +303,7 @@
         out_specs=(INSIDE, OUTSIDE, INSIDE, INSIDE),
         scratch_shapes=[
             pltpu.VMEM((NODE_LEAVES, half, columns), bf16),
-            pltpu.SemaphoreType.DMA((2,)),
+            pltpu.SemaphoreType.DMA((4,)),
         ],
         compiler_params=pltpu.CompilerParams(vmem_limit_bytes=6 << 20),
     )(near(placed), near(table), near(narrow))
@@ -383,7 +374,7 @@
 
     arrived = spread(right_sides.reshape(leaf_count, columns // leaf_count, row_count), first_members)
 
-    places, upper_own, three = early_stage(block_order, merge_two, merge_three)
+    order_kept, upper_own, three = early_stage(block_order, merge_two, merge_three)
     upper_pieces = [upper_own, exchanged(upper_own, "leaf", 1)]
     upper_pieces += [exchanged(three, "leaf", flip) for flip in (2, 3)]
     inverse, _ = lax.optimization_barrier((leaf_inverse[0], upper_own))
@@ -408,7 +399,7 @@
     )
 
     if one_node:
-        returning = reorder(arrived, places)
+        returning = reorder(arrived, order_kept)
     else:
         returning = reorder_anywhere(arrived, block_order)
     placed = spread(returning, members)

time: 39.3 us -> 39.2 us (level)
  waiting for transfers between devices: 4.85 us -> 5.57 us
  starting transfers between devices: 25.5 us -> 25 us
    all_to_all x3, waiting for transfers between devices: 0.55 us -> 1.27 us  [spread(): lax.all_to_all(pieces, 'leaf', split_axis=0, concat_axis=0, tiled=True, a...]
    all_to_all x3, starting transfers between devices: 19.3 us -> 18.8 us  [spread(): lax.all_to_all(pieces, 'leaf', split_axis=0, concat_axis=0, tiled=True, a...]
    pallas_call x1, Pallas kernels: 1.31 us -> 0.88 us  [early_stage(): pl.pallas_call(early_kernel, out_shape=[pltpu.SMEM(block_order.shape, blo...]
  transfers between devices with their start and end apart: 11 -> 11, of which waited for: 4 -> 4; matrix products, arithmetic and copies ran while one was open for 0% -> 0% of each run, Pallas kernels for 14% -> 13%
where the time goes in v6:
time: 39.2 us; the launch traced here: 38.7 us
  starting transfers between devices  25 us (64%)
  Pallas kernels  7.37 us (19%)
  waiting for transfers between devices  5.57 us (14%)
  between operations  0.72 us (2%)
    all_to_all x3, starting transfers between devices, spread(): lax.all_to_all(pieces, 'leaf', split_axis=0, concat_axis=0, tiled=True, a...  18.8 us
    ppermute x8, starting transfers between devices, exchanged(): lax.ppermute(piece, axis, [(i, i ^ flip) for i in range(count) if i ^ fli...  6.25 us
    ppermute x8, waiting for transfers between devices, exchanged(): lax.ppermute(piece, axis, [(i, i ^ flip) for i in range(count) if i ^ fli...  4.3 us
    pallas_call x1, Pallas kernels, weights_stage(): pl.pallas_call(weights_kernel, out_shape=[pltpu.VMEM(shape, bf16) for sha...  2.1 us
    pallas_call x1, Pallas kernels, leaf_stage(): pl.pallas_call(leaf_kernel, out_shape=(pltpu.VMEM((columns, placed.shape[...  1.72 us
    all_to_all x3, waiting for transfers between devices, spread(): lax.all_to_all(pieces, 'leaf', split_axis=0, concat_axis=0, tiled=True, a...  1.27 us
    pallas_call x1, Pallas kernels, reorder(): pl.pallas_call(reorder_kernel, out_shape=pltpu.HBM(rows.shape, rows.dtype...  1.01 us
    pallas_call x1, Pallas kernels, eliminate_stage(): pl.pallas_call(eliminate_kernel, out_shape=jax.ShapeDtypeStruct(leading.s...  1.01 us
  transfers between devices with their start and end apart: 11, of which 4 were waited for; matrix products, arithmetic and copies ran while one was open for 0% of the time, Pallas kernels for 13%

profile of v6, /device:TPU:0, one launch (start us, length us, event | category | flops | bytes accessed | tf_op | source)
XLA Modules:
  0.0 38.7 jit_solution(10699367890567716534)
XLA Ops:
  0.6 0.0 copy-start
  0.6 8.0 %all-to-all-start = ((bf16[8,16,1024]{2,1,0:T(8,128)(2,1)}), bf16[8,16,1024]{2,1,0:T(8,128)(2,1)S(1)}, u32[]{:S(2)}, u32[]{:S(2)}) async-start(bf16[8,16,1024]{2,1,0:T(8,128)(2,1)} %bitcast.8), calls=%async_computation | async-start | bytes 524288 | tf_op jit(solution)/shard_map/all_to_all | solution.py:371
  8.6 0.9 %shard_map.128 = (s32[64]{0:T(128)S(4)}, bf16[96,512]{1,0:T(8,128)(2,1)S(1)}, bf16[32,512]{1,0:T(8,128)(2,1)S(1)}) custom-call(s32[64]{0:T(128)} %order_ref.1, bf16[128,512]{1,0:T(8,128)(2,1)} %two_ref.1, bf16[64,512]{1,0:T(8,128)(2,1)} %three_ref.1), custom_call_target="tpu_custom_call" | custom-call | tf_op jit(solution)/shard_map/pallas_call | solution.py:97
  9.5 1.6 %collective-permute-start = (bf16[192,768]{1,0:T(8,128)(2,1)}, bf16[192,768]{1,0:T(8,128)(2,1)S(1)}, u32[]{:S(2)}, u32[]{:S(2)}) collective-permute-start(bf16[192,768]{1,0:T(8,128)(2,1)} %bitcast.11), channel_id=1, source_target_pairs={{0,2},{1,3},{2,0},{3,1},{4,6},{5,7},{6,4},{7,5},{8,10},{9,11},{10,... | collective-permute-start | bytes 884744 | tf_op jit(solution)/shard_map/ppermute | solution.py:28
  11.1 1.5 %collective-permute-start.1 = (bf16[96,512]{1,0:T(8,128)(2,1)S(1)}, bf16[96,512]{1,0:T(8,128)(2,1)S(1)}, u32[]{:S(2)}, u32[]{:S(2)}) collective-permute-start(bf16[96,512]{1,0:T(8,128)(2,1)S(1)} %get-tuple-element.24), channel_id=1, source_target_pairs={{0,4},{4,0},{8,12},{12,8},{16,20},{20,16},{24,28},{28,24},{1,5},{5... | collective-permute-start | bytes 294920 | tf_op jit(solution)/shard_map/ppermute | solution.py:28
  12.5 0.6 %collective-permute-start.3 = (bf16[32,512]{1,0:T(8,128)(2,1)S(1)}, bf16[32,512]{1,0:T(8,128)(2,1)S(1)}, u32[]{:S(2)}, u32[]{:S(2)}) collective-permute-start(bf16[32,512]{1,0:T(8,128)(2,1)S(1)} %get-tuple-element.26), channel_id=1, source_target_pairs={{0,12},{4,8},{8,4},{12,0},{16,28},{20,24},{24,20},{28,16},{1,13},{... | collective-permute-start | bytes 98312 | tf_op jit(solution)/shard_map/ppermute | solution.py:28
  13.1 1.5 %collective-permute-start.2 = (bf16[32,512]{1,0:T(8,128)(2,1)S(1)}, bf16[32,512]{1,0:T(8,128)(2,1)S(1)}, u32[]{:S(2)}, u32[]{:S(2)}) collective-permute-start(bf16[32,512]{1,0:T(8,128)(2,1)S(1)} %get-tuple-element.26), channel_id=1, source_target_pairs={{0,8},{4,12},{8,0},{12,4},{16,24},{20,28},{24,16},{28,20},{1,9},{5... | collective-permute-start | bytes 98312 | tf_op jit(solution)/shard_map/ppermute | solution.py:28
  14.6 1.0 %all-to-all-done.rows_ref = bf16[8,16,1024]{2,1,0:T(8,128)(2,1)S(1)} async-done(((bf16[8,16,1024]{2,1,0:T(8,128)(2,1)}), bf16[8,16,1024]{2,1,0:T(8,128)(2,1)S(1)}, u32[]{:S(2)}, u32[]{:S(2)}) %all-to-all-start) | async-done | bytes 262176 | tf_op jit(solution)/shard_map/all_to_all | solution.py:371
  15.5 1.0 %shard_map.129 = bf16[8,16,1024]{2,1,0:T(8,128)(2,1)} custom-call(s32[64]{0:T(128)S(4)} %get-tuple-element.23.order_ref, bf16[8,16,1024]{2,1,0:T(8,128)(2,1)S(1)} %all-to-all-done.rows_ref), custom_call_target="tpu_custom_call" | custom-call | tf_op jit(solution)/shard_map/pallas_call | solution.py:65
  16.6 4.7 %all-to-all-start.1 = ((bf16[8,16,1024]{2,1,0:T(8,128)(2,1)}), bf16[8,16,1024]{2,1,0:T(8,128)(2,1)S(1)}, u32[]{:S(2)}, u32[]{:S(2)}) async-start(bf16[8,16,1024]{2,1,0:T(8,128)(2,1)} %shard_map.129), calls=%async_computation.1 | async-start | bytes 524288 | tf_op jit(solution)/shard_map/all_to_all | solution.py:371
  21.3 0.0 collective-permute-done.1
  21.3 0.0 collective-permute-done.inverse_far_ref
  21.3 0.1 collective-permute-start.4
  21.4 0.5 %collective-permute-start.5 = (bf16[192,768]{1,0:T(8,128)(2,1)S(1)}, bf16[192,768]{1,0:T(8,128)(2,1)S(1)}, u32[]{:S(2)}, u32[]{:S(2)}) collective-permute-start(bf16[192,768]{1,0:T(8,128)(2,1)S(1)} %collective-permute-done.inverse_far_ref), channel_id=1, source_target_pairs={{0,1},{1,0},{2,3},{3,2},{4,5},{5,4},{6,7},{7,6},{8,9},{9,8},{10,11... | collective-permute-start | bytes 884744 | tf_op jit(solution)/shard_map/ppermute | solution.py:28
  21.9 0.1 collective-permute-start.6
  22.0 1.8 %collective-permute-done.6.upper_near_ref = bf16[256,512]{1,0:T(8,128)(2,1)S(1)} collective-permute-done((bf16[256,512]{1,0:T(8,128)(2,1)S(1)}, bf16[256,512]{1,0:T(8,128)(2,1)S(1)}, u32[]{:S(2)}, u32[]{:S(2)}) %collective-permute-start.6) | collective-permute-done | bytes 262176 | tf_op jit(solution)/shard_map/ppermute | solution.py:28
  23.8 2.1 %shard_map.130 = (bf16[768,768]{1,0:T(8,128)(2,1)S(1)}, bf16[1024,256]{1,0:T(8,128)(2,1)S(1)}, bf16[2304,256]{1,0:T(8,128)(2,1)S(1)}) custom-call(bf16[192,768]{1,0:T(8,128)(2,1)} %bitcast.12, bf16[192,768]{1,0:T(8,128)(2,1)S(1)} %collective-permute-done.inverse_far_ref, bf16[192,768]{1,0:T(8,128)(2,1)S(1)} %collective-permute-done.4.inverse_near_ref, ...), custom_call_target="tpu_custom_call" | custom-call | flops 1000000000 | bytes 6000000 | tf_op jit(solution)/shard_map/pallas_call | solution.py:208
  25.9 0.3 all-to-all-done.1.placed_ref
  26.2 1.7 %shard_map.131 = (bf16[128,768]{1,0:T(8,128)(2,1)S(1)}, bf16[8,128,128]{2,1,0:T(8,128)(2,1)}, bf16[128,128]{1,0:T(8,128)(2,1)S(1)}, f32[128,128]{1,0:T(8,128)S(1)}) custom-call(bf16[8,16,1024]{2,1,0:T(8,128)(2,1)S(1)} %all-to-all-done.1.placed_ref, bf16[1024,256]{1,0:T(8,128)(2,1)S(1)} %get-tuple-element.30.table_ref, ...), custom_call_target="tpu_custom_call" | custom-call | tf_op jit(solution)/shard_map/pallas_call | solution.py:294
  27.9 6.1 %all-to-all-start.2 = ((bf16[8,128,128]{2,1,0:T(8,128)(2,1)}), bf16[8,128,128]{2,1,0:T(8,128)(2,1)S(1)}, u32[]{:S(2)}, u32[]{:S(2)}) async-start(bf16[8,128,128]{2,1,0:T(8,128)(2,1)} %get-tuple-element.34), calls=%async_computation.2 | async-start | bytes 524288 | tf_op jit(solution)/shard_map/all_to_all | solution.py:371
  34.0 0.6 %collective-permute-start.7 = (bf16[128,128]{1,0:T(8,128)(2,1)S(1)}, bf16[128,128]{1,0:T(8,128)(2,1)S(1)}, u32[]{:S(2)}, u32[]{:S(2)}) collective-permute-start(bf16[128,128]{1,0:T(8,128)(2,1)S(1)} %get-tuple-element.35), channel_id=1, source_target_pairs={{0,4},{4,0},{8,12},{12,8},{16,20},{20,16},{24,28},{28,24},{1,5},{5... | collective-permute-start | bytes 98312 | tf_op jit(solution)/shard_map/ppermute | solution.py:28
  34.6 1.0 %shard_map.132 = bf16[128,768]{1,0:T(8,128)(2,1)} custom-call(bf16[128,768]{1,0:T(8,128)(2,1)S(1)} %get-tuple-element.32.leading_ref, bf16[768,768]{1,0:T(8,128)(2,1)S(1)} %get-tuple-element.33.inverse_ref), custom_call_target="tpu_custom_call" | custom-call | flops 1000000000 | bytes 6000000 | tf_op jit(solution)/shard_map/pallas_call | solution.py:317
  35.6 2.5 %collective-permute-done.7.received_one_ref = bf16[128,128]{1,0:T(8,128)(2,1)S(1)} collective-permute-done((bf16[128,128]{1,0:T(8,128)(2,1)S(1)}, bf16[128,128]{1,0:T(8,128)(2,1)S(1)}, u32[]{:S(2)}, u32[]{:S(2)}) %collective-permute-start.7) | collective-permute-done | bytes 32800 | tf_op jit(solution)/shard_map/ppermute | solution.py:28
  38.1 0.7 %shard_map.133 = (f32[128,128]{1,0:T(8,128)}, f32[64,128]{1,0:T(8,128)}, f32[32,128]{1,0:T(8,128)}, f32[32,128]{1,0:T(8,128)}) custom-call(bf16[8,128,128]{2,1,0:T(8,128)(2,1)S(1)} %all-to-all-done.2.received_ref, bf16[128,128]{1,0:T(8,128)(2,1)S(1)} %collective-permute-done.7.received_one_ref, f32[128,128]{1,0:T(8,128)S(1)} %get-tuple-element.36.kept_one_ref), custom_call_target="tpu_custom_call" | custom-call | tf_op jit(solution)/shard_map/pallas_call | solution.py:344
  (7 shorter events, 0.0 us)
Async XLA Ops:
  0.6 20.7 %copy-start = (bf16[1,192,768]{2,1,0:T(8,128)(2,1)S(1)}, bf16[1,192,768]{2,1,0:T(8,128)(2,1)}, u32[]{:S(2)}) copy-start(bf16[1,192,768]{2,1,0:T(8,128)(2,1)} %param.13) | copy-start | bytes 884740
  0.6 14.9 %all-to-all-start = ((bf16[8,16,1024]{2,1,0:T(8,128)(2,1)}), bf16[8,16,1024]{2,1,0:T(8,128)(2,1)S(1)}, u32[]{:S(2)}, u32[]{:S(2)}) async-start(bf16[8,16,1024]{2,1,0:T(8,128)(2,1)} %bitcast.8), calls=%async_computation | async-start | bytes 524288 | tf_op jit(solution)/shard_map/all_to_all | solution.py:371
  9.5 11.8 %collective-permute-start = (bf16[192,768]{1,0:T(8,128)(2,1)}, bf16[192,768]{1,0:T(8,128)(2,1)S(1)}, u32[]{:S(2)}, u32[]{:S(2)}) collective-permute-start(bf16[192,768]{1,0:T(8,128)(2,1)} %bitcast.11), channel_id=1, source_target_pairs={{0,2},{1,3},{2,0},{3,1},{4,6},{5,7},{6,4},{7,5},{8,10},{9,11},{10,... | collective-permute-start | bytes 884744 | tf_op jit(solution)/shard_map/ppermute | solution.py:28
  11.1 10.2 %collective-permute-start.1 = (bf16[96,512]{1,0:T(8,128)(2,1)S(1)}, bf16[96,512]{1,0:T(8,128)(2,1)S(1)}, u32[]{:S(2)}, u32[]{:S(2)}) collective-permute-start(bf16[96,512]{1,0:T(8,128)(2,1)S(1)} %get-tuple-element.24), channel_id=1, source_target_pairs={{0,4},{4,0},{8,12},{12,8},{16,20},{20,16},{24,28},{28,24},{1,5},{5... | collective-permute-start | bytes 294920 | tf_op jit(solution)/shard_map/ppermute | solution.py:28
  12.5 8.7 %collective-permute-start.3 = (bf16[32,512]{1,0:T(8,128)(2,1)S(1)}, bf16[32,512]{1,0:T(8,128)(2,1)S(1)}, u32[]{:S(2)}, u32[]{:S(2)}) collective-permute-start(bf16[32,512]{1,0:T(8,128)(2,1)S(1)} %get-tuple-element.26), channel_id=1, source_target_pairs={{0,12},{4,8},{8,4},{12,0},{16,28},{20,24},{24,20},{28,16},{1,13},{... | collective-permute-start | bytes 98312 | tf_op jit(solution)/shard_map/ppermute | solution.py:28
  13.1 8.2 %collective-permute-start.2 = (bf16[32,512]{1,0:T(8,128)(2,1)S(1)}, bf16[32,512]{1,0:T(8,128)(2,1)S(1)}, u32[]{:S(2)}, u32[]{:S(2)}) collective-permute-start(bf16[32,512]{1,0:T(8,128)(2,1)S(1)} %get-tuple-element.26), channel_id=1, source_target_pairs={{0,8},{4,12},{8,0},{12,4},{16,24},{20,28},{24,16},{28,20},{1,9},{5... | collective-permute-start | bytes 98312 | tf_op jit(solution)/shard_map/ppermute | solution.py:28
  16.6 9.6 %all-to-all-start.1 = ((bf16[8,16,1024]{2,1,0:T(8,128)(2,1)}), bf16[8,16,1024]{2,1,0:T(8,128)(2,1)S(1)}, u32[]{:S(2)}, u32[]{:S(2)}) async-start(bf16[8,16,1024]{2,1,0:T(8,128)(2,1)} %shard_map.129), calls=%async_computation.1 | async-start | bytes 524288 | tf_op jit(solution)/shard_map/all_to_all | solution.py:371
  21.3 2.4 %collective-permute-start.4 = (bf16[192,768]{1,0:T(8,128)(2,1)S(1)}, bf16[192,768]{1,0:T(8,128)(2,1)S(1)}, u32[]{:S(2)}, u32[]{:S(2)}) collective-permute-start(bf16[192,768]{1,0:T(8,128)(2,1)S(1)} %bitcast.13), channel_id=1, source_target_pairs={{0,1},{1,0},{2,3},{3,2},{4,5},{5,4},{6,7},{7,6},{8,9},{9,8},{10,11... | collective-permute-start | bytes 884744 | tf_op jit(solution)/shard_map/ppermute | solution.py:28
  21.4 2.4 %collective-permute-start.5 = (bf16[192,768]{1,0:T(8,128)(2,1)S(1)}, bf16[192,768]{1,0:T(8,128)(2,1)S(1)}, u32[]{:S(2)}, u32[]{:S(2)}) collective-permute-start(bf16[192,768]{1,0:T(8,128)(2,1)S(1)} %collective-permute-done.inverse_far_ref), channel_id=1, source_target_pairs={{0,1},{1,0},{2,3},{3,2},{4,5},{5,4},{6,7},{7,6},{8,9},{9,8},{10,11... | collective-permute-start | bytes 884744 | tf_op jit(solution)/shard_map/ppermute | solution.py:28
  21.9 1.9 %collective-permute-start.6 = (bf16[256,512]{1,0:T(8,128)(2,1)S(1)}, bf16[256,512]{1,0:T(8,128)(2,1)S(1)}, u32[]{:S(2)}, u32[]{:S(2)}) collective-permute-start(bf16[256,512]{1,0:T(8,128)(2,1)S(1)} %pad_maximum_fusion.upper_ref), channel_id=1, source_target_pairs={{0,1},{1,0},{2,3},{3,2},{4,5},{5,4},{6,7},{7,6},{8,9},{9,8},{10,11... | collective-permute-start | bytes 786440 | tf_op jit(solution)/shard_map/ppermute | solution.py:28
  27.9 10.2 %all-to-all-start.2 = ((bf16[8,128,128]{2,1,0:T(8,128)(2,1)}), bf16[8,128,128]{2,1,0:T(8,128)(2,1)S(1)}, u32[]{:S(2)}, u32[]{:S(2)}) async-start(bf16[8,128,128]{2,1,0:T(8,128)(2,1)} %get-tuple-element.34), calls=%async_computation.2 | async-start | bytes 524288 | tf_op jit(solution)/shard_map/all_to_all | solution.py:371
  34.0 4.1 %collective-permute-start.7 = (bf16[128,128]{1,0:T(8,128)(2,1)S(1)}, bf16[128,128]{1,0:T(8,128)(2,1)S(1)}, u32[]{:S(2)}, u32[]{:S(2)}) collective-permute-start(bf16[128,128]{1,0:T(8,128)(2,1)S(1)} %get-tuple-element.35), channel_id=1, source_target_pairs={{0,4},{4,0},{8,12},{12,8},{16,20},{20,16},{24,28},{28,24},{1,5},{5... | collective-permute-start | bytes 98312 | tf_op jit(solution)/shard_map/ppermute | solution.py:28

commit v7 on v6

--- a/solution.py
+++ b/solution.py
@@ -8,7 +8,7 @@
 BLOCK = 128
 NODE_LEAVES = 8
 FIRST_MEMBERS = (4, 5, 6, 7, 0, 1, 2, 3)
-MEMBERS = (4, 7, 3, 1, 0, 2, 6, 5)
+MEMBERS = (4, 2, 3, 5, 0, 6, 7, 1)
 LAST_MEMBERS = (5, 4, 1, 0, 7, 6, 3, 2)
 INSIDE = pl.BlockSpec(memory_space=pltpu.VMEM)
 SCALARS = pl.BlockSpec(memory_space=pltpu.SMEM)

time: 39.2 us -> 39.2 us (level)
  no operation moved by 1% of the time
where the time goes in v7:
time: 39.2 us; the launch traced here: 38.7 us
  starting transfers between devices  25 us (64%)
  Pallas kernels  7.37 us (19%)
  waiting for transfers between devices  5.63 us (14%)
  between operations  0.72 us (2%)
    all_to_all x3, starting transfers between devices, spread(): lax.all_to_all(pieces, 'leaf', split_axis=0, concat_axis=0, tiled=True, a...  18.8 us
    ppermute x8, starting transfers between devices, exchanged(): lax.ppermute(piece, axis, [(i, i ^ flip) for i in range(count) if i ^ fli...  6.25 us
    ppermute x8, waiting for transfers between devices, exchanged(): lax.ppermute(piece, axis, [(i, i ^ flip) for i in range(count) if i ^ fli...  4.3 us
    pallas_call x1, Pallas kernels, weights_stage(): pl.pallas_call(weights_kernel, out_shape=[pltpu.VMEM(shape, bf16) for sha...  2.1 us
    pallas_call x1, Pallas kernels, leaf_stage(): pl.pallas_call(leaf_kernel, out_shape=(pltpu.VMEM((columns, placed.shape[...  1.71 us
    all_to_all x3, waiting for transfers between devices, spread(): lax.all_to_all(pieces, 'leaf', split_axis=0, concat_axis=0, tiled=True, a...  1.32 us
    pallas_call x1, Pallas kernels, reorder(): pl.pallas_call(reorder_kernel, out_shape=pltpu.HBM(rows.shape, rows.dtype...  1.01 us
    pallas_call x1, Pallas kernels, eliminate_stage(): pl.pallas_call(eliminate_kernel, out_shape=jax.ShapeDtypeStruct(leading.s...  1 us
  transfers between devices with their start and end apart: 11, of which 4 were waited for; matrix products, arithmetic and copies ran while one was open for 0% of the time, Pallas kernels for 13%

profile of v7, /device:TPU:0, one launch (start us, length us, event | category | flops | bytes accessed | tf_op | source)
XLA Modules:
  0.0 38.7 jit_solution(4062225374651227845)
XLA Ops:
  0.6 0.0 copy-start
  0.6 8.0 %all-to-all-start = ((bf16[8,16,1024]{2,1,0:T(8,128)(2,1)}), bf16[8,16,1024]{2,1,0:T(8,128)(2,1)S(1)}, u32[]{:S(2)}, u32[]{:S(2)}) async-start(bf16[8,16,1024]{2,1,0:T(8,128)(2,1)} %bitcast.8), calls=%async_computation | async-start | bytes 524288 | tf_op jit(solution)/shard_map/all_to_all | solution.py:371
  8.6 0.9 %shard_map.128 = (s32[64]{0:T(128)S(4)}, bf16[96,512]{1,0:T(8,128)(2,1)S(1)}, bf16[32,512]{1,0:T(8,128)(2,1)S(1)}) custom-call(s32[64]{0:T(128)} %order_ref.1, bf16[128,512]{1,0:T(8,128)(2,1)} %two_ref.1, bf16[64,512]{1,0:T(8,128)(2,1)} %three_ref.1), custom_call_target="tpu_custom_call" | custom-call | tf_op jit(solution)/shard_map/pallas_call | solution.py:97
  9.5 1.6 %collective-permute-start = (bf16[192,768]{1,0:T(8,128)(2,1)}, bf16[192,768]{1,0:T(8,128)(2,1)S(1)}, u32[]{:S(2)}, u32[]{:S(2)}) collective-permute-start(bf16[192,768]{1,0:T(8,128)(2,1)} %bitcast.11), channel_id=1, source_target_pairs={{0,2},{1,3},{2,0},{3,1},{4,6},{5,7},{6,4},{7,5},{8,10},{9,11},{10,... | collective-permute-start | bytes 884744 | tf_op jit(solution)/shard_map/ppermute | solution.py:28
  11.1 1.5 %collective-permute-start.1 = (bf16[96,512]{1,0:T(8,128)(2,1)S(1)}, bf16[96,512]{1,0:T(8,128)(2,1)S(1)}, u32[]{:S(2)}, u32[]{:S(2)}) collective-permute-start(bf16[96,512]{1,0:T(8,128)(2,1)S(1)} %get-tuple-element.24), channel_id=1, source_target_pairs={{0,4},{4,0},{8,12},{12,8},{16,20},{20,16},{24,28},{28,24},{1,5},{5... | collective-permute-start | bytes 294920 | tf_op jit(solution)/shard_map/ppermute | solution.py:28
  12.5 0.6 %collective-permute-start.3 = (bf16[32,512]{1,0:T(8,128)(2,1)S(1)}, bf16[32,512]{1,0:T(8,128)(2,1)S(1)}, u32[]{:S(2)}, u32[]{:S(2)}) collective-permute-start(bf16[32,512]{1,0:T(8,128)(2,1)S(1)} %get-tuple-element.26), channel_id=1, source_target_pairs={{0,12},{4,8},{8,4},{12,0},{16,28},{20,24},{24,20},{28,16},{1,13},{... | collective-permute-start | bytes 98312 | tf_op jit(solution)/shard_map/ppermute | solution.py:28
  13.1 1.5 %collective-permute-start.2 = (bf16[32,512]{1,0:T(8,128)(2,1)S(1)}, bf16[32,512]{1,0:T(8,128)(2,1)S(1)}, u32[]{:S(2)}, u32[]{:S(2)}) collective-permute-start(bf16[32,512]{1,0:T(8,128)(2,1)S(1)} %get-tuple-element.26), channel_id=1, source_target_pairs={{0,8},{4,12},{8,0},{12,4},{16,24},{20,28},{24,16},{28,20},{1,9},{5... | collective-permute-start | bytes 98312 | tf_op jit(solution)/shard_map/ppermute | solution.py:28
  14.6 1.0 %all-to-all-done.rows_ref = bf16[8,16,1024]{2,1,0:T(8,128)(2,1)S(1)} async-done(((bf16[8,16,1024]{2,1,0:T(8,128)(2,1)}), bf16[8,16,1024]{2,1,0:T(8,128)(2,1)S(1)}, u32[]{:S(2)}, u32[]{:S(2)}) %all-to-all-start) | async-done | bytes 262176 | tf_op jit(solution)/shard_map/all_to_all | solution.py:371
  15.5 1.0 %shard_map.129 = bf16[8,16,1024]{2,1,0:T(8,128)(2,1)} custom-call(s32[64]{0:T(128)S(4)} %get-tuple-element.23.order_ref, bf16[8,16,1024]{2,1,0:T(8,128)(2,1)S(1)} %all-to-all-done.rows_ref), custom_call_target="tpu_custom_call" | custom-call | tf_op jit(solution)/shard_map/pallas_call | solution.py:65
  16.6 4.7 %all-to-all-start.1 = ((bf16[8,16,1024]{2,1,0:T(8,128)(2,1)}), bf16[8,16,1024]{2,1,0:T(8,128)(2,1)S(1)}, u32[]{:S(2)}, u32[]{:S(2)}) async-start(bf16[8,16,1024]{2,1,0:T(8,128)(2,1)} %shard_map.129), calls=%async_computation.1 | async-start | bytes 524288 | tf_op jit(solution)/shard_map/all_to_all | solution.py:371
  21.3 0.0 collective-permute-done.3
  21.3 0.0 collective-permute-done.2
  21.3 0.1 collective-permute-start.4
  21.4 0.5 %collective-permute-start.5 = (bf16[192,768]{1,0:T(8,128)(2,1)S(1)}, bf16[192,768]{1,0:T(8,128)(2,1)S(1)}, u32[]{:S(2)}, u32[]{:S(2)}) collective-permute-start(bf16[192,768]{1,0:T(8,128)(2,1)S(1)} %collective-permute-done.inverse_far_ref), channel_id=1, source_target_pairs={{0,1},{1,0},{2,3},{3,2},{4,5},{5,4},{6,7},{7,6},{8,9},{9,8},{10,11... | collective-permute-start | bytes 884744 | tf_op jit(solution)/shard_map/ppermute | solution.py:28
  21.9 0.1 collective-permute-start.6
  22.0 1.8 %collective-permute-done.6.upper_near_ref = bf16[256,512]{1,0:T(8,128)(2,1)S(1)} collective-permute-done((bf16[256,512]{1,0:T(8,128)(2,1)S(1)}, bf16[256,512]{1,0:T(8,128)(2,1)S(1)}, u32[]{:S(2)}, u32[]{:S(2)}) %collective-permute-start.6) | collective-permute-done | bytes 262176 | tf_op jit(solution)/shard_map/ppermute | solution.py:28
  23.8 2.1 %shard_map.130 = (bf16[768,768]{1,0:T(8,128)(2,1)S(1)}, bf16[1024,256]{1,0:T(8,128)(2,1)S(1)}, bf16[2304,256]{1,0:T(8,128)(2,1)S(1)}) custom-call(bf16[192,768]{1,0:T(8,128)(2,1)} %bitcast.12, bf16[192,768]{1,0:T(8,128)(2,1)S(1)} %collective-permute-done.inverse_far_ref, bf16[192,768]{1,0:T(8,128)(2,1)S(1)} %collective-permute-done.4.inverse_near_ref, ...), custom_call_target="tpu_custom_call" | custom-call | flops 1000000000 | bytes 6000000 | tf_op jit(solution)/shard_map/pallas_call | solution.py:208
  25.9 0.3 all-to-all-done.1.placed_ref
  26.2 1.7 %shard_map.131 = (bf16[128,768]{1,0:T(8,128)(2,1)S(1)}, bf16[8,128,128]{2,1,0:T(8,128)(2,1)}, bf16[128,128]{1,0:T(8,128)(2,1)S(1)}, f32[128,128]{1,0:T(8,128)S(1)}) custom-call(bf16[8,16,1024]{2,1,0:T(8,128)(2,1)S(1)} %all-to-all-done.1.placed_ref, bf16[1024,256]{1,0:T(8,128)(2,1)S(1)} %get-tuple-element.30.table_ref, ...), custom_call_target="tpu_custom_call" | custom-call | tf_op jit(solution)/shard_map/pallas_call | solution.py:294
  28.0 6.0 %all-to-all-start.2 = ((bf16[8,128,128]{2,1,0:T(8,128)(2,1)}), bf16[8,128,128]{2,1,0:T(8,128)(2,1)S(1)}, u32[]{:S(2)}, u32[]{:S(2)}) async-start(bf16[8,128,128]{2,1,0:T(8,128)(2,1)} %get-tuple-element.34), calls=%async_computation.2 | async-start | bytes 524288 | tf_op jit(solution)/shard_map/all_to_all | solution.py:371
  34.0 0.6 %collective-permute-start.7 = (bf16[128,128]{1,0:T(8,128)(2,1)S(1)}, bf16[128,128]{1,0:T(8,128)(2,1)S(1)}, u32[]{:S(2)}, u32[]{:S(2)}) collective-permute-start(bf16[128,128]{1,0:T(8,128)(2,1)S(1)} %get-tuple-element.35), channel_id=1, source_target_pairs={{0,4},{4,0},{8,12},{12,8},{16,20},{20,16},{24,28},{28,24},{1,5},{5... | collective-permute-start | bytes 98312 | tf_op jit(solution)/shard_map/ppermute | solution.py:28
  34.6 1.0 %shard_map.132 = bf16[128,768]{1,0:T(8,128)(2,1)} custom-call(bf16[128,768]{1,0:T(8,128)(2,1)S(1)} %get-tuple-element.32.leading_ref, bf16[768,768]{1,0:T(8,128)(2,1)S(1)} %get-tuple-element.33.inverse_ref), custom_call_target="tpu_custom_call" | custom-call | flops 1000000000 | bytes 6000000 | tf_op jit(solution)/shard_map/pallas_call | solution.py:317
  35.6 2.5 %collective-permute-done.7.received_one_ref = bf16[128,128]{1,0:T(8,128)(2,1)S(1)} collective-permute-done((bf16[128,128]{1,0:T(8,128)(2,1)S(1)}, bf16[128,128]{1,0:T(8,128)(2,1)S(1)}, u32[]{:S(2)}, u32[]{:S(2)}) %collective-permute-start.7) | collective-permute-done | bytes 32800 | tf_op jit(solution)/shard_map/ppermute | solution.py:28
  38.1 0.7 %shard_map.133 = (f32[128,128]{1,0:T(8,128)}, f32[64,128]{1,0:T(8,128)}, f32[32,128]{1,0:T(8,128)}, f32[32,128]{1,0:T(8,128)}) custom-call(bf16[8,128,128]{2,1,0:T(8,128)(2,1)S(1)} %all-to-all-done.2.received_ref, bf16[128,128]{1,0:T(8,128)(2,1)S(1)} %collective-permute-done.7.received_one_ref, f32[128,128]{1,0:T(8,128)S(1)} %get-tuple-element.36.kept_one_ref), custom_call_target="tpu_custom_call" | custom-call | tf_op jit(solution)/shard_map/pallas_call | solution.py:344
  (7 shorter events, 0.0 us)
Async XLA Ops:
  0.6 20.7 %copy-start = (bf16[1,192,768]{2,1,0:T(8,128)(2,1)S(1)}, bf16[1,192,768]{2,1,0:T(8,128)(2,1)}, u32[]{:S(2)}) copy-start(bf16[1,192,768]{2,1,0:T(8,128)(2,1)} %param.13) | copy-start | bytes 884740
  0.6 14.9 %all-to-all-start = ((bf16[8,16,1024]{2,1,0:T(8,128)(2,1)}), bf16[8,16,1024]{2,1,0:T(8,128)(2,1)S(1)}, u32[]{:S(2)}, u32[]{:S(2)}) async-start(bf16[8,16,1024]{2,1,0:T(8,128)(2,1)} %bitcast.8), calls=%async_computation | async-start | bytes 524288 | tf_op jit(solution)/shard_map/all_to_all | solution.py:371
  9.5 11.8 %collective-permute-start = (bf16[192,768]{1,0:T(8,128)(2,1)}, bf16[192,768]{1,0:T(8,128)(2,1)S(1)}, u32[]{:S(2)}, u32[]{:S(2)}) collective-permute-start(bf16[192,768]{1,0:T(8,128)(2,1)} %bitcast.11), channel_id=1, source_target_pairs={{0,2},{1,3},{2,0},{3,1},{4,6},{5,7},{6,4},{7,5},{8,10},{9,11},{10,... | collective-permute-start | bytes 884744 | tf_op jit(solution)/shard_map/ppermute | solution.py:28
  11.1 10.2 %collective-permute-start.1 = (bf16[96,512]{1,0:T(8,128)(2,1)S(1)}, bf16[96,512]{1,0:T(8,128)(2,1)S(1)}, u32[]{:S(2)}, u32[]{:S(2)}) collective-permute-start(bf16[96,512]{1,0:T(8,128)(2,1)S(1)} %get-tuple-element.24), channel_id=1, source_target_pairs={{0,4},{4,0},{8,12},{12,8},{16,20},{20,16},{24,28},{28,24},{1,5},{5... | collective-permute-start | bytes 294920 | tf_op jit(solution)/shard_map/ppermute | solution.py:28
  12.5 8.7 %collective-permute-start.3 = (bf16[32,512]{1,0:T(8,128)(2,1)S(1)}, bf16[32,512]{1,0:T(8,128)(2,1)S(1)}, u32[]{:S(2)}, u32[]{:S(2)}) collective-permute-start(bf16[32,512]{1,0:T(8,128)(2,1)S(1)} %get-tuple-element.26), channel_id=1, source_target_pairs={{0,12},{4,8},{8,4},{12,0},{16,28},{20,24},{24,20},{28,16},{1,13},{... | collective-permute-start | bytes 98312 | tf_op jit(solution)/shard_map/ppermute | solution.py:28
  13.1 8.2 %collective-permute-start.2 = (bf16[32,512]{1,0:T(8,128)(2,1)S(1)}, bf16[32,512]{1,0:T(8,128)(2,1)S(1)}, u32[]{:S(2)}, u32[]{:S(2)}) collective-permute-start(bf16[32,512]{1,0:T(8,128)(2,1)S(1)} %get-tuple-element.26), channel_id=1, source_target_pairs={{0,8},{4,12},{8,0},{12,4},{16,24},{20,28},{24,16},{28,20},{1,9},{5... | collective-permute-start | bytes 98312 | tf_op jit(solution)/shard_map/ppermute | solution.py:28
  16.6 9.7 %all-to-all-start.1 = ((bf16[8,16,1024]{2,1,0:T(8,128)(2,1)}), bf16[8,16,1024]{2,1,0:T(8,128)(2,1)S(1)}, u32[]{:S(2)}, u32[]{:S(2)}) async-start(bf16[8,16,1024]{2,1,0:T(8,128)(2,1)} %shard_map.129), calls=%async_computation.1 | async-start | bytes 524288 | tf_op jit(solution)/shard_map/all_to_all | solution.py:371
  21.3 2.4 %collective-permute-start.4 = (bf16[192,768]{1,0:T(8,128)(2,1)S(1)}, bf16[192,768]{1,0:T(8,128)(2,1)S(1)}, u32[]{:S(2)}, u32[]{:S(2)}) collective-permute-start(bf16[192,768]{1,0:T(8,128)(2,1)S(1)} %bitcast.13), channel_id=1, source_target_pairs={{0,1},{1,0},{2,3},{3,2},{4,5},{5,4},{6,7},{7,6},{8,9},{9,8},{10,11... | collective-permute-start | bytes 884744 | tf_op jit(solution)/shard_map/ppermute | solution.py:28
  21.4 2.4 %collective-permute-start.5 = (bf16[192,768]{1,0:T(8,128)(2,1)S(1)}, bf16[192,768]{1,0:T(8,128)(2,1)S(1)}, u32[]{:S(2)}, u32[]{:S(2)}) collective-permute-start(bf16[192,768]{1,0:T(8,128)(2,1)S(1)} %collective-permute-done.inverse_far_ref), channel_id=1, source_target_pairs={{0,1},{1,0},{2,3},{3,2},{4,5},{5,4},{6,7},{7,6},{8,9},{9,8},{10,11... | collective-permute-start | bytes 884744 | tf_op jit(solution)/shard_map/ppermute | solution.py:28
  21.9 1.9 %collective-permute-start.6 = (bf16[256,512]{1,0:T(8,128)(2,1)S(1)}, bf16[256,512]{1,0:T(8,128)(2,1)S(1)}, u32[]{:S(2)}, u32[]{:S(2)}) collective-permute-start(bf16[256,512]{1,0:T(8,128)(2,1)S(1)} %pad_maximum_fusion.upper_ref), channel_id=1, source_target_pairs={{0,1},{1,0},{2,3},{3,2},{4,5},{5,4},{6,7},{7,6},{8,9},{9,8},{10,11... | collective-permute-start | bytes 786440 | tf_op jit(solution)/shard_map/ppermute | solution.py:28
  28.0 10.1 %all-to-all-start.2 = ((bf16[8,128,128]{2,1,0:T(8,128)(2,1)}), bf16[8,128,128]{2,1,0:T(8,128)(2,1)S(1)}, u32[]{:S(2)}, u32[]{:S(2)}) async-start(bf16[8,128,128]{2,1,0:T(8,128)(2,1)} %get-tuple-element.34), calls=%async_computation.2 | async-start | bytes 524288 | tf_op jit(solution)/shard_map/all_to_all | solution.py:371
  34.0 4.1 %collective-permute-start.7 = (bf16[128,128]{1,0:T(8,128)(2,1)S(1)}, bf16[128,128]{1,0:T(8,128)(2,1)S(1)}, u32[]{:S(2)}, u32[]{:S(2)}) collective-permute-start(bf16[128,128]{1,0:T(8,128)(2,1)S(1)} %get-tuple-element.35), channel_id=1, source_target_pairs={{0,4},{4,0},{8,12},{12,8},{16,20},{20,16},{24,28},{28,24},{1,5},{5... | collective-permute-start | bytes 98312 | tf_op jit(solution)/shard_map/ppermute | solution.py:28

commit v8 on v7

--- a/solution.py
+++ b/solution.py
@@ -35,14 +35,13 @@
 def reorder_kernel(order_ref, rows_ref, out_ref, staged, leaving):
     per_leaf = rows_ref.shape[2] // BLOCK
     copies = []
+    bits = per_leaf.bit_length() - 1
     arrived_slots = sum(slot << 3 * leaf for slot, leaf in enumerate(FIRST_MEMBERS))
     for slot, leaf in enumerate(MEMBERS):
         for t in range(per_leaf):
             source = order_ref[leaf * per_leaf + t]
-            column = pl.multiple_of(lax.rem(source, per_leaf) * BLOCK, BLOCK)
-            from_slot = lax.shift_right_logical(
-                jnp.int32(arrived_slots), 3 * lax.div(source, per_leaf)
-            )
+            column = pl.multiple_of((source & per_leaf - 1) * BLOCK, BLOCK)
+            from_slot = lax.shift_right_logical(jnp.int32(arrived_slots), (source >> bits) * 3)
             staged[slot, :, pl.ds(t * BLOCK, BLOCK)] = rows_ref[
                 from_slot & 7, :, pl.ds(column, BLOCK)
             ]

time: 39.2 us -> 39.1 us (level)
  no operation moved by 1% of the time
where the time goes in v8:
time: 39.1 us; the launch traced here: 38.6 us
  starting transfers between devices  25 us (64%)
  Pallas kernels  7.25 us (19%)
  waiting for transfers between devices  5.63 us (14%)
  between operations  0.72 us (2%)
    all_to_all x3, starting transfers between devices, spread(): lax.all_to_all(pieces, 'leaf', split_axis=0, concat_axis=0, tiled=True, a...  18.8 us
    ppermute x8, starting transfers between devices, exchanged(): lax.ppermute(piece, axis, [(i, i ^ flip) for i in range(count) if i ^ fli...  6.25 us
    ppermute x8, waiting for transfers between devices, exchanged(): lax.ppermute(piece, axis, [(i, i ^ flip) for i in range(count) if i ^ fli...  4.3 us
    pallas_call x1, Pallas kernels, weights_stage(): pl.pallas_call(weights_kernel, out_shape=[pltpu.VMEM(shape, bf16) for sha...  2.09 us
    pallas_call x1, Pallas kernels, leaf_stage(): pl.pallas_call(leaf_kernel, out_shape=(pltpu.VMEM((columns, placed.shape[...  1.71 us
    all_to_all x3, waiting for transfers between devices, spread(): lax.all_to_all(pieces, 'leaf', split_axis=0, concat_axis=0, tiled=True, a...  1.33 us
    pallas_call x1, Pallas kernels, eliminate_stage(): pl.pallas_call(eliminate_kernel, out_shape=jax.ShapeDtypeStruct(leading.s...  1.01 us
    pallas_call x1, Pallas kernels, reorder(): pl.pallas_call(reorder_kernel, out_shape=pltpu.HBM(rows.shape, rows.dtype...  0.9 us
  transfers between devices with their start and end apart: 11, of which 4 were waited for; matrix products, arithmetic and copies ran while one was open for 0% of the time, Pallas kernels for 13%

profile of v8, /device:TPU:0, one launch (start us, length us, event | category | flops | bytes accessed | tf_op | source)
XLA Modules:
  0.0 38.6 jit_solution(17388256095977293146)
XLA Ops:
  0.6 0.0 copy-start
  0.6 8.0 %all-to-all-start = ((bf16[8,16,1024]{2,1,0:T(8,128)(2,1)}), bf16[8,16,1024]{2,1,0:T(8,128)(2,1)S(1)}, u32[]{:S(2)}, u32[]{:S(2)}) async-start(bf16[8,16,1024]{2,1,0:T(8,128)(2,1)} %bitcast.8), calls=%async_computation | async-start | bytes 524288 | tf_op jit(solution)/shard_map/all_to_all | solution.py:370
  8.6 0.9 %shard_map.128 = (s32[64]{0:T(128)S(4)}, bf16[96,512]{1,0:T(8,128)(2,1)S(1)}, bf16[32,512]{1,0:T(8,128)(2,1)S(1)}) custom-call(s32[64]{0:T(128)} %order_ref.1, bf16[128,512]{1,0:T(8,128)(2,1)} %two_ref.1, bf16[64,512]{1,0:T(8,128)(2,1)} %three_ref.1), custom_call_target="tpu_custom_call" | custom-call | tf_op jit(solution)/shard_map/pallas_call | solution.py:96
  9.5 1.6 %collective-permute-start = (bf16[192,768]{1,0:T(8,128)(2,1)}, bf16[192,768]{1,0:T(8,128)(2,1)S(1)}, u32[]{:S(2)}, u32[]{:S(2)}) collective-permute-start(bf16[192,768]{1,0:T(8,128)(2,1)} %bitcast.11), channel_id=1, source_target_pairs={{0,2},{1,3},{2,0},{3,1},{4,6},{5,7},{6,4},{7,5},{8,10},{9,11},{10,... | collective-permute-start | bytes 884744 | tf_op jit(solution)/shard_map/ppermute | solution.py:28
  11.1 1.5 %collective-permute-start.1 = (bf16[96,512]{1,0:T(8,128)(2,1)S(1)}, bf16[96,512]{1,0:T(8,128)(2,1)S(1)}, u32[]{:S(2)}, u32[]{:S(2)}) collective-permute-start(bf16[96,512]{1,0:T(8,128)(2,1)S(1)} %get-tuple-element.24), channel_id=1, source_target_pairs={{0,4},{4,0},{8,12},{12,8},{16,20},{20,16},{24,28},{28,24},{1,5},{5... | collective-permute-start | bytes 294920 | tf_op jit(solution)/shard_map/ppermute | solution.py:28
  12.5 0.6 %collective-permute-start.3 = (bf16[32,512]{1,0:T(8,128)(2,1)S(1)}, bf16[32,512]{1,0:T(8,128)(2,1)S(1)}, u32[]{:S(2)}, u32[]{:S(2)}) collective-permute-start(bf16[32,512]{1,0:T(8,128)(2,1)S(1)} %get-tuple-element.26), channel_id=1, source_target_pairs={{0,12},{4,8},{8,4},{12,0},{16,28},{20,24},{24,20},{28,16},{1,13},{... | collective-permute-start | bytes 98312 | tf_op jit(solution)/shard_map/ppermute | solution.py:28
  13.1 1.5 %collective-permute-start.2 = (bf16[32,512]{1,0:T(8,128)(2,1)S(1)}, bf16[32,512]{1,0:T(8,128)(2,1)S(1)}, u32[]{:S(2)}, u32[]{:S(2)}) collective-permute-start(bf16[32,512]{1,0:T(8,128)(2,1)S(1)} %get-tuple-element.26), channel_id=1, source_target_pairs={{0,8},{4,12},{8,0},{12,4},{16,24},{20,28},{24,16},{28,20},{1,9},{5... | collective-permute-start | bytes 98312 | tf_op jit(solution)/shard_map/ppermute | solution.py:28
  14.6 1.0 %all-to-all-done.rows_ref = bf16[8,16,1024]{2,1,0:T(8,128)(2,1)S(1)} async-done(((bf16[8,16,1024]{2,1,0:T(8,128)(2,1)}), bf16[8,16,1024]{2,1,0:T(8,128)(2,1)S(1)}, u32[]{:S(2)}, u32[]{:S(2)}) %all-to-all-start) | async-done | bytes 262176 | tf_op jit(solution)/shard_map/all_to_all | solution.py:370
  15.5 0.9 %shard_map.129 = bf16[8,16,1024]{2,1,0:T(8,128)(2,1)} custom-call(s32[64]{0:T(128)S(4)} %get-tuple-element.23.order_ref, bf16[8,16,1024]{2,1,0:T(8,128)(2,1)S(1)} %all-to-all-done.rows_ref), custom_call_target="tpu_custom_call" | custom-call | tf_op jit(solution)/shard_map/pallas_call | solution.py:64
  16.5 4.7 %all-to-all-start.1 = ((bf16[8,16,1024]{2,1,0:T(8,128)(2,1)}), bf16[8,16,1024]{2,1,0:T(8,128)(2,1)S(1)}, u32[]{:S(2)}, u32[]{:S(2)}) async-start(bf16[8,16,1024]{2,1,0:T(8,128)(2,1)} %shard_map.129), calls=%async_computation.1 | async-start | bytes 524288 | tf_op jit(solution)/shard_map/all_to_all | solution.py:370
  21.2 0.0 collective-permute-done.1
  21.2 0.0 collective-permute-done.inverse_far_ref
  21.2 0.1 collective-permute-start.4
  21.3 0.5 %collective-permute-start.5 = (bf16[192,768]{1,0:T(8,128)(2,1)S(1)}, bf16[192,768]{1,0:T(8,128)(2,1)S(1)}, u32[]{:S(2)}, u32[]{:S(2)}) collective-permute-start(bf16[192,768]{1,0:T(8,128)(2,1)S(1)} %collective-permute-done.inverse_far_ref), channel_id=1, source_target_pairs={{0,1},{1,0},{2,3},{3,2},{4,5},{5,4},{6,7},{7,6},{8,9},{9,8},{10,11... | collective-permute-start | bytes 884744 | tf_op jit(solution)/shard_map/ppermute | solution.py:28
  21.8 0.1 collective-permute-start.6
  21.9 1.8 %collective-permute-done.6.upper_near_ref = bf16[256,512]{1,0:T(8,128)(2,1)S(1)} collective-permute-done((bf16[256,512]{1,0:T(8,128)(2,1)S(1)}, bf16[256,512]{1,0:T(8,128)(2,1)S(1)}, u32[]{:S(2)}, u32[]{:S(2)}) %collective-permute-start.6) | collective-permute-done | bytes 262176 | tf_op jit(solution)/shard_map/ppermute | solution.py:28
  23.7 2.1 %shard_map.130 = (bf16[768,768]{1,0:T(8,128)(2,1)S(1)}, bf16[1024,256]{1,0:T(8,128)(2,1)S(1)}, bf16[2304,256]{1,0:T(8,128)(2,1)S(1)}) custom-call(bf16[192,768]{1,0:T(8,128)(2,1)} %bitcast.12, bf16[192,768]{1,0:T(8,128)(2,1)S(1)} %collective-permute-done.inverse_far_ref, bf16[192,768]{1,0:T(8,128)(2,1)S(1)} %collective-permute-done.4.inverse_near_ref, ...), custom_call_target="tpu_custom_call" | custom-call | flops 1000000000 | bytes 6000000 | tf_op jit(solution)/shard_map/pallas_call | solution.py:207
  25.8 0.3 all-to-all-done.1.placed_ref
  26.1 1.7 %shard_map.131 = (bf16[128,768]{1,0:T(8,128)(2,1)S(1)}, bf16[8,128,128]{2,1,0:T(8,128)(2,1)}, bf16[128,128]{1,0:T(8,128)(2,1)S(1)}, f32[128,128]{1,0:T(8,128)S(1)}) custom-call(bf16[8,16,1024]{2,1,0:T(8,128)(2,1)S(1)} %all-to-all-done.1.placed_ref, bf16[1024,256]{1,0:T(8,128)(2,1)S(1)} %get-tuple-element.30.table_ref, ...), custom_call_target="tpu_custom_call" | custom-call | tf_op jit(solution)/shard_map/pallas_call | solution.py:293
  27.9 6.1 %all-to-all-start.2 = ((bf16[8,128,128]{2,1,0:T(8,128)(2,1)}), bf16[8,128,128]{2,1,0:T(8,128)(2,1)S(1)}, u32[]{:S(2)}, u32[]{:S(2)}) async-start(bf16[8,128,128]{2,1,0:T(8,128)(2,1)} %get-tuple-element.34), calls=%async_computation.2 | async-start | bytes 524288 | tf_op jit(solution)/shard_map/all_to_all | solution.py:370
  33.9 0.6 %collective-permute-start.7 = (bf16[128,128]{1,0:T(8,128)(2,1)S(1)}, bf16[128,128]{1,0:T(8,128)(2,1)S(1)}, u32[]{:S(2)}, u32[]{:S(2)}) collective-permute-start(bf16[128,128]{1,0:T(8,128)(2,1)S(1)} %get-tuple-element.35), channel_id=1, source_target_pairs={{0,4},{4,0},{8,12},{12,8},{16,20},{20,16},{24,28},{28,24},{1,5},{5... | collective-permute-start | bytes 98312 | tf_op jit(solution)/shard_map/ppermute | solution.py:28
  34.5 1.0 %shard_map.132 = bf16[128,768]{1,0:T(8,128)(2,1)} custom-call(bf16[128,768]{1,0:T(8,128)(2,1)S(1)} %get-tuple-element.32.leading_ref, bf16[768,768]{1,0:T(8,128)(2,1)S(1)} %get-tuple-element.33.inverse_ref), custom_call_target="tpu_custom_call" | custom-call | flops 1000000000 | bytes 6000000 | tf_op jit(solution)/shard_map/pallas_call | solution.py:316
  35.5 2.5 %collective-permute-done.7.received_one_ref = bf16[128,128]{1,0:T(8,128)(2,1)S(1)} collective-permute-done((bf16[128,128]{1,0:T(8,128)(2,1)S(1)}, bf16[128,128]{1,0:T(8,128)(2,1)S(1)}, u32[]{:S(2)}, u32[]{:S(2)}) %collective-permute-start.7) | collective-permute-done | bytes 32800 | tf_op jit(solution)/shard_map/ppermute | solution.py:28
  38.0 0.7 %shard_map.133 = (f32[128,128]{1,0:T(8,128)}, f32[64,128]{1,0:T(8,128)}, f32[32,128]{1,0:T(8,128)}, f32[32,128]{1,0:T(8,128)}) custom-call(bf16[8,128,128]{2,1,0:T(8,128)(2,1)S(1)} %all-to-all-done.2.received_ref, bf16[128,128]{1,0:T(8,128)(2,1)S(1)} %collective-permute-done.7.received_one_ref, f32[128,128]{1,0:T(8,128)S(1)} %get-tuple-element.36.kept_one_ref), custom_call_target="tpu_custom_call" | custom-call | tf_op jit(solution)/shard_map/pallas_call | solution.py:343
  (7 shorter events, 0.0 us)
Async XLA Ops:
  0.6 20.6 %copy-start = (bf16[1,192,768]{2,1,0:T(8,128)(2,1)S(1)}, bf16[1,192,768]{2,1,0:T(8,128)(2,1)}, u32[]{:S(2)}) copy-start(bf16[1,192,768]{2,1,0:T(8,128)(2,1)} %param.13) | copy-start | bytes 884740
  0.6 14.9 %all-to-all-start = ((bf16[8,16,1024]{2,1,0:T(8,128)(2,1)}), bf16[8,16,1024]{2,1,0:T(8,128)(2,1)S(1)}, u32[]{:S(2)}, u32[]{:S(2)}) async-start(bf16[8,16,1024]{2,1,0:T(8,128)(2,1)} %bitcast.8), calls=%async_computation | async-start | bytes 524288 | tf_op jit(solution)/shard_map/all_to_all | solution.py:370
  9.5 11.7 %collective-permute-start = (bf16[192,768]{1,0:T(8,128)(2,1)}, bf16[192,768]{1,0:T(8,128)(2,1)S(1)}, u32[]{:S(2)}, u32[]{:S(2)}) collective-permute-start(bf16[192,768]{1,0:T(8,128)(2,1)} %bitcast.11), channel_id=1, source_target_pairs={{0,2},{1,3},{2,0},{3,1},{4,6},{5,7},{6,4},{7,5},{8,10},{9,11},{10,... | collective-permute-start | bytes 884744 | tf_op jit(solution)/shard_map/ppermute | solution.py:28
  11.1 10.1 %collective-permute-start.1 = (bf16[96,512]{1,0:T(8,128)(2,1)S(1)}, bf16[96,512]{1,0:T(8,128)(2,1)S(1)}, u32[]{:S(2)}, u32[]{:S(2)}) collective-permute-start(bf16[96,512]{1,0:T(8,128)(2,1)S(1)} %get-tuple-element.24), channel_id=1, source_target_pairs={{0,4},{4,0},{8,12},{12,8},{16,20},{20,16},{24,28},{28,24},{1,5},{5... | collective-permute-start | bytes 294920 | tf_op jit(solution)/shard_map/ppermute | solution.py:28
  12.5 8.6 %collective-permute-start.3 = (bf16[32,512]{1,0:T(8,128)(2,1)S(1)}, bf16[32,512]{1,0:T(8,128)(2,1)S(1)}, u32[]{:S(2)}, u32[]{:S(2)}) collective-permute-start(bf16[32,512]{1,0:T(8,128)(2,1)S(1)} %get-tuple-element.26), channel_id=1, source_target_pairs={{0,12},{4,8},{8,4},{12,0},{16,28},{20,24},{24,20},{28,16},{1,13},{... | collective-permute-start | bytes 98312 | tf_op jit(solution)/shard_map/ppermute | solution.py:28
  13.1 8.1 %collective-permute-start.2 = (bf16[32,512]{1,0:T(8,128)(2,1)S(1)}, bf16[32,512]{1,0:T(8,128)(2,1)S(1)}, u32[]{:S(2)}, u32[]{:S(2)}) collective-permute-start(bf16[32,512]{1,0:T(8,128)(2,1)S(1)} %get-tuple-element.26), channel_id=1, source_target_pairs={{0,8},{4,12},{8,0},{12,4},{16,24},{20,28},{24,16},{28,20},{1,9},{5... | collective-permute-start | bytes 98312 | tf_op jit(solution)/shard_map/ppermute | solution.py:28
  16.5 9.7 %all-to-all-start.1 = ((bf16[8,16,1024]{2,1,0:T(8,128)(2,1)}), bf16[8,16,1024]{2,1,0:T(8,128)(2,1)S(1)}, u32[]{:S(2)}, u32[]{:S(2)}) async-start(bf16[8,16,1024]{2,1,0:T(8,128)(2,1)} %shard_map.129), calls=%async_computation.1 | async-start | bytes 524288 | tf_op jit(solution)/shard_map/all_to_all | solution.py:370
  21.2 2.4 %collective-permute-start.4 = (bf16[192,768]{1,0:T(8,128)(2,1)S(1)}, bf16[192,768]{1,0:T(8,128)(2,1)S(1)}, u32[]{:S(2)}, u32[]{:S(2)}) collective-permute-start(bf16[192,768]{1,0:T(8,128)(2,1)S(1)} %bitcast.13), channel_id=1, source_target_pairs={{0,1},{1,0},{2,3},{3,2},{4,5},{5,4},{6,7},{7,6},{8,9},{9,8},{10,11... | collective-permute-start | bytes 884744 | tf_op jit(solution)/shard_map/ppermute | solution.py:28
  21.3 2.4 %collective-permute-start.5 = (bf16[192,768]{1,0:T(8,128)(2,1)S(1)}, bf16[192,768]{1,0:T(8,128)(2,1)S(1)}, u32[]{:S(2)}, u32[]{:S(2)}) collective-permute-start(bf16[192,768]{1,0:T(8,128)(2,1)S(1)} %collective-permute-done.inverse_far_ref), channel_id=1, source_target_pairs={{0,1},{1,0},{2,3},{3,2},{4,5},{5,4},{6,7},{7,6},{8,9},{9,8},{10,11... | collective-permute-start | bytes 884744 | tf_op jit(solution)/shard_map/ppermute | solution.py:28
  21.8 1.9 %collective-permute-start.6 = (bf16[256,512]{1,0:T(8,128)(2,1)S(1)}, bf16[256,512]{1,0:T(8,128)(2,1)S(1)}, u32[]{:S(2)}, u32[]{:S(2)}) collective-permute-start(bf16[256,512]{1,0:T(8,128)(2,1)S(1)} %pad_maximum_fusion.upper_ref), channel_id=1, source_target_pairs={{0,1},{1,0},{2,3},{3,2},{4,5},{5,4},{6,7},{7,6},{8,9},{9,8},{10,11... | collective-permute-start | bytes 786440 | tf_op jit(solution)/shard_map/ppermute | solution.py:28
  27.9 10.1 %all-to-all-start.2 = ((bf16[8,128,128]{2,1,0:T(8,128)(2,1)}), bf16[8,128,128]{2,1,0:T(8,128)(2,1)S(1)}, u32[]{:S(2)}, u32[]{:S(2)}) async-start(bf16[8,128,128]{2,1,0:T(8,128)(2,1)} %get-tuple-element.34), calls=%async_computation.2 | async-start | bytes 524288 | tf_op jit(solution)/shard_map/all_to_all | solution.py:370
  33.9 4.1 %collective-permute-start.7 = (bf16[128,128]{1,0:T(8,128)(2,1)S(1)}, bf16[128,128]{1,0:T(8,128)(2,1)S(1)}, u32[]{:S(2)}, u32[]{:S(2)}) collective-permute-start(bf16[128,128]{1,0:T(8,128)(2,1)S(1)} %get-tuple-element.35), channel_id=1, source_target_pairs={{0,4},{4,0},{8,12},{12,8},{16,20},{20,16},{24,28},{28,24},{1,5},{5... | collective-permute-start | bytes 98312 | tf_op jit(solution)/shard_map/ppermute | solution.py:28

commit v9 on v8

--- a/solution.py
+++ b/solution.py
@@ -9,7 +9,7 @@
 NODE_LEAVES = 8
 FIRST_MEMBERS = (4, 5, 6, 7, 0, 1, 2, 3)
 MEMBERS = (4, 2, 3, 5, 0, 6, 7, 1)
-LAST_MEMBERS = (5, 4, 1, 0, 7, 6, 3, 2)
+LAST_MEMBERS = (5, 3, 4, 2, 1, 0, 7, 6)
 INSIDE = pl.BlockSpec(memory_space=pltpu.VMEM)
 SCALARS = pl.BlockSpec(memory_space=pltpu.SMEM)
 OUTSIDE = pl.BlockSpec(memory_space=pl.ANY)

time: 39.1 us -> 39.1 us (level)
  no operation moved by 1% of the time
where the time goes in v9:
time: 39.1 us; the launch traced here: 38.6 us
  starting transfers between devices  25 us (64%)
  Pallas kernels  7.25 us (19%)
  waiting for transfers between devices  5.63 us (14%)
  between operations  0.72 us (2%)
    all_to_all x3, starting transfers between devices, spread(): lax.all_to_all(pieces, 'leaf', split_axis=0, concat_axis=0, tiled=True, a...  18.8 us
    ppermute x8, starting transfers between devices, exchanged(): lax.ppermute(piece, axis, [(i, i ^ flip) for i in range(count) if i ^ fli...  6.25 us
    ppermute x8, waiting for transfers between devices, exchanged(): lax.ppermute(piece, axis, [(i, i ^ flip) for i in range(count) if i ^ fli...  4.3 us
    pallas_call x1, Pallas kernels, weights_stage(): pl.pallas_call(weights_kernel, out_shape=[pltpu.VMEM(shape, bf16) for sha...  2.09 us
    pallas_call x1, Pallas kernels, leaf_stage(): pl.pallas_call(leaf_kernel, out_shape=(pltpu.VMEM((columns, placed.shape[...  1.71 us
    all_to_all x3, waiting for transfers between devices, spread(): lax.all_to_all(pieces, 'leaf', split_axis=0, concat_axis=0, tiled=True, a...  1.33 us
    pallas_call x1, Pallas kernels, eliminate_stage(): pl.pallas_call(eliminate_kernel, out_shape=jax.ShapeDtypeStruct(leading.s...  1 us
    pallas_call x1, Pallas kernels, reorder(): pl.pallas_call(reorder_kernel, out_shape=pltpu.HBM(rows.shape, rows.dtype...  0.9 us
  transfers between devices with their start and end apart: 11, of which 4 were waited for; matrix products, arithmetic and copies ran while one was open for 0% of the time, Pallas kernels for 13%

profile of v9, /device:TPU:0, one launch (start us, length us, event | category | flops | bytes accessed | tf_op | source)
XLA Modules:
  0.0 38.6 jit_solution(17299767416625993785)
XLA Ops:
  0.6 0.0 copy-start
  0.6 8.0 %all-to-all-start = ((bf16[8,16,1024]{2,1,0:T(8,128)(2,1)}), bf16[8,16,1024]{2,1,0:T(8,128)(2,1)S(1)}, u32[]{:S(2)}, u32[]{:S(2)}) async-start(bf16[8,16,1024]{2,1,0:T(8,128)(2,1)} %bitcast.8), calls=%async_computation | async-start | bytes 524288 | tf_op jit(solution)/shard_map/all_to_all | solution.py:370
  8.6 0.9 %shard_map.128 = (s32[64]{0:T(128)S(4)}, bf16[96,512]{1,0:T(8,128)(2,1)S(1)}, bf16[32,512]{1,0:T(8,128)(2,1)S(1)}) custom-call(s32[64]{0:T(128)} %order_ref.1, bf16[128,512]{1,0:T(8,128)(2,1)} %two_ref.1, bf16[64,512]{1,0:T(8,128)(2,1)} %three_ref.1), custom_call_target="tpu_custom_call" | custom-call | tf_op jit(solution)/shard_map/pallas_call | solution.py:96
  9.5 1.6 %collective-permute-start = (bf16[192,768]{1,0:T(8,128)(2,1)}, bf16[192,768]{1,0:T(8,128)(2,1)S(1)}, u32[]{:S(2)}, u32[]{:S(2)}) collective-permute-start(bf16[192,768]{1,0:T(8,128)(2,1)} %bitcast.11), channel_id=1, source_target_pairs={{0,2},{1,3},{2,0},{3,1},{4,6},{5,7},{6,4},{7,5},{8,10},{9,11},{10,... | collective-permute-start | bytes 884744 | tf_op jit(solution)/shard_map/ppermute | solution.py:28
  11.1 1.5 %collective-permute-start.1 = (bf16[96,512]{1,0:T(8,128)(2,1)S(1)}, bf16[96,512]{1,0:T(8,128)(2,1)S(1)}, u32[]{:S(2)}, u32[]{:S(2)}) collective-permute-start(bf16[96,512]{1,0:T(8,128)(2,1)S(1)} %get-tuple-element.24), channel_id=1, source_target_pairs={{0,4},{4,0},{8,12},{12,8},{16,20},{20,16},{24,28},{28,24},{1,5},{5... | collective-permute-start | bytes 294920 | tf_op jit(solution)/shard_map/ppermute | solution.py:28
  12.5 0.6 %collective-permute-start.3 = (bf16[32,512]{1,0:T(8,128)(2,1)S(1)}, bf16[32,512]{1,0:T(8,128)(2,1)S(1)}, u32[]{:S(2)}, u32[]{:S(2)}) collective-permute-start(bf16[32,512]{1,0:T(8,128)(2,1)S(1)} %get-tuple-element.26), channel_id=1, source_target_pairs={{0,12},{4,8},{8,4},{12,0},{16,28},{20,24},{24,20},{28,16},{1,13},{... | collective-permute-start | bytes 98312 | tf_op jit(solution)/shard_map/ppermute | solution.py:28
  13.1 1.5 %collective-permute-start.2 = (bf16[32,512]{1,0:T(8,128)(2,1)S(1)}, bf16[32,512]{1,0:T(8,128)(2,1)S(1)}, u32[]{:S(2)}, u32[]{:S(2)}) collective-permute-start(bf16[32,512]{1,0:T(8,128)(2,1)S(1)} %get-tuple-element.26), channel_id=1, source_target_pairs={{0,8},{4,12},{8,0},{12,4},{16,24},{20,28},{24,16},{28,20},{1,9},{5... | collective-permute-start | bytes 98312 | tf_op jit(solution)/shard_map/ppermute | solution.py:28
  14.6 1.0 %all-to-all-done.rows_ref = bf16[8,16,1024]{2,1,0:T(8,128)(2,1)S(1)} async-done(((bf16[8,16,1024]{2,1,0:T(8,128)(2,1)}), bf16[8,16,1024]{2,1,0:T(8,128)(2,1)S(1)}, u32[]{:S(2)}, u32[]{:S(2)}) %all-to-all-start) | async-done | bytes 262176 | tf_op jit(solution)/shard_map/all_to_all | solution.py:370
  15.5 0.9 %shard_map.129 = bf16[8,16,1024]{2,1,0:T(8,128)(2,1)} custom-call(s32[64]{0:T(128)S(4)} %get-tuple-element.23.order_ref, bf16[8,16,1024]{2,1,0:T(8,128)(2,1)S(1)} %all-to-all-done.rows_ref), custom_call_target="tpu_custom_call" | custom-call | tf_op jit(solution)/shard_map/pallas_call | solution.py:64
  16.5 4.7 %all-to-all-start.1 = ((bf16[8,16,1024]{2,1,0:T(8,128)(2,1)}), bf16[8,16,1024]{2,1,0:T(8,128)(2,1)S(1)}, u32[]{:S(2)}, u32[]{:S(2)}) async-start(bf16[8,16,1024]{2,1,0:T(8,128)(2,1)} %shard_map.129), calls=%async_computation.1 | async-start | bytes 524288 | tf_op jit(solution)/shard_map/all_to_all | solution.py:370
  21.2 0.0 collective-permute-done.2
  21.2 0.0 collective-permute-done.1
  21.2 0.1 collective-permute-start.4
  21.3 0.5 %collective-permute-start.5 = (bf16[192,768]{1,0:T(8,128)(2,1)S(1)}, bf16[192,768]{1,0:T(8,128)(2,1)S(1)}, u32[]{:S(2)}, u32[]{:S(2)}) collective-permute-start(bf16[192,768]{1,0:T(8,128)(2,1)S(1)} %collective-permute-done.inverse_far_ref), channel_id=1, source_target_pairs={{0,1},{1,0},{2,3},{3,2},{4,5},{5,4},{6,7},{7,6},{8,9},{9,8},{10,11... | collective-permute-start | bytes 884744 | tf_op jit(solution)/shard_map/ppermute | solution.py:28
  21.8 0.1 collective-permute-start.6
  21.9 1.8 %collective-permute-done.6.upper_near_ref = bf16[256,512]{1,0:T(8,128)(2,1)S(1)} collective-permute-done((bf16[256,512]{1,0:T(8,128)(2,1)S(1)}, bf16[256,512]{1,0:T(8,128)(2,1)S(1)}, u32[]{:S(2)}, u32[]{:S(2)}) %collective-permute-start.6) | collective-permute-done | bytes 262176 | tf_op jit(solution)/shard_map/ppermute | solution.py:28
  23.7 2.1 %shard_map.130 = (bf16[768,768]{1,0:T(8,128)(2,1)S(1)}, bf16[1024,256]{1,0:T(8,128)(2,1)S(1)}, bf16[2304,256]{1,0:T(8,128)(2,1)S(1)}) custom-call(bf16[192,768]{1,0:T(8,128)(2,1)} %bitcast.12, bf16[192,768]{1,0:T(8,128)(2,1)S(1)} %collective-permute-done.inverse_far_ref, bf16[192,768]{1,0:T(8,128)(2,1)S(1)} %collective-permute-done.4.inverse_near_ref, ...), custom_call_target="tpu_custom_call" | custom-call | flops 1000000000 | bytes 6000000 | tf_op jit(solution)/shard_map/pallas_call | solution.py:207
  25.8 0.3 all-to-all-done.1.placed_ref
  26.1 1.7 %shard_map.131 = (bf16[128,768]{1,0:T(8,128)(2,1)S(1)}, bf16[8,128,128]{2,1,0:T(8,128)(2,1)}, bf16[128,128]{1,0:T(8,128)(2,1)S(1)}, f32[128,128]{1,0:T(8,128)S(1)}) custom-call(bf16[8,16,1024]{2,1,0:T(8,128)(2,1)S(1)} %all-to-all-done.1.placed_ref, bf16[1024,256]{1,0:T(8,128)(2,1)S(1)} %get-tuple-element.30.table_ref, ...), custom_call_target="tpu_custom_call" | custom-call | tf_op jit(solution)/shard_map/pallas_call | solution.py:293
  27.9 6.1 %all-to-all-start.2 = ((bf16[8,128,128]{2,1,0:T(8,128)(2,1)}), bf16[8,128,128]{2,1,0:T(8,128)(2,1)S(1)}, u32[]{:S(2)}, u32[]{:S(2)}) async-start(bf16[8,128,128]{2,1,0:T(8,128)(2,1)} %get-tuple-element.34), calls=%async_computation.2 | async-start | bytes 524288 | tf_op jit(solution)/shard_map/all_to_all | solution.py:370
  33.9 0.6 %collective-permute-start.7 = (bf16[128,128]{1,0:T(8,128)(2,1)S(1)}, bf16[128,128]{1,0:T(8,128)(2,1)S(1)}, u32[]{:S(2)}, u32[]{:S(2)}) collective-permute-start(bf16[128,128]{1,0:T(8,128)(2,1)S(1)} %get-tuple-element.35), channel_id=1, source_target_pairs={{0,4},{4,0},{8,12},{12,8},{16,20},{20,16},{24,28},{28,24},{1,5},{5... | collective-permute-start | bytes 98312 | tf_op jit(solution)/shard_map/ppermute | solution.py:28
  34.5 1.0 %shard_map.132 = bf16[128,768]{1,0:T(8,128)(2,1)} custom-call(bf16[128,768]{1,0:T(8,128)(2,1)S(1)} %get-tuple-element.32.leading_ref, bf16[768,768]{1,0:T(8,128)(2,1)S(1)} %get-tuple-element.33.inverse_ref), custom_call_target="tpu_custom_call" | custom-call | flops 1000000000 | bytes 6000000 | tf_op jit(solution)/shard_map/pallas_call | solution.py:316
  35.5 2.5 %collective-permute-done.7.received_one_ref = bf16[128,128]{1,0:T(8,128)(2,1)S(1)} collective-permute-done((bf16[128,128]{1,0:T(8,128)(2,1)S(1)}, bf16[128,128]{1,0:T(8,128)(2,1)S(1)}, u32[]{:S(2)}, u32[]{:S(2)}) %collective-permute-start.7) | collective-permute-done | bytes 32800 | tf_op jit(solution)/shard_map/ppermute | solution.py:28
  38.0 0.7 %shard_map.133 = (f32[128,128]{1,0:T(8,128)}, f32[64,128]{1,0:T(8,128)}, f32[32,128]{1,0:T(8,128)}, f32[32,128]{1,0:T(8,128)}) custom-call(bf16[8,128,128]{2,1,0:T(8,128)(2,1)S(1)} %all-to-all-done.2.received_ref, bf16[128,128]{1,0:T(8,128)(2,1)S(1)} %collective-permute-done.7.received_one_ref, f32[128,128]{1,0:T(8,128)S(1)} %get-tuple-element.36.kept_one_ref), custom_call_target="tpu_custom_call" | custom-call | tf_op jit(solution)/shard_map/pallas_call | solution.py:343
  (7 shorter events, 0.0 us)
Async XLA Ops:
  0.6 20.6 %copy-start = (bf16[1,192,768]{2,1,0:T(8,128)(2,1)S(1)}, bf16[1,192,768]{2,1,0:T(8,128)(2,1)}, u32[]{:S(2)}) copy-start(bf16[1,192,768]{2,1,0:T(8,128)(2,1)} %param.13) | copy-start | bytes 884740
  0.6 14.9 %all-to-all-start = ((bf16[8,16,1024]{2,1,0:T(8,128)(2,1)}), bf16[8,16,1024]{2,1,0:T(8,128)(2,1)S(1)}, u32[]{:S(2)}, u32[]{:S(2)}) async-start(bf16[8,16,1024]{2,1,0:T(8,128)(2,1)} %bitcast.8), calls=%async_computation | async-start | bytes 524288 | tf_op jit(solution)/shard_map/all_to_all | solution.py:370
  9.5 11.7 %collective-permute-start = (bf16[192,768]{1,0:T(8,128)(2,1)}, bf16[192,768]{1,0:T(8,128)(2,1)S(1)}, u32[]{:S(2)}, u32[]{:S(2)}) collective-permute-start(bf16[192,768]{1,0:T(8,128)(2,1)} %bitcast.11), channel_id=1, source_target_pairs={{0,2},{1,3},{2,0},{3,1},{4,6},{5,7},{6,4},{7,5},{8,10},{9,11},{10,... | collective-permute-start | bytes 884744 | tf_op jit(solution)/shard_map/ppermute | solution.py:28
  11.1 10.1 %collective-permute-start.1 = (bf16[96,512]{1,0:T(8,128)(2,1)S(1)}, bf16[96,512]{1,0:T(8,128)(2,1)S(1)}, u32[]{:S(2)}, u32[]{:S(2)}) collective-permute-start(bf16[96,512]{1,0:T(8,128)(2,1)S(1)} %get-tuple-element.24), channel_id=1, source_target_pairs={{0,4},{4,0},{8,12},{12,8},{16,20},{20,16},{24,28},{28,24},{1,5},{5... | collective-permute-start | bytes 294920 | tf_op jit(solution)/shard_map/ppermute | solution.py:28
  12.5 8.6 %collective-permute-start.3 = (bf16[32,512]{1,0:T(8,128)(2,1)S(1)}, bf16[32,512]{1,0:T(8,128)(2,1)S(1)}, u32[]{:S(2)}, u32[]{:S(2)}) collective-permute-start(bf16[32,512]{1,0:T(8,128)(2,1)S(1)} %get-tuple-element.26), channel_id=1, source_target_pairs={{0,12},{4,8},{8,4},{12,0},{16,28},{20,24},{24,20},{28,16},{1,13},{... | collective-permute-start | bytes 98312 | tf_op jit(solution)/shard_map/ppermute | solution.py:28
  13.1 8.1 %collective-permute-start.2 = (bf16[32,512]{1,0:T(8,128)(2,1)S(1)}, bf16[32,512]{1,0:T(8,128)(2,1)S(1)}, u32[]{:S(2)}, u32[]{:S(2)}) collective-permute-start(bf16[32,512]{1,0:T(8,128)(2,1)S(1)} %get-tuple-element.26), channel_id=1, source_target_pairs={{0,8},{4,12},{8,0},{12,4},{16,24},{20,28},{24,16},{28,20},{1,9},{5... | collective-permute-start | bytes 98312 | tf_op jit(solution)/shard_map/ppermute | solution.py:28
  16.5 9.7 %all-to-all-start.1 = ((bf16[8,16,1024]{2,1,0:T(8,128)(2,1)}), bf16[8,16,1024]{2,1,0:T(8,128)(2,1)S(1)}, u32[]{:S(2)}, u32[]{:S(2)}) async-start(bf16[8,16,1024]{2,1,0:T(8,128)(2,1)} %shard_map.129), calls=%async_computation.1 | async-start | bytes 524288 | tf_op jit(solution)/shard_map/all_to_all | solution.py:370
  21.2 2.4 %collective-permute-start.4 = (bf16[192,768]{1,0:T(8,128)(2,1)S(1)}, bf16[192,768]{1,0:T(8,128)(2,1)S(1)}, u32[]{:S(2)}, u32[]{:S(2)}) collective-permute-start(bf16[192,768]{1,0:T(8,128)(2,1)S(1)} %bitcast.13), channel_id=1, source_target_pairs={{0,1},{1,0},{2,3},{3,2},{4,5},{5,4},{6,7},{7,6},{8,9},{9,8},{10,11... | collective-permute-start | bytes 884744 | tf_op jit(solution)/shard_map/ppermute | solution.py:28
  21.3 2.4 %collective-permute-start.5 = (bf16[192,768]{1,0:T(8,128)(2,1)S(1)}, bf16[192,768]{1,0:T(8,128)(2,1)S(1)}, u32[]{:S(2)}, u32[]{:S(2)}) collective-permute-start(bf16[192,768]{1,0:T(8,128)(2,1)S(1)} %collective-permute-done.inverse_far_ref), channel_id=1, source_target_pairs={{0,1},{1,0},{2,3},{3,2},{4,5},{5,4},{6,7},{7,6},{8,9},{9,8},{10,11... | collective-permute-start | bytes 884744 | tf_op jit(solution)/shard_map/ppermute | solution.py:28
  21.8 1.9 %collective-permute-start.6 = (bf16[256,512]{1,0:T(8,128)(2,1)S(1)}, bf16[256,512]{1,0:T(8,128)(2,1)S(1)}, u32[]{:S(2)}, u32[]{:S(2)}) collective-permute-start(bf16[256,512]{1,0:T(8,128)(2,1)S(1)} %pad_maximum_fusion.upper_ref), channel_id=1, source_target_pairs={{0,1},{1,0},{2,3},{3,2},{4,5},{5,4},{6,7},{7,6},{8,9},{9,8},{10,11... | collective-permute-start | bytes 786440 | tf_op jit(solution)/shard_map/ppermute | solution.py:28
  27.9 10.1 %all-to-all-start.2 = ((bf16[8,128,128]{2,1,0:T(8,128)(2,1)}), bf16[8,128,128]{2,1,0:T(8,128)(2,1)S(1)}, u32[]{:S(2)}, u32[]{:S(2)}) async-start(bf16[8,128,128]{2,1,0:T(8,128)(2,1)} %get-tuple-element.34), calls=%async_computation.2 | async-start | bytes 524288 | tf_op jit(solution)/shard_map/all_to_all | solution.py:370
  33.9 4.1 %collective-permute-start.7 = (bf16[128,128]{1,0:T(8,128)(2,1)S(1)}, bf16[128,128]{1,0:T(8,128)(2,1)S(1)}, u32[]{:S(2)}, u32[]{:S(2)}) collective-permute-start(bf16[128,128]{1,0:T(8,128)(2,1)S(1)} %get-tuple-element.35), channel_id=1, source_target_pairs={{0,4},{4,0},{8,12},{12,8},{16,20},{20,16},{24,28},{28,24},{1,5},{5... | collective-permute-start | bytes 98312 | tf_op jit(solution)/shard_map/ppermute | solution.py:28
